TPU v7x, 32 devices: a whole 2x2x4 slice. The times are simulated.
32 devices in a mesh: dp: 4 (over y, x), seq: 8 (over z, core).
Axes of the slice: x: 2, y: 2, z: 4, core: 2. Of those that a mesh axis runs over, the one named last changes fastest.
Arguments:
- tokens: bfloat16 [4, 2048, 1024], P('dp', 'seq'), may hold values from -6 to 6
- segments: int32 [4, 2048], P('dp'), may hold values from 0 to 2047, as said below
- cotangent: bfloat16 [4, 2048, 1024], P('dp', 'seq'), may hold values from -6 to 6
- in_weight: float32 [1024, 3072], P(('dp', 'seq')), may hold values from -0.1875 to 0.1875
- out_weight: float32 [1024, 1024], P(('dp', 'seq')), may hold values from -0.1875 to 0.1875
- gate_weight: float32 [1024, 4608], P(('dp', 'seq')), may hold values from -0.1875 to 0.1875
- up_weight: float32 [1024, 4608], P(('dp', 'seq')), may hold values from -0.1875 to 0.1875
- down_weight: float32 [4608, 1024], P(('dp', 'seq')), may hold values from -0.09375 to 0.09375
- norm_one: float32 [1024], P(('dp', 'seq')), may hold values from 0.1 to 1.9
- norm_two: float32 [1024], P(('dp', 'seq')), may hold values from 0.1 to 1.9
- kernel: float32 [3, 1024], P(None, ('dp', 'seq')), may hold values from -3.5 to 3.5
Outputs:
- output: bfloat16 [4, 2048, 1024], P('dp', 'seq')
- grad_tokens: bfloat16 [4, 2048, 1024], P('dp', 'seq')
- grad_in: float32 [1024, 3072], P(('dp', 'seq'))
- grad_out: float32 [1024, 1024], P(('dp', 'seq'))
- grad_gate: float32 [1024, 4608], P(('dp', 'seq'))
- grad_up: float32 [1024, 4608], P(('dp', 'seq'))
- grad_down: float32 [4608, 1024], P(('dp', 'seq'))
- grad_norm_one: float32 [1024], P(('dp', 'seq'))
- grad_norm_two: float32 [1024], P(('dp', 'seq'))
- grad_kernel: float32 [3, 1024], P(None, ('dp', 'seq'))
Inputs may be any that keep to these rules, and one draw needn't show every extreme that they name: `segments`: within a sequence document numbers never fall and differ between documents; a document's number is the position of its first token in the sequence, except that the last document of each sequence is numbered 2048 - 1; documents hold about 200 to 2000 tokens; no document but the first begins at the first two positions of a block of 256 tokens.
All inputs are finite; a program needn't handle non-finite values.
Results may differ from a plain program's by a relative error of at most 0.014.
The roundings to bfloat16 on the way count: a program that leaves them out, or rounds other values in their place, can miss the bound.
Values may be sent and summed in bfloat16 or wider, within the bound.
A program may use at most 192 MiB of HBM per device.

v0:
```python
import jax
import jax.numpy as jnp
from jax import lax
from jax.sharding import PartitionSpec as P

epsilon = 1e-05


def from_behind(value, axis, steps):
    count = lax.axis_size(axis)
    leading, last = (max(0, -steps), min(count, count - steps))
    return lax.ppermute(value, axis, [(source, source + steps) for source in range(leading, last)])


def matmul(left, right):
    return jnp.dot(left, right, preferred_element_type=jnp.float32)


def matmul_tn(left, right):
    return lax.dot_general(
        left, right, (((0,), (0,)), ((), ())), preferred_element_type=jnp.float32
    )


def matmul_nt(left, right):
    return lax.dot_general(
        left, right, (((1,), (1,)), ((), ())), preferred_element_type=jnp.float32
    )


def norm_back(grad_unit, unit_rows, inverse):
    return inverse * (
        grad_unit - unit_rows * jnp.mean(grad_unit * unit_rows, axis=1, keepdims=True)
    )


def split_rows(grads):
    n_dp = lax.axis_size("dp")
    n_seq = lax.axis_size("seq")
    return tuple(
        (
            value.reshape((n_dp, n_seq, value.shape[0] // (n_dp * n_seq)) + value.shape[1:])
            for value in grads
        )
    )


def join_rows(grads):
    return tuple((value.reshape(value.shape[1:]) for value in grads))


def spread_all(grads):
    shaped = split_rows(grads)
    moved = (
        lax.all_to_all(
            shaped[0].astype(jnp.bfloat16), "seq", split_axis=1, concat_axis=1, tiled=True
        ).astype(jnp.float32),
        lax.all_to_all(
            shaped[1].astype(jnp.bfloat16), "seq", split_axis=1, concat_axis=1, tiled=True
        ).astype(jnp.float32),
        lax.all_to_all(
            shaped[2].astype(jnp.bfloat16), "seq", split_axis=1, concat_axis=1, tiled=True
        ).astype(jnp.float32),
        lax.all_to_all(
            shaped[3].astype(jnp.bfloat16), "seq", split_axis=1, concat_axis=1, tiled=True
        ).astype(jnp.float32),
        lax.all_to_all(
            shaped[4].astype(jnp.bfloat16), "seq", split_axis=1, concat_axis=1, tiled=True
        ).astype(jnp.float32),
        lax.all_to_all(
            shaped[5].astype(jnp.bfloat16), "seq", split_axis=1, concat_axis=1, tiled=True
        ).astype(jnp.float32),
        lax.all_to_all(
            shaped[6].astype(jnp.bfloat16), "seq", split_axis=1, concat_axis=1, tiled=True
        ).astype(jnp.float32),
        lax.all_to_all(
            shaped[7].astype(jnp.bfloat16), "seq", split_axis=1, concat_axis=1, tiled=True
        ).astype(jnp.float32),
    )
    summed = tuple((jnp.sum(value, axis=1) for value in moved))
    owned = (
        lax.psum_scatter(
            summed[0].astype(jnp.bfloat16), "dp", scatter_dimension=0, tiled=True
        ).astype(jnp.float32),
        lax.psum_scatter(
            summed[1].astype(jnp.bfloat16), "dp", scatter_dimension=0, tiled=True
        ).astype(jnp.float32),
        lax.psum_scatter(
            summed[2].astype(jnp.bfloat16), "dp", scatter_dimension=0, tiled=True
        ).astype(jnp.float32),
        lax.psum_scatter(
            summed[3].astype(jnp.bfloat16), "dp", scatter_dimension=0, tiled=True
        ).astype(jnp.float32),
        lax.psum_scatter(
            summed[4].astype(jnp.bfloat16), "dp", scatter_dimension=0, tiled=True
        ).astype(jnp.float32),
        lax.psum_scatter(
            summed[5].astype(jnp.bfloat16), "dp", scatter_dimension=0, tiled=True
        ).astype(jnp.float32),
        lax.psum_scatter(
            summed[6].astype(jnp.bfloat16), "dp", scatter_dimension=0, tiled=True
        ).astype(jnp.float32),
        lax.psum_scatter(
            summed[7].astype(jnp.bfloat16), "dp", scatter_dimension=0, tiled=True
        ).astype(jnp.float32),
    )
    return join_rows(owned)


def body(
    tokens,
    segments,
    cotangent,
    in_weight,
    out_weight,
    gate_weight,
    up_weight,
    down_weight,
    norm_one,
    norm_two,
    kernel,
):
    feature_width = tokens.shape[2]
    count_rows = tokens.shape[1]
    gathered = (
        lax.all_gather(in_weight.astype(jnp.bfloat16), ("dp", "seq"), axis=0, tiled=True),
        lax.all_gather(out_weight.astype(jnp.bfloat16), ("dp", "seq"), axis=0, tiled=True),
        lax.all_gather(gate_weight.astype(jnp.bfloat16), ("dp", "seq"), axis=0, tiled=True),
        lax.all_gather(up_weight.astype(jnp.bfloat16), ("dp", "seq"), axis=0, tiled=True),
        lax.all_gather(down_weight.astype(jnp.bfloat16), ("dp", "seq"), axis=0, tiled=True),
        lax.all_gather(norm_one.astype(jnp.bfloat16), ("dp", "seq"), axis=0, tiled=True),
        lax.all_gather(norm_two.astype(jnp.bfloat16), ("dp", "seq"), axis=0, tiled=True),
        lax.all_gather(kernel.astype(jnp.bfloat16), ("dp", "seq"), axis=1, tiled=True),
    )
    in_mat, out_mat, gate_mat, up_mat, down_mat, gain_a, gain_b, kernel_b = gathered
    offset_row = lax.axis_index("seq") * count_rows
    filler = jnp.full((2,), -1, jnp.int32)
    doc_ids = jnp.concatenate([filler, segments[0], filler])
    near_ids = lax.dynamic_slice_in_dim(doc_ids, offset_row, count_rows + 4)
    own_ids = near_ids[2 : count_rows + 2]
    back_one = (own_ids == near_ids[1 : count_rows + 1]).astype(jnp.float32)[:, None]
    back_two = (own_ids == near_ids[0:count_rows]).astype(jnp.float32)[:, None]
    ahead_one = (near_ids[3 : count_rows + 3] == own_ids).astype(jnp.float32)[:, None]
    ahead_two = (near_ids[4 : count_rows + 4] == own_ids).astype(jnp.float32)[:, None]
    resident = tokens[0].astype(jnp.float32)
    inverse_a = lax.rsqrt(jnp.mean(resident * resident, axis=1, keepdims=True) + epsilon)
    unit_a = resident * inverse_a
    gain_af = gain_a.astype(jnp.float32)
    normed_a = (unit_a * gain_af).astype(jnp.bfloat16)
    mixed = matmul(normed_a, in_mat)
    b_part = mixed[:, :feature_width]
    c_part = mixed[:, feature_width : 2 * feature_width]
    x_part = mixed[:, 2 * feature_width :]
    conv_in = (b_part * x_part).astype(jnp.bfloat16)
    earlier = from_behind(conv_in[count_rows - 2 :], "seq", 1)
    extended = jnp.concatenate([earlier, conv_in], axis=0).astype(jnp.float32)
    kernel_f = kernel_b.astype(jnp.float32)
    current = extended[2:]
    prev_one = extended[1 : count_rows + 1] * back_one
    prev_two = extended[0:count_rows] * back_two
    convolved = kernel_f[0] * current + kernel_f[1] * prev_one + kernel_f[2] * prev_two
    gated = (c_part * convolved).astype(jnp.bfloat16)
    hidden = resident + matmul(gated, out_mat)
    inverse_b = lax.rsqrt(jnp.mean(hidden * hidden, axis=1, keepdims=True) + epsilon)
    unit_b = hidden * inverse_b
    gain_bf = gain_b.astype(jnp.float32)
    normed_b = (unit_b * gain_bf).astype(jnp.bfloat16)
    gate_pre = matmul(normed_b, gate_mat)
    up_pre = matmul(normed_b, up_mat)
    swish = jax.nn.silu(gate_pre)
    active = (swish * up_pre).astype(jnp.bfloat16)
    output = hidden + matmul(active, down_mat)
    regathered = (
        lax.all_gather(in_weight.astype(jnp.bfloat16), ("dp", "seq"), axis=0, tiled=True),
        lax.all_gather(out_weight.astype(jnp.bfloat16), ("dp", "seq"), axis=0, tiled=True),
        lax.all_gather(gate_weight.astype(jnp.bfloat16), ("dp", "seq"), axis=0, tiled=True),
        lax.all_gather(up_weight.astype(jnp.bfloat16), ("dp", "seq"), axis=0, tiled=True),
        lax.all_gather(down_weight.astype(jnp.bfloat16), ("dp", "seq"), axis=0, tiled=True),
        lax.all_gather(norm_one.astype(jnp.bfloat16), ("dp", "seq"), axis=0, tiled=True),
        lax.all_gather(norm_two.astype(jnp.bfloat16), ("dp", "seq"), axis=0, tiled=True),
        lax.all_gather(kernel.astype(jnp.bfloat16), ("dp", "seq"), axis=1, tiled=True),
    )
    in_back, out_back, gate_back, up_back, down_back = (
        regathered[0],
        regathered[1],
        regathered[2],
        regathered[3],
        regathered[4],
    )
    grad_low = cotangent[0]
    grad_seed = grad_low.astype(jnp.float32)
    grad_down = matmul_tn(active, grad_low)
    grad_active = matmul_nt(grad_low, down_back)
    sigmoid_gate = jax.nn.sigmoid(gate_pre)
    grad_gate_pre = (
        grad_active * up_pre * sigmoid_gate * (1.0 + gate_pre * (1.0 - sigmoid_gate))
    ).astype(jnp.bfloat16)
    grad_up_pre = (grad_active * swish).astype(jnp.bfloat16)
    grad_gate = matmul_tn(normed_b, grad_gate_pre)
    grad_up = matmul_tn(normed_b, grad_up_pre)
    grad_normed_b = matmul_nt(grad_gate_pre, gate_back) + matmul_nt(grad_up_pre, up_back)
    grad_gain_b = jnp.sum(grad_normed_b * unit_b, axis=0)
    grad_hidden = grad_seed + norm_back(grad_normed_b * gain_bf, unit_b, inverse_b)
    grad_branch = grad_hidden.astype(jnp.bfloat16)
    grad_out = matmul_tn(gated, grad_branch)
    grad_gated = matmul_nt(grad_branch, out_back)
    grad_c = grad_gated * convolved
    grad_conv = grad_gated * c_part
    next_rows = from_behind(grad_conv[:2], "seq", -1)
    ahead_grad = jnp.concatenate([grad_conv, next_rows], axis=0)
    grad_conv_in = (
        kernel_f[0] * grad_conv
        + kernel_f[1] * (ahead_grad[1 : count_rows + 1] * ahead_one)
        + kernel_f[2] * (ahead_grad[2 : count_rows + 2] * ahead_two)
    )
    grad_kernel = jnp.stack(
        [
            jnp.sum(grad_conv * current, axis=0),
            jnp.sum(grad_conv * prev_one, axis=0),
            jnp.sum(grad_conv * prev_two, axis=0),
        ]
    )
    grad_mixed = jnp.concatenate(
        [grad_conv_in * x_part, grad_c, grad_conv_in * b_part], axis=1
    ).astype(jnp.bfloat16)
    grad_in = matmul_tn(normed_a, grad_mixed)
    grad_normed_a = matmul_nt(grad_mixed, in_back)
    grad_gain_a = jnp.sum(grad_normed_a * unit_a, axis=0)
    grad_resident = grad_hidden + norm_back(grad_normed_a * gain_af, unit_a, inverse_a)
    kernel_rows = jnp.transpose(grad_kernel)
    summed = spread_all(
        (grad_in, grad_out, grad_gate, grad_up, grad_down, grad_gain_a, grad_gain_b, kernel_rows)
    )
    reduced = (
        summed[0],
        summed[1],
        summed[2],
        summed[3],
        summed[4],
        summed[5],
        summed[6],
        jnp.transpose(summed[7]),
    )
    return (
        output.astype(jnp.bfloat16)[None],
        grad_resident.astype(jnp.bfloat16)[None],
        reduced[0],
        reduced[1],
        reduced[2],
        reduced[3],
        reduced[4],
        reduced[5],
        reduced[6],
        reduced[7],
    )


def solution(mesh):
    return jax.shard_map(
        body,
        mesh=mesh,
        in_specs=(
            P("dp", "seq", None),
            P("dp", None),
            P("dp", "seq", None),
            P(("dp", "seq"), None),
            P(("dp", "seq"), None),
            P(("dp", "seq"), None),
            P(("dp", "seq"), None),
            P(("dp", "seq"), None),
            P(("dp", "seq")),
            P(("dp", "seq")),
            P(None, ("dp", "seq")),
        ),
        out_specs=(
            P("dp", "seq", None),
            P("dp", "seq", None),
            P(("dp", "seq"), None),
            P(("dp", "seq"), None),
            P(("dp", "seq"), None),
            P(("dp", "seq"), None),
            P(("dp", "seq"), None),
            P(("dp", "seq")),
            P(("dp", "seq")),
            P(None, ("dp", "seq")),
        ),
        check_vma=False,
    )
```

profile of v0, /device:TPU:0, one launch (start us, length us, event | category | flops | bytes accessed | tf_op | source)
XLA Modules:
  0.0 1334.6 jit_solution(15763101258723438557)
XLA Ops:
  18.0 42.1 %all-reduce.10 = (bf16[1024]{0:T(1024)(128)(2,1)S(1)}, bf16[1024]{0:T(1024)(128)(2,1)S(1)}) all-reduce(bf16[1024]{0:T(1024)(128)(2,1)S(1)} %dynamic-update-slice, bf16[1024]{0:T(1024)(128)(2,1)S(1)} %dynamic-update-slice.1), channel_id=1, replica_groups=mesh['dp'=4,'seq'=8] {'dp','seq'}, use_global_device_ids=true, to_apply=%add | all-reduce | flops 2048 | bytes 8192
  60.8 40.6 %all-gather = bf16[32,32,3]{1,2,0:T(4,128)(2,1)S(1)} all-gather(bf16[1,32,3]{1,2,0:T(4,128)(2,1)S(1)} %convert_bitcast_fusion.1), channel_id=1, replica_groups=mesh['dp'=4,'seq'=8] {'dp','seq'}, dimensions={0}, use_global_device_ids=true | all-gather | bytes 6336 | tf_op jit(solution)/shard_map/all_gather | solution.py:133
  111.5 31.5 %all-gather.9.cloned.1.call-done = bf16[1024,1024]{1,0:T(8,128)(2,1)} async-done(((bf16[32,1024]{1,0:T(8,128)(2,1)}), bf16[1024,1024]{1,0:T(8,128)(2,1)}) %all-gather.9.cloned.1.call-update) | async-done | bytes 2097168 | tf_op jit(solution)/shard_map/all_gather | solution.py:127
  145.6 82.0 %all-gather.11.cloned.1.call-done = bf16[1024,4608]{1,0:T(8,128)(2,1)} async-done(((bf16[32,4608]{1,0:T(8,128)(2,1)}), bf16[1024,4608]{1,0:T(8,128)(2,1)}) %all-gather.11.cloned.1.call-update) | async-done | bytes 9437200 | tf_op jit(solution)/shard_map/all_gather | solution.py:128
  227.6 8.1 fusion.50
  235.6 76.1 %all-gather.13.cloned.1.call-done = bf16[1024,4608]{1,0:T(8,128)(2,1)} async-done(((bf16[32,4608]{1,0:T(8,128)(2,1)}), bf16[1024,4608]{1,0:T(8,128)(2,1)}) %all-gather.13.cloned.1.call-update) | async-done | bytes 9437200 | tf_op jit(solution)/shard_map/all_gather | solution.py:129
  311.8 10.7 fusion
  322.5 73.5 %all-gather.15.cloned.1.call-done = bf16[4608,1024]{1,0:T(8,128)(2,1)} async-done(((bf16[144,1024]{1,0:T(8,128)(2,1)}), bf16[4608,1024]{1,0:T(8,128)(2,1)}) %all-gather.15.cloned.1.call-update) | async-done | bytes 9437200 | tf_op jit(solution)/shard_map/all_gather | solution.py:130
  395.9 12.2 multiply_convert_fusion
  408.2 6.9 fusion.51
  471.5 41.7 %all-to-all-done.1 = bf16[4,8,32,1024]{3,2,0,1:T(8,128)(2,1)} async-done(((bf16[4,8,32,1024]{3,2,0,1:T(8,128)(2,1)}), bf16[4,8,32,1024]{3,2,0,1:T(8,128)(2,1)}, u32[]{:S(2)}, u32[]{:S(2)}) %all-to-all-start.1) | async-done | bytes 2097184 | tf_op jit(solution)/shard_map/all_to_all | solution.py:58
  518.0 6.8 convolution_convert_fusion.1
  524.8 8.3 copy.61
  533.2 123.8 %all-to-all-done = bf16[4,8,32,3072]{3,2,0,1:T(8,128)(2,1)} async-done(((bf16[4,8,32,3072]{3,2,0,1:T(8,128)(2,1)}), bf16[4,8,32,3072]{3,2,0,1:T(8,128)(2,1)}, u32[]{:S(2)}, u32[]{:S(2)}) %all-to-all-start) | async-done | bytes 6291488 | tf_op jit(solution)/shard_map/all_to_all | solution.py:55
  662.0 6.8 convolution_convert_fusion
  668.8 8.4 copy.62
  677.1 191.2 %all-to-all-done.2 = bf16[4,8,32,4608]{3,2,0,1:T(8,128)(2,1)} async-done(((bf16[4,8,32,4608]{3,2,0,1:T(8,128)(2,1)}), bf16[4,8,32,4608]{3,2,0,1:T(8,128)(2,1)}, u32[]{:S(2)}, u32[]{:S(2)}) %all-to-all-start.2) | async-done | bytes 9437216 | tf_op jit(solution)/shard_map/all_to_all | solution.py:61
  882.7 9.1 copy.64
  891.8 188.4 %all-to-all-done.3 = bf16[4,8,32,4608]{3,2,0,1:T(8,128)(2,1)} async-done(((bf16[4,8,32,4608]{3,2,0,1:T(8,128)(2,1)}), bf16[4,8,32,4608]{3,2,0,1:T(8,128)(2,1)}, u32[]{:S(2)}, u32[]{:S(2)}) %all-to-all-start.3) | async-done | bytes 9437216 | tf_op jit(solution)/shard_map/all_to_all | solution.py:64
  1106.9 10.1 fusion.13
  1119.6 9.5 all-reduce.11
  1133.0 158.7 %all-to-all-done.4 = bf16[4,8,144,1024]{3,2,0,1:T(8,128)(2,1)} async-done(((bf16[4,8,144,1024]{3,2,0,1:T(8,128)(2,1)}), bf16[4,8,144,1024]{3,2,0,1:T(8,128)(2,1)}, u32[]{:S(2)}, u32[]{:S(2)}) %all-to-all-start.4) | async-done | bytes 9437216 | tf_op jit(solution)/shard_map/all_to_all | solution.py:67
  1291.6 7.4 reduce_sum.185
  1304.5 21.3 %reduce-scatter.24.cloned.1.call-done = bf16[1,144,1024]{2,1,0:T(8,128)(2,1)} async-done(((bf16[4,144,1024]{2,1,0:T(8,128)(2,1)}), bf16[1,144,1024]{2,1,0:T(8,128)(2,1)}) %reduce-scatter.24.cloned.1.call-update) | async-done | bytes 294928
  (166 shorter events, 144.5 us)
Async XLA Ops:
  7.2 94.5 %copy-start.6 = (bf16[1,256,1024]{2,1,0:T(8,128)(2,1)S(1)}, bf16[1,256,1024]{2,1,0:T(8,128)(2,1)}, u32[]{:S(2)}) copy-start(bf16[1,256,1024]{2,1,0:T(8,128)(2,1)} %param.11) | copy-start | bytes 1572868
  7.2 94.7 %all-gather.7.cloned.1.call-start = ((), (), s32[]{:S(2)}) async-start(), calls=%async_computation.13 | async-start | bytes 6488064 | tf_op jit(solution)/shard_map/all_gather | solution.py:126
  9.0 133.9 %all-gather.9.cloned.1.call-start = ((), (), s32[]{:S(2)}) async-start(), calls=%async_computation.14 | async-start | bytes 2162688 | tf_op jit(solution)/shard_map/all_gather | solution.py:127
  10.6 216.9 %all-gather.11.cloned.1.call-start = ((), (), s32[]{:S(2)}) async-start(), calls=%async_computation.15 | async-start | bytes 9732096 | tf_op jit(solution)/shard_map/all_gather | solution.py:128
  12.5 299.2 %all-gather.13.cloned.1.call-start = ((), (), s32[]{:S(2)}) async-start(), calls=%async_computation.16 | async-start | bytes 9732096 | tf_op jit(solution)/shard_map/all_gather | solution.py:129
  14.4 381.5 %all-gather.15.cloned.1.call-start = ((), (), s32[]{:S(2)}) async-start(), calls=%async_computation.17 | async-start | bytes 9732096 | tf_op jit(solution)/shard_map/all_gather | solution.py:130
  106.8 3.0 collective-permute-start
  111.5 124.2 %copy-start.9 = (bf16[256,1024]{1,0:T(8,128)(2,1)}, bf16[256,1024]{1,0:T(8,128)(2,1)S(1)}, u32[]{:S(2)}) copy-start(bf16[256,1024]{1,0:T(8,128)(2,1)S(1)} %get-tuple-element.25) | copy-start | bytes 1572868
  145.4 273.9 %copy-start.1 = (f32[256,1024]{1,0:T(8,128)}, f32[256,1024]{1,0:T(8,128)S(1)}, u32[]{:S(2)}) copy-start(f32[256,1024]{1,0:T(8,128)S(1)} %get-tuple-element.39) | copy-start | bytes 3145732
  145.5 166.2 %copy-start.3 = (bf16[256,1024]{1,0:T(8,128)(2,1)}, bf16[256,1024]{1,0:T(8,128)(2,1)S(1)}, u32[]{:S(2)}) copy-start(bf16[256,1024]{1,0:T(8,128)(2,1)S(1)} %multiply_convert_fusion.13) | copy-start | bytes 1572868
  423.1 8.2 collective-permute-start.1
  425.0 15.1 %all-to-all-start.6 = ((bf16[4,8,32]{2,0,1:T(4,128)(2,1)}), bf16[4,8,32]{2,0,1:T(4,128)(2,1)S(1)}, u32[]{:S(2)}, u32[]{:S(2)}) async-start(bf16[4,8,32]{2,0,1:T(4,128)(2,1)} %copy.66), calls=%async_computation.6 | async-start | bytes 16384 | tf_op jit(solution)/shard_map/all_to_all | solution.py:73
  440.2 10.7 all-to-all-start.7
  450.9 8.9 all-to-all-start.5
  459.8 53.4 %all-to-all-start.1 = ((bf16[4,8,32,1024]{3,2,0,1:T(8,128)(2,1)}), bf16[4,8,32,1024]{3,2,0,1:T(8,128)(2,1)}, u32[]{:S(2)}, u32[]{:S(2)}) async-start(bf16[4,8,32,1024]{3,2,0,1:T(8,128)(2,1)} %copy.60), calls=%async_computation.1 | async-start | bytes 4194304 | tf_op jit(solution)/shard_map/all_to_all | solution.py:58
  513.2 143.8 %all-to-all-start = ((bf16[4,8,32,3072]{3,2,0,1:T(8,128)(2,1)}), bf16[4,8,32,3072]{3,2,0,1:T(8,128)(2,1)}, u32[]{:S(2)}, u32[]{:S(2)}) async-start(bf16[4,8,32,3072]{3,2,0,1:T(8,128)(2,1)} %copy.59), calls=%async_computation | async-start | bytes 12582912 | tf_op jit(solution)/shard_map/all_to_all | solution.py:55
  656.9 211.4 %all-to-all-start.2 = ((bf16[4,8,32,4608]{3,2,0,1:T(8,128)(2,1)}), bf16[4,8,32,4608]{3,2,0,1:T(8,128)(2,1)}, u32[]{:S(2)}, u32[]{:S(2)}) async-start(bf16[4,8,32,4608]{3,2,0,1:T(8,128)(2,1)} %copy.61), calls=%async_computation.2 | async-start | bytes 18874368 | tf_op jit(solution)/shard_map/all_to_all | solution.py:61
  868.4 211.8 %all-to-all-start.3 = ((bf16[4,8,32,4608]{3,2,0,1:T(8,128)(2,1)}), bf16[4,8,32,4608]{3,2,0,1:T(8,128)(2,1)}, u32[]{:S(2)}, u32[]{:S(2)}) async-start(bf16[4,8,32,4608]{3,2,0,1:T(8,128)(2,1)} %copy.62), calls=%async_computation.3 | async-start | bytes 18874368 | tf_op jit(solution)/shard_map/all_to_all | solution.py:64
  1080.2 211.4 %all-to-all-start.4 = ((bf16[4,8,144,1024]{3,2,0,1:T(8,128)(2,1)}), bf16[4,8,144,1024]{3,2,0,1:T(8,128)(2,1)}, u32[]{:S(2)}, u32[]{:S(2)}) async-start(bf16[4,8,144,1024]{3,2,0,1:T(8,128)(2,1)} %copy.64), calls=%async_computation.4 | async-start | bytes 18874368 | tf_op jit(solution)/shard_map/all_to_all | solution.py:67
  1085.3 46.2 %reduce-scatter.18.cloned.1.call-start = ((), (), s32[]{:S(2)}) async-start(), calls=%async_computation.19 | async-start | bytes 327680
  1088.1 211.0 %reduce-scatter.16.cloned.1.call-start = ((), (), s32[]{:S(2)}) async-start(), calls=%async_computation.18 | async-start | bytes 983040
  1093.2 207.7 %reduce-scatter.20.cloned.1.call-start = ((), (), s32[]{:S(2)}) async-start(), calls=%async_computation.20 | async-start | bytes 1474560
  1099.7 203.0 %reduce-scatter.22.cloned.1.call-start = ((), (), s32[]{:S(2)}) async-start(), calls=%async_computation.21 | async-start | bytes 1474560
  1106.9 218.9 %reduce-scatter.24.cloned.1.call-start = ((), (), s32[]{:S(2)}) async-start(), calls=%async_computation.22 | async-start | bytes 1474560
  (20 other events, 343.1 us)
Sparse Core Ops, SparseCore 0:
  11.6 72.7 all-gather.6
  87.9 55.0 all-gather.8
  146.6 80.9 all-gather.10
  231.0 80.7 all-gather.12
  315.2 80.7 all-gather.14
  1089.1 24.4 reduce-scatter.17
  1116.8 26.1 reduce-scatter.15
  1146.2 28.5 reduce-scatter.19
  1177.9 28.5 reduce-scatter.21
  1299.2 26.4 reduce-scatter.23
where the time goes:
time: 1340 us; the launch traced here: 1330 us
  waiting for transfers between devices  996 us (74%)
  blocking collectives  92.2 us (7%)
  matrix products  86.7 us (6%)
  other arithmetic  62.1 us (5%)
  starting transfers between devices  42.5 us (3%)
  local copies, waits for them, and re-layouts  40.1 us (3%)
  between operations  14.9 us (1%)
    all_to_all x1, waiting for transfers between devices, spread_all(): lax.all_to_all(shaped[2].astype(jnp.bfloat16), 'seq', split_axis=1, conca...  191 us
    all_to_all x1, waiting for transfers between devices, spread_all(): lax.all_to_all(shaped[3].astype(jnp.bfloat16), 'seq', split_axis=1, conca...  188 us
    all_to_all x1, waiting for transfers between devices, spread_all(): lax.all_to_all(shaped[4].astype(jnp.bfloat16), 'seq', split_axis=1, conca...  159 us
    all_to_all x1, waiting for transfers between devices, spread_all(): lax.all_to_all(shaped[0].astype(jnp.bfloat16), 'seq', split_axis=1, conca...  124 us
    all_gather x1, waiting for transfers between devices, body(): lax.all_gather(gate_weight.astype(jnp.bfloat16), ('dp', 'seq'), axis=0, t...  82 us
    all_gather x1, waiting for transfers between devices, body(): lax.all_gather(up_weight.astype(jnp.bfloat16), ('dp', 'seq'), axis=0, til...  76.1 us
    all_gather x1, waiting for transfers between devices, body(): lax.all_gather(down_weight.astype(jnp.bfloat16), ('dp', 'seq'), axis=0, t...  73.5 us
    unnamed x2, blocking collectives  51.6 us
  transfers between devices with their start and end apart: 20, of which 13 were waited for; matrix products, arithmetic and copies ran while one was open for 12% of the time, Pallas kernels for 0%

commit v1 on v0

v1 whole, which is shorter than its diff:
```python
import functools

import jax
import jax.numpy as jnp
from jax import lax
from jax.experimental import pallas as pl
from jax.experimental.pallas import tpu as pltpu
from jax.sharding import PartitionSpec as P

epsilon = 1e-05
MESH = pl.DeviceIdType.MESH
BF = jnp.bfloat16
F32 = jnp.float32


def dot_nn(a, b):
    return jnp.dot(a, b, preferred_element_type=F32)


def dot_nt(a, b):
    return lax.dot_general(a, b, (((1,), (1,)), ((), ())), preferred_element_type=F32)


def dot_tn(a, b):
    return lax.dot_general(a, b, (((0,), (0,)), ((), ())), preferred_element_type=F32)


def when(pred, body):
    if pred is True:
        body()
    else:
        pl.when(pred)(body)


GAIN, IN, OUT, GU0, DOWN, GU1, GU2 = range(7)
UNITS = (GAIN, IN, OUT, GU0, DOWN, GU1, GU2)
SLOT = {IN: 0, GU0: 1, GU1: 2, GU2: 3}
AX, AZ, AO, AR = range(4)


def block_kernel(
    dims,
    x_ref, do_ref, mask_ref, gain_ref, win_ref, wout_ref, wg_ref, wu_ref, wdn_ref,
    out_ref, gtok_ref, rbuf, gout_ref, gdown_ref, gsmall_ref,
    stage, wall, wo, wd, gb, gv, xa, ma, za, oa, ra, big, mbuf, pbuf, ybuf, halo_p, halo_q,
    sb_a, rx_a, ry_a, fx_a, fy_a, rx_b, ry_b, fx_b, fy_b, hid, own, dh,
    gw, gd, go, dd_g, dd_d, dd_o, up_g, up_d, up_o, dn_g, dn_d, dn_o,
    gvec, sg, sgx, s2, dd_s, up_s, dn_s,
    zs, zr, ws, wr, gs, gr, ms, mr, hs, hr, ags, agr, rss, rsr, ds_, dr_, us, ur, vs, vr, qs, qr, ss, sr, ins,
):
    tok, wid, nz, rows, ch, fs, cj, uw, drows = dims
    half = tok // 2
    d = lax.axis_index("dp")
    s = lax.axis_index("seq")
    x = lax.rem(d, 2)
    y = lax.div(d, 2)
    z = lax.div(s, 2)
    c = lax.rem(s, 2)
    xn = 2 * y + (1 - x)
    yn = 2 * (1 - y) + x
    dg = 2 * (1 - y) + (1 - x)
    oc = 1 - c
    top = nz - 1
    to_x, to_y, to_g = (xn, s), (yn, s), (dg, s)
    to_sib = (d, 2 * z + oc)
    to_up, to_dn = (d, s + 2), (d, s - 2)
    to_next, to_prev = (d, s + 1), (d, s - 1)
    pending = []

    def copy(src, dst, ssem, rsem, tgt):
        return pltpu.make_async_remote_copy(
            src_ref=src(), dst_ref=dst(), send_sem=ssem(), recv_sem=rsem(), device_id=tgt, device_id_type=MESH
        )

    def send(tag, pred, src, dst, ssem, rsem, tgt):
        when(pred, lambda: copy(src, dst, ssem, rsem, tgt).start())
        pending.append((tag, pred, src, dst, ssem, rsem, tgt))

    def recv(pred, dst, rsem):
        when(pred, lambda: copy(dst, dst, rsem, rsem, to_sib).wait_recv())

    def drain(tag=None):
        keep = []
        for item in pending:
            if tag is None or item[0] == tag:
                when(item[1], lambda item=item: copy(*item[2:]).wait_send())
            else:
                keep.append(item)
        pending[:] = keep

    barrier = pltpu.get_barrier_semaphore()

    def greet(tgt):
        pl.semaphore_signal(barrier, inc=1, device_id=tgt, device_id_type=MESH)

    for tgt in (to_x, to_y, to_g, to_sib):
        greet(tgt)
    has_up, has_dn = z < top, z > 0
    pl.when(has_up)(lambda: greet(to_up))
    pl.when(has_dn)(lambda: greet(to_dn))
    cross_next = jnp.logical_and(c == 1, z < top)
    cross_prev = jnp.logical_and(c == 0, z > 0)
    pl.when(cross_next)(lambda: greet(to_next))
    pl.when(cross_prev)(lambda: greet(to_prev))
    ones = [jnp.where(p, 1, 0) for p in (has_up, has_dn, cross_next, cross_prev)]
    pl.semaphore_wait(barrier, 4 + ones[0] + ones[1] + ones[2] + ones[3])

    def cols(unit):
        return pl.ds(SLOT[unit] * uw, uw)

    def w_block(unit, zz, cc):
        if unit == GAIN:
            return gb.at[d, zz, cc]
        if unit == OUT:
            return wo.at[pl.ds(pl.multiple_of((2 * zz + cc) * rows, rows), rows), :]
        if unit == DOWN:
            return wd.at[pl.ds(pl.multiple_of((2 * zz + cc) * drows, drows), drows), :]
        return wall.at[:, zz, cc, :, cols(unit)]

    def z_send(unit, pred, zz, ssem, tgt):
        blk = lambda: w_block(unit, zz, c)
        send("w", pred, blk, blk, lambda: zs.at[unit * 13 + ssem], lambda: zr.at[unit * 2 * nz + 2 * zz + c], tgt)

    def z_own(unit):
        z_send(unit, has_up, z, 0, to_up)
        z_send(unit, has_dn, z, 3, to_dn)
        z_send(unit, True, z, 6, to_sib)

    def z_fwd(unit, k):
        low, high = z - k, z + k
        has_low, has_high = z >= k, z + k <= top
        recv(has_low, lambda: w_block(unit, low, c), lambda: zr.at[unit * 2 * nz + 2 * low + c])
        if k < top:
            z_send(unit, jnp.logical_and(has_low, has_up), low, k, to_up)
        z_send(unit, has_low, low, 6 + k, to_sib)
        recv(has_high, lambda: w_block(unit, high, c), lambda: zr.at[unit * 2 * nz + 2 * high + c])
        if k < top:
            z_send(unit, jnp.logical_and(has_high, has_dn), high, 3 + k, to_dn)
        z_send(unit, has_high, high, 9 + k, to_sib)

    def z_finish(unit):
        for zz in range(nz):
            recv(True, lambda zz=zz: w_block(unit, zz, oc), lambda zz=zz: zr.at[unit * 2 * nz + 2 * zz + oc])

    peers = ((xn, to_x), (yn, to_y), (dg, to_g))

    def w_slice(unit):
        u = SLOT[unit]
        wall[d, z, c, :, cols(unit)] = stage[d, :, cols(unit)]
        for k, (idx, tgt) in enumerate(peers):
            send(
                "stage", True,
                lambda idx=idx: stage.at[idx, :, cols(unit)],
                lambda: wall.at[d, z, c, :, cols(unit)],
                lambda k=k: ws.at[u * 3 + k], lambda k=k: wr.at[u * 3 + k], tgt,
            )

    def w_slice_wait(unit):
        u = SLOT[unit]
        for k, (idx, _) in enumerate(peers):
            recv(True, lambda idx=idx: wall.at[idx, z, c, :, cols(unit)], lambda k=k: wr.at[u * 3 + k])

    lo, hi = pl.ds(0, half), pl.ds(half, half)

    def ag_send(a, buf, idx, part, k, rk, tgt):
        blk = lambda: buf.at[idx, part, :]
        send("ag", True, blk, blk, lambda: ags.at[a * 6 + k], lambda: agr.at[a * 6 + rk], tgt)

    def ag_start(a, buf):
        ag_send(a, buf, d, hi, 0, 1, to_x)
        ag_send(a, buf, d, lo, 1, 2, to_y)
        ag_send(a, buf, d, lo, 2, 0, to_x)
        ag_send(a, buf, d, hi, 3, 3, to_y)

    def ag_recv(a, buf, idx, part, rk):
        recv(True, lambda: buf.at[idx, part, :], lambda: agr.at[a * 6 + rk])

    def ag_fwd(a, buf):
        ag_recv(a, buf, yn, lo, 2)
        ag_send(a, buf, yn, lo, 4, 4, to_x)
        ag_recv(a, buf, xn, hi, 1)
        ag_send(a, buf, xn, hi, 5, 5, to_y)

    def ag_near(a, buf):
        ag_recv(a, buf, xn, lo, 0)
        ag_recv(a, buf, yn, hi, 3)

    def ag_far(a, buf):
        ag_recv(a, buf, dg, lo, 4)
        ag_recv(a, buf, dg, hi, 5)

    def rs_send(r, tag, src, dst, k, tgt):
        send(tag, True, src, dst, lambda: rss.at[r * 6 + k], lambda: rsr.at[r * 6 + k], tgt)

    def rs_run(r, sb, bufs, tile, tag, first=0):
        wide = pl.ds(first, wid)
        rx, ry, fx, fy = bufs
        sb[dg, :, wide] = tile(dg).astype(BF)
        rs_send(r, tag, lambda: sb.at[dg, lo, wide], lambda: fx, 0, to_x)
        rs_send(r, tag, lambda: sb.at[dg, hi, wide], lambda: fy, 1, to_y)
        sb[xn, :, wide] = tile(xn).astype(BF)
        rs_send(r, tag, lambda: sb.at[xn, lo, wide], lambda: rx.at[lo, :], 2, to_x)
        sb[yn, :, wide] = tile(yn).astype(BF)
        rs_send(r, tag, lambda: sb.at[yn, hi, wide], lambda: ry.at[hi, :], 3, to_y)

    def rs_pass(r, sb, bufs, tag, first=0):
        wide = pl.ds(first, wid)
        rx, ry, fx, fy = bufs
        recv(True, lambda: fx, lambda: rsr.at[r * 6 + 0])
        sb[yn, lo, wide] = (sb[yn, lo, wide].astype(F32) + fx[...].astype(F32)).astype(BF)
        rs_send(r, tag, lambda: sb.at[yn, lo, wide], lambda: ry.at[lo, :], 4, to_y)
        recv(True, lambda: fy, lambda: rsr.at[r * 6 + 1])
        sb[xn, hi, wide] = (sb[xn, hi, wide].astype(F32) + fy[...].astype(F32)).astype(BF)
        rs_send(r, tag, lambda: sb.at[xn, hi, wide], lambda: rx.at[hi, :], 5, to_x)

    def rs_wait(r, bufs):
        rx, ry, fx, fy = bufs
        recv(True, lambda: rx.at[lo, :], lambda: rsr.at[r * 6 + 2])
        recv(True, lambda: ry.at[hi, :], lambda: rsr.at[r * 6 + 3])
        recv(True, lambda: ry.at[lo, :], lambda: rsr.at[r * 6 + 4])
        recv(True, lambda: rx.at[hi, :], lambda: rsr.at[r * 6 + 5])

    bufs_a = (rx_a, ry_a, fx_a, fy_a)
    bufs_b = (rx_b, ry_b, fx_b, fy_b)

    def g_own(unit, zz, cc):
        if unit == GAIN:
            return s2.at[zz, cc]
        if unit == OUT:
            return go.at[pl.ds(pl.multiple_of((2 * zz + cc) * rows, rows), rows), :]
        if unit == DOWN:
            return gd.at[pl.ds(pl.multiple_of((2 * zz + cc) * drows, drows), drows), :]
        return gw.at[:, zz, cc, :, cols(unit)]

    def g_in(unit, trio, zz):
        buf = trio[{GAIN: 3, OUT: 2, DOWN: 1}.get(unit, 0)]
        if unit in SLOT:
            return buf.at[zz, :, :, cols(unit)]
        return buf.at[zz]

    t_dd = (dd_g, dd_d, dd_o, dd_s)
    t_up = (up_g, up_d, up_o, up_s)
    t_dn = (dn_g, dn_d, dn_o, dn_s)

    def g_pair(unit):
        for zz in range(nz):
            send(
                "g", True, lambda zz=zz: g_own(unit, zz, oc), lambda zz=zz: g_in(unit, t_dd, zz),
                lambda zz=zz: ds_.at[unit * nz + zz], lambda zz=zz: dr_.at[unit * nz + zz], to_sib,
            )

    def g_pair_wait(unit):
        for zz in range(nz):
            recv(True, lambda zz=zz: g_in(unit, t_dd, zz), lambda zz=zz: dr_.at[unit * nz + zz])

    def g_add(unit, dst, parts):
        shape = dst.shape
        if len(shape) == 3:
            for k in range(shape[0]):
                dst[k] = sum(p[k].astype(F32) for p in parts).astype(dst.dtype)
        else:
            dst[...] = sum(p[...].astype(F32) for p in parts).astype(dst.dtype)

    def g_up(unit, cond):
        for zt in range(top, 0, -1):
            pred = jnp.logical_and(cond, z < zt)
            mine, pair, came = (lambda: g_own(unit, zt, c)), (lambda: g_in(unit, t_dd, zt)), (lambda: g_in(unit, t_up, zt - 1))

            def first():
                g_add(unit, mine(), (mine(), pair()))

            def later():
                g_add(unit, mine(), (mine(), pair(), came()))

            recv(jnp.logical_and(pred, z > 0), came, lambda: ur.at[unit * top + zt - 1])
            pl.when(jnp.logical_and(pred, z == 0))(first)
            pl.when(jnp.logical_and(pred, z > 0))(later)
            send("g", pred, lambda zt=zt: g_own(unit, zt, c), lambda zt=zt: g_in(unit, t_up, zt - 1),
                 lambda zt=zt: us.at[(unit * top + zt - 1) * 2 + (0 if cond is low_z else 1)],
                 lambda zt=zt: ur.at[unit * top + zt - 1], to_up)

    def g_down(unit):
        for zt in range(top):
            pred = z > zt
            mine, pair, came = (lambda: g_own(unit, zt, c)), (lambda: g_in(unit, t_dd, zt)), (lambda: g_in(unit, t_dn, zt))

            def first():
                g_add(unit, mine(), (mine(), pair()))

            def later():
                g_add(unit, mine(), (mine(), pair(), came()))

            recv(jnp.logical_and(pred, z < top), came, lambda: vr.at[unit * top + zt])
            pl.when(jnp.logical_and(pred, z == top))(first)
            pl.when(jnp.logical_and(pred, z < top))(later)
            send("g", pred, lambda zt=zt: g_own(unit, zt, c), lambda zt=zt: g_in(unit, t_dn, zt),
                 lambda zt=zt: vs.at[unit * top + zt], lambda zt=zt: vr.at[unit * top + zt], to_dn)

    low_z = z < nz // 2
    high_z = z >= nz // 2

    def g_line(unit):
        g_up(unit, low_z)
        g_down(unit)
        g_up(unit, high_z)

    def g_last(unit, acc):
        up_ref = lambda: g_in(unit, t_up, z - 1)
        dn_ref = lambda: g_in(unit, t_dn, z)
        recv(has_dn, up_ref, lambda: ur.at[unit * top + z - 1])
        recv(has_up, dn_ref, lambda: vr.at[unit * top + z])
        g_add(unit, acc, (g_own(unit, z, c), g_in(unit, t_dd, z)))
        pl.when(has_dn)(lambda: g_add(unit, acc, (acc, up_ref())))
        pl.when(has_up)(lambda: g_add(unit, acc, (acc, dn_ref())))

    def g_rows(unit):
        facc = mbuf.at[:, pl.ds(0, rows), :]
        g_last(unit, facc)
        u = SLOT[unit]
        for k in range(4):
            stage[k, :, cols(unit)] = facc[k].astype(BF)
        rbuf[d, :, cols(unit)] = facc[d].astype(BF)
        for k, (idx, tgt) in enumerate(peers):
            send(
                "stage", True,
                lambda idx=idx: stage.at[idx, :, cols(unit)],
                lambda: rbuf.at[d, :, cols(unit)],
                lambda k=k: qs.at[u * 3 + k], lambda k=k: qr.at[u * 3 + k], tgt,
            )

    def g_rows_wait(unit):
        u = SLOT[unit]
        for k, (idx, _) in enumerate(peers):
            recv(True, lambda idx=idx: rbuf.at[idx, :, cols(unit)], lambda k=k: qr.at[u * 3 + k])

    count = 4 * fs // uw

    def wide_in(i):
        ref = wg_ref if i < count else wu_ref
        return pltpu.make_async_copy(
            ref.at[:, pl.ds((i % count) * uw, uw)], mbuf.at[i // 8, pl.ds((i % 8) * rows, rows), :], ins.at[i]
        )

    def wide_read(i, first, n):
        b = i * count + first // uw
        return mbuf[b // 8, pl.ds((b % 8) * rows, rows), pl.ds(first % uw, n)]

    for i in range(2 * count):
        wide_in(i).start()
    for k in range(4):
        for p in range(3):
            stage[k, :, pl.ds(p * ch, ch)] = win_ref[:, pl.ds(p * wid + k * ch, ch)].astype(BF)
    w_slice(IN)
    gb[d, z, c] = gain_ref[...]
    z_own(GAIN)
    xa[d] = x_ref[...]
    ag_start(AX, xa)
    ma[d] = mask_ref[...]
    for k, (idx, tgt) in enumerate(peers):
        send("ag", True, lambda: ma.at[d], lambda: ma.at[d], lambda k=k: ms.at[k], lambda k=k: mr.at[k], tgt)
    wo[pl.ds(pl.multiple_of(s * rows, rows), rows), :] = wout_ref[...].astype(BF)
    for i in range(2 * count):
        wide_in(i).wait()
    for k in range(4):
        for j in range(3):
            stage[k, :, pl.ds((1 + j) * uw, cj)] = wide_read(0, k * fs + j * cj, cj).astype(BF)
            stage[k, :, pl.ds((1 + j) * uw + cj, cj)] = wide_read(1, k * fs + j * cj, cj).astype(BF)
    w_slice_wait(IN)
    z_own(IN)
    z_own(OUT)
    for unit in (GU0, GU1, GU2):
        w_slice(unit)
    wd[pl.ds(pl.multiple_of(s * drows, drows), drows), :] = wdn_ref[...].astype(BF)
    z_fwd(GAIN, 1)
    z_fwd(IN, 1)
    ag_fwd(AX, xa)
    z_fwd(GAIN, 2)
    z_fwd(IN, 2)
    z_fwd(OUT, 1)
    w_slice_wait(GU0)
    z_own(GU0)
    z_fwd(GAIN, 3)
    z_finish(GAIN)
    for k, (idx, tgt) in enumerate(peers):
        send("w", True, lambda: gb.at[d], lambda: gb.at[d], lambda k=k: gs.at[k], lambda k=k: gr.at[k], tgt)
    z_fwd(IN, 3)
    z_fwd(OUT, 2)
    ag_near(AX, xa)
    for k, (idx, _) in enumerate(peers):
        recv(True, lambda idx=idx: gb.at[idx], lambda k=k: gr.at[k])
    per = 128 // rows
    for g in range(wid // 128):
        tot = None
        for i in range(g * per, (g + 1) * per):
            dd, q = i // (2 * nz), i % (2 * nz)
            piece = gb[dd, q // 2, q % 2].astype(F32)
            tot = piece if tot is None else tot + piece
        gv[:, pl.ds(g * 128, 128)] = tot
    ag_far(AX, xa)

    step = 32

    def norm_rows(xv):
        return lax.rsqrt(jnp.mean(xv * xv, axis=1, keepdims=True) + epsilon)

    zcol = pl.ds(0, wid)

    def make_z1():
        @pl.loop(0, 4 * tok // step)
        def _(i):
            dd = lax.div(i, tok // step)
            rr = pl.ds(pl.multiple_of(lax.rem(i, tok // step) * step, step), step)
            xv = xa[dd, rr, :].astype(F32)
            big[dd, rr, zcol] = (xv * norm_rows(xv) * gv[0:1, :]).astype(BF)

    make_z1()
    z_finish(IN)
    z_own(DOWN)
    z_fwd(GU0, 1)
    for k, (idx, _) in enumerate(peers):
        recv(True, lambda idx=idx: ma.at[idx], lambda k=k: mr.at[k])

    def unit_w(lo_col, n):
        return wall[:, :, :, :, pl.ds(lo_col, n)].reshape(wid, n)

    @pl.loop(0, 4)
    def _(dd):
        m = dot_nn(big[dd, :, zcol], unit_w(0, uw))
        mbuf[dd] = m
        pbuf[dd] = (m[:, :ch] * m[:, 2 * ch :]).astype(BF)

    tail = 16
    send("halo", s < 2 * nz - 1, lambda: pbuf.at[:, pl.ds(tok - tail, tail), :], lambda: halo_p,
         lambda: hs.at[0], lambda: hr.at[0], to_next)

    @pl.when(s == 0)
    def _():
        halo_p[...] = jnp.zeros_like(halo_p)

    z_fwd(OUT, 3)
    z_finish(OUT)
    recv(s > 0, lambda: halo_p, lambda: hr.at[0])
    tap_cols = pl.ds(pl.multiple_of(d * ch, ch), ch)
    row = lax.broadcasted_iota(jnp.int32, (tok, ch), 0)

    def past(dd):
        cur = pbuf[dd].astype(F32)
        old = halo_p[dd].astype(F32)
        masks = ma[dd].astype(F32)
        one = jnp.where(row == 0, old[tail - 1 : tail], pltpu.roll(cur, 1, 0)) * masks[:, 0:1]
        two = jnp.where(row == 0, old[tail - 2 : tail - 1], jnp.where(row == 1, old[tail - 1 : tail], pltpu.roll(cur, 2, 0)))
        return cur, one, two * masks[:, 1:2], masks

    def convolve(cur, one, two):
        return gv[2:3, tap_cols] * cur + gv[3:4, tap_cols] * one + gv[4:5, tap_cols] * two

    @pl.loop(0, 4)
    def _(dd):
        cur, one, two, _ = past(dd)
        ybuf[dd] = (mbuf[dd, :, pl.ds(ch, ch)] * convolve(cur, one, two)).astype(BF)

    def h_tile(dd):
        return dot_nn(ybuf[dd], wo[...])

    rs_run(0, sb_a, bufs_a, h_tile, "rs0")
    own[...] = h_tile(d)
    w_slice_wait(GU1)
    z_own(GU1)
    z_fwd(GU0, 2)
    rs_pass(0, sb_a, bufs_a, "rs0")
    z_fwd(DOWN, 1)
    z_fwd(GU0, 3)
    w_slice_wait(GU2)
    z_own(GU2)
    z_fwd(GU1, 1)
    z_fwd(DOWN, 2)
    rs_wait(0, bufs_a)

    @pl.loop(0, tok // step)
    def _(i):
        rr = pl.ds(pl.multiple_of(i * step, step), step)
        h = xa[d, rr, :].astype(F32) + own[rr, :] + rx_a[rr, :].astype(F32) + ry_a[rr, :].astype(F32)
        hid[rr, :] = h
        za[d, rr, :] = (h * norm_rows(h) * gv[1:2, :]).astype(BF)

    ag_start(AZ, za)
    oa[d] = do_ref[...]
    ag_start(AO, oa)
    z_fwd(GU1, 2)
    z_fwd(DOWN, 3)
    z_fwd(GU2, 1)
    ag_fwd(AZ, za)
    z_fwd(GU1, 3)
    z_fwd(GU2, 2)
    z_finish(GU0)
    ag_near(AZ, za)
    ag_far(AZ, za)
    ag_fwd(AO, oa)
    z_finish(DOWN)
    ag_near(AO, oa)
    ag_far(AO, oa)

    def gated(j):
        acol = pl.ds(j * cj, cj)
        gcol = pl.ds(fs + j * uw, cj)
        ucol = pl.ds(fs + j * uw + cj, cj)

        @pl.loop(0, 4)
        def _(dd):
            gu = dot_nn(za[dd], unit_w((1 + j) * uw, uw))
            da = dot_nt(oa[dd], wd[pl.ds(j * cj, cj), :])
            g, u = gu[:, :cj], gu[:, cj:]
            sig = jax.nn.sigmoid(g)
            sw = g * sig
            big[dd, :, acol] = (sw * u).astype(BF)
            big[dd, :, gcol] = (da * u * sig * (1.0 + g * (1.0 - sig))).astype(BF)
            big[dd, :, ucol] = (da * sw).astype(BF)

    def grad_gu(j):
        @pl.loop(0, 4)
        def _(dd):
            left = za[:, :, pl.ds(pl.multiple_of(dd * ch, ch), ch)].reshape(4 * tok, ch)
            right = big[:, :, pl.ds(fs + j * uw, uw)].reshape(4 * tok, uw)
            res = dot_tn(left, right).astype(BF)
            gw[dd, :, :, :, pl.ds((1 + j) * uw, uw)] = res.reshape(nz, 2, rows, uw)

    gated(0)
    grad_gu(0)
    g_pair(GU0)
    z_fwd(GU2, 3)
    z_finish(GU1)
    gated(1)
    z_finish(GU2)
    gated(2)

    drain("rs0")

    def dz2_tile(dd):
        return dot_nt(big[dd, :, pl.ds(fs, 3 * uw)], unit_w(uw, 3 * uw))

    rs_run(1, sb_a, bufs_a, dz2_tile, "rs1")
    own[...] = dz2_tile(d)
    rs_pass(1, sb_a, bufs_a, "rs1")
    g_pair_wait(GU0)
    g_line(GU0)
    grad_gu(1)
    g_pair(GU1)

    def grad_down(j):
        left = big[:, :, pl.ds(j * cj, cj)].reshape(4 * tok, cj)
        gd[pl.ds(j * cj, cj), :] = dot_tn(left, oa[...].reshape(4 * tok, wid)).astype(BF)

    rs_wait(1, bufs_a)
    gvec[...] = jnp.zeros_like(gvec)
    zero_row = jnp.zeros((8, wid), F32)

    def fold(v):
        return v.reshape(step // 8, 8, wid).sum(axis=0)

    def back_two(i, acc):
        rr = pl.ds(pl.multiple_of(i * step, step), step)
        dz = own[rr, :] + rx_a[rr, :].astype(F32) + ry_a[rr, :].astype(F32)
        h = hid[rr, :]
        inv = norm_rows(h)
        unit = h * inv
        e = dz * gv[1:2, :]
        g = oa[d, rr, :].astype(F32) + inv * (e - unit * jnp.mean(e * unit, axis=1, keepdims=True))
        dh[rr, :] = g
        ra[d, rr, :] = g.astype(BF)
        return acc + fold(dz * unit)

    gain2 = lax.fori_loop(0, tok // step, back_two, zero_row)
    gvec[1:2, :] = jnp.sum(gain2, axis=0, keepdims=True)
    ag_start(AR, ra)
    g_pair_wait(GU1)
    g_line(GU1)
    grad_gu(2)
    g_pair(GU2)
    ag_fwd(AR, ra)
    for j in range(3):
        grad_down(j)
    g_pair(DOWN)
    g_pair_wait(GU2)
    g_line(GU2)

    def out_tile(dd):
        return dot_nn(big[dd, :, pl.ds(0, fs)], wd[...])

    ag_near(AR, ra)
    ag_far(AR, ra)

    mcol = fs

    @pl.loop(0, 4)
    def _(dd):
        dy = dot_nt(ra[dd], wo[...])
        cur, one, two, _ = past(dd)
        q = dy * mbuf[dd, :, pl.ds(ch, ch)]
        mbuf[dd, :, pl.ds(ch, ch)] = q
        big[dd, :, pl.ds(mcol + ch, ch)] = (dy * convolve(cur, one, two)).astype(BF)
        gvec[2:3, tap_cols] = gvec[2:3, tap_cols] + jnp.sum(q * cur, axis=0, keepdims=True)
        gvec[3:4, tap_cols] = gvec[3:4, tap_cols] + jnp.sum(q * one, axis=0, keepdims=True)
        gvec[4:5, tap_cols] = gvec[4:5, tap_cols] + jnp.sum(q * two, axis=0, keepdims=True)

    head = 8
    send("halo", s > 0, lambda: mbuf.at[:, pl.ds(0, head), pl.ds(ch, ch)], lambda: halo_q, lambda: hs.at[1], lambda: hr.at[1], to_prev)

    @pl.when(s == 2 * nz - 1)
    def _():
        halo_q[...] = jnp.zeros_like(halo_q)

    rs_run(2, big, bufs_b, out_tile, "rs2", 2 * fs)
    own[...] = out_tile(d)
    rs_pass(2, big, bufs_b, "rs2", 2 * fs)
    make_z1()
    go[...] = dot_tn(ybuf[...].reshape(4 * tok, ch), ra[...].reshape(4 * tok, wid)).astype(BF)
    g_pair(OUT)
    g_pair_wait(DOWN)
    g_line(DOWN)
    recv(s < 2 * nz - 1, lambda: halo_q, lambda: hr.at[1])
    @pl.loop(0, 4)
    def _(dd):
        q = mbuf[dd, :, pl.ds(ch, ch)]
        new = halo_q[dd]
        masks = ma[dd].astype(F32)
        one = jnp.where(row == tok - 1, new[0:1], pltpu.roll(q, tok - 1, 0)) * masks[:, 2:3]
        two = jnp.where(row == tok - 2, new[0:1], jnp.where(row == tok - 1, new[1:2], pltpu.roll(q, tok - 2, 0)))
        dp = gv[2:3, tap_cols] * q + gv[3:4, tap_cols] * one + gv[4:5, tap_cols] * (two * masks[:, 3:4])
        big[dd, :, pl.ds(mcol, ch)] = (dp * mbuf[dd, :, pl.ds(2 * ch, ch)]).astype(BF)
        big[dd, :, pl.ds(mcol + 2 * ch, ch)] = (dp * mbuf[dd, :, pl.ds(0, ch)]).astype(BF)

    rs_wait(2, bufs_b)

    @pl.loop(0, tok // step)
    def _(i):
        rr = pl.ds(pl.multiple_of(i * step, step), step)
        out_ref[rr, :] = (hid[rr, :] + own[rr, :] + rx_b[rr, :].astype(F32) + ry_b[rr, :].astype(F32)).astype(BF)

    drain("rs1")

    def dz1_tile(dd):
        return dot_nt(big[dd, :, pl.ds(mcol, uw)], unit_w(0, uw))

    rs_run(3, sb_a, bufs_a, dz1_tile, "rs3")
    own[...] = dz1_tile(d)

    @pl.loop(0, 4)
    def _(dd):
        left = big[:, :, pl.ds(pl.multiple_of(dd * ch, ch), ch)].reshape(4 * tok, ch)
        right = big[:, :, pl.ds(mcol, uw)].reshape(4 * tok, uw)
        gw[dd, :, :, :, pl.ds(0, uw)] = dot_tn(left, right).astype(BF).reshape(nz, 2, rows, uw)

    g_pair(IN)
    rs_pass(3, sb_a, bufs_a, "rs3")
    g_pair_wait(OUT)
    g_line(OUT)
    g_pair_wait(IN)
    g_line(IN)
    drain("halo")
    drain("stage")
    g_rows(GU0)
    g_rows(GU1)
    g_rows(GU2)
    rs_wait(3, bufs_a)

    def back_one(i, acc):
        rr = pl.ds(pl.multiple_of(i * step, step), step)
        dz = own[rr, :] + rx_a[rr, :].astype(F32) + ry_a[rr, :].astype(F32)
        xv = xa[d, rr, :].astype(F32)
        inv = norm_rows(xv)
        unit = xv * inv
        e = dz * gv[0:1, :]
        g = dh[rr, :] + inv * (e - unit * jnp.mean(e * unit, axis=1, keepdims=True))
        gtok_ref[rr, :] = g.astype(BF)
        return acc + fold(dz * unit)

    gain1 = lax.fori_loop(0, tok // step, back_one, zero_row)
    gvec[0:1, :] = jnp.sum(gain1, axis=0, keepdims=True)
    for g in range(wid // 128):
        val = gvec[:, pl.ds(g * 128, 128)].astype(BF)
        for i in range(g * per, (g + 1) * per):
            dd, q = i // (2 * nz), i % (2 * nz)
            sg[dd, q // 2, q % 2] = val
    for k, (idx, tgt) in enumerate(peers):
        send("g", True, lambda idx=idx: sg.at[idx], lambda k=k: sgx.at[k], lambda k=k: ss.at[k], lambda k=k: sr.at[k], tgt)
    g_rows(IN)
    for unit in (GU0, GU1, GU2):
        g_rows_wait(unit)
    g_last(DOWN, gdown_ref)
    g_last(OUT, gout_ref)
    for k in range(3):
        recv(True, lambda k=k: sgx.at[k], lambda k=k: sr.at[k])
    for zz in range(nz):
        for cc in range(2):
            tot = sg[d, zz, cc].astype(F32)
            for k in range(3):
                tot = tot + sgx[k, zz, cc].astype(F32)
            s2[zz, cc] = tot.astype(BF)
    g_pair(GAIN)
    g_rows_wait(IN)
    g_pair_wait(GAIN)
    g_line(GAIN)
    g_last(GAIN, gsmall_ref)
    drain()


def fast_body(n_dp, n_seq, tokens, segments, cotangent, in_weight, out_weight, gate_weight, up_weight, down_weight, norm_one, norm_two, kernel):
    tok, wid = tokens.shape[1], tokens.shape[2]
    nz = n_seq // 2
    rows = in_weight.shape[0]
    drows = down_weight.shape[0]
    ch = wid // n_dp
    fs = gate_weight.shape[1] // n_dp
    uw = 3 * ch
    cj = uw // 2
    lanes = kernel.shape[1]
    place = lax.axis_index("dp") * n_seq + lax.axis_index("seq")
    lane0 = lax.rem(place, 128 // lanes) * lanes
    gains = jnp.concatenate([norm_one[None], norm_two[None], kernel], axis=0).astype(BF)
    gain_tile = lax.dynamic_update_slice(jnp.zeros((16, 128), BF), gains, (0, lane0))
    offset = lax.axis_index("seq") * tok
    filler = jnp.full((2,), -1, jnp.int32)
    near = lax.dynamic_slice_in_dim(jnp.concatenate([filler, segments[0], filler]), offset, tok + 4)
    mid = near[2 : tok + 2]
    same = [mid == near[1 : tok + 1], mid == near[0:tok], mid == near[3 : tok + 3], mid == near[4 : tok + 4]]
    masks = jnp.pad(jnp.stack(same, axis=1).astype(BF), ((0, 0), (0, 124)))

    dims = (tok, wid, nz, rows, ch, fs, cj, uw, drows)
    top = nz - 1
    vm = pltpu.VMEM
    dma = lambda n: pltpu.SemaphoreType.DMA((n,))
    plane = lambda w, t=BF: vm((n_dp, tok, w), t)
    rs_set = [vm((tok, wid), BF)] * 2 + [vm((tok // 2, wid), BF)] * 2
    scratch = [
        vm((n_dp, rows, 4 * uw), BF),
        vm((n_dp, nz, 2, rows, 4 * uw), BF),
        vm((ch, wid), BF),
        vm((fs, wid), BF),
        vm((n_dp, nz, 2, 16, 128), BF),
        vm((16, wid), F32),
        plane(wid), plane(128), plane(wid), plane(wid), plane(wid),
        plane(3 * fs),
        plane(uw, F32), plane(ch), plane(ch),
        vm((n_dp, 16, ch), BF),
        vm((n_dp, 8, ch), F32),
        plane(wid),
        *rs_set, *rs_set,
        vm((tok, wid), F32), vm((tok, wid), F32), vm((tok, wid), F32),
        vm((n_dp, nz, 2, rows, 4 * uw), BF), vm((fs, wid), BF), vm((ch, wid), BF),
        vm((nz, n_dp, rows, 4 * uw), BF), vm((nz, drows, wid), BF), vm((nz, rows, wid), BF),
        vm((top, n_dp, rows, 4 * uw), BF), vm((top, drows, wid), BF), vm((top, rows, wid), BF),
        vm((top, n_dp, rows, 4 * uw), BF), vm((top, drows, wid), BF), vm((top, rows, wid), BF),
        vm((16, wid), F32),
        vm((n_dp, nz, 2, 16, 128), BF),
        vm((3, nz, 2, 16, 128), BF),
        vm((nz, 2, 16, 128), BF),
        vm((nz, 16, 128), BF), vm((top, 16, 128), BF), vm((top, 16, 128), BF),
        dma(7 * 13), dma(7 * 2 * nz), dma(12), dma(12), dma(3), dma(3), dma(3), dma(3), dma(2), dma(2),
        dma(24), dma(24), dma(24), dma(24), dma(7 * nz), dma(7 * nz),
        dma(7 * top * 2), dma(7 * top), dma(7 * top), dma(7 * top), dma(12), dma(12), dma(3), dma(3), dma(8 * fs // uw),
    ]
    f32 = lambda a: jax.ShapeDtypeStruct(a.shape, F32)
    vspec = pl.BlockSpec(memory_space=vm)
    res = pl.pallas_call(
        functools.partial(block_kernel, dims),
        out_shape=(
            jax.ShapeDtypeStruct((tok, wid), BF), jax.ShapeDtypeStruct((tok, wid), BF),
            jax.ShapeDtypeStruct((n_dp, rows, 4 * uw), BF), f32(out_weight), f32(down_weight),
            jax.ShapeDtypeStruct((16, 128), F32),
        ),
        in_specs=[vspec] * 6 + [pl.BlockSpec(memory_space=pl.ANY)] * 2 + [vspec],
        out_specs=(vspec,) * 6,
        scratch_shapes=scratch,
        compiler_params=pltpu.CompilerParams(collective_id=0, has_side_effects=True, vmem_limit_bytes=64 * 1024 * 1024),
    )(tokens[0], cotangent[0], masks, gain_tile, in_weight, out_weight, gate_weight, up_weight, down_weight)
    grad_tile = res[2].astype(F32)
    grad_in = grad_tile[:, :, :uw].reshape(n_dp, rows, 3, ch).transpose(1, 2, 0, 3).reshape(rows, 3 * wid)
    pairs = grad_tile[:, :, uw:].reshape(n_dp, rows, 3, 2, cj).transpose(3, 1, 0, 2, 4).reshape(2, rows, n_dp * fs)
    small = lax.dynamic_slice(res[5], (0, lane0), (16, lanes))
    return (res[0][None], res[1][None], grad_in, res[3], pairs[0], pairs[1], res[4], small[0], small[1], small[2:5])


def gather(value, axis=0):
    return lax.all_gather(value.astype(BF), ("dp", "seq"), axis=axis, tiled=True)


def norm_back(grad_unit, unit_rows, inverse):
    return inverse * (grad_unit - unit_rows * jnp.mean(grad_unit * unit_rows, axis=1, keepdims=True))


def from_behind(value, axis, steps):
    count = lax.axis_size(axis)
    leading, last = (max(0, -steps), min(count, count - steps))
    return lax.ppermute(value, axis, [(source, source + steps) for source in range(leading, last)])


def spread(value):
    n_dp, n_seq = lax.axis_size("dp"), lax.axis_size("seq")
    shaped = value.reshape((n_dp, n_seq, value.shape[0] // (n_dp * n_seq)) + value.shape[1:]).astype(BF)
    moved = lax.all_to_all(shaped, "seq", split_axis=1, concat_axis=1, tiled=True).astype(F32)
    summed = jnp.sum(moved, axis=1).astype(BF)
    owned = lax.psum_scatter(summed, "dp", scatter_dimension=0, tiled=True).astype(F32)
    return owned.reshape(owned.shape[1:])


def plain_body(tokens, segments, cotangent, in_weight, out_weight, gate_weight, up_weight, down_weight, norm_one, norm_two, kernel):
    width, count = tokens.shape[2], tokens.shape[1]
    in_mat, out_mat, gate_mat, up_mat, down_mat = map(gather, (in_weight, out_weight, gate_weight, up_weight, down_weight))
    gain_a, gain_b = gather(norm_one).astype(F32), gather(norm_two).astype(F32)
    taps = gather(kernel, 1).astype(F32)
    filler = jnp.full((2,), -1, jnp.int32)
    near = lax.dynamic_slice_in_dim(jnp.concatenate([filler, segments[0], filler]), lax.axis_index("seq") * count, count + 4)
    mid = near[2 : count + 2]
    same = lambda first: (mid == near[first : count + first]).astype(F32)[:, None]
    resident = tokens[0].astype(F32)
    inverse_a = lax.rsqrt(jnp.mean(resident * resident, axis=1, keepdims=True) + epsilon)
    unit_a = resident * inverse_a
    normed_a = (unit_a * gain_a).astype(BF)
    mixed = dot_nn(normed_a, in_mat)
    b_part, c_part, x_part = mixed[:, :width], mixed[:, width : 2 * width], mixed[:, 2 * width :]
    conv_in = (b_part * x_part).astype(BF)
    extended = jnp.concatenate([from_behind(conv_in[count - 2 :], "seq", 1), conv_in], axis=0).astype(F32)
    current, prev_one, prev_two = extended[2:], extended[1 : count + 1] * same(1), extended[0:count] * same(0)
    convolved = taps[0] * current + taps[1] * prev_one + taps[2] * prev_two
    gated = (c_part * convolved).astype(BF)
    hidden = resident + dot_nn(gated, out_mat)
    inverse_b = lax.rsqrt(jnp.mean(hidden * hidden, axis=1, keepdims=True) + epsilon)
    unit_b = hidden * inverse_b
    normed_b = (unit_b * gain_b).astype(BF)
    gate_pre, up_pre = dot_nn(normed_b, gate_mat), dot_nn(normed_b, up_mat)
    sig = jax.nn.sigmoid(gate_pre)
    swish = gate_pre * sig
    active = (swish * up_pre).astype(BF)
    output = hidden + dot_nn(active, down_mat)
    grad_low = cotangent[0]
    grad_active = dot_nt(grad_low, down_mat)
    grad_gate_pre = (grad_active * up_pre * sig * (1.0 + gate_pre * (1.0 - sig))).astype(BF)
    grad_up_pre = (grad_active * swish).astype(BF)
    grad_normed_b = dot_nt(grad_gate_pre, gate_mat) + dot_nt(grad_up_pre, up_mat)
    grad_hidden = grad_low.astype(F32) + norm_back(grad_normed_b * gain_b, unit_b, inverse_b)
    grad_branch = grad_hidden.astype(BF)
    grad_gated = dot_nt(grad_branch, out_mat)
    grad_conv = grad_gated * c_part
    ahead = jnp.concatenate([grad_conv, from_behind(grad_conv[:2], "seq", -1)], axis=0)
    grad_conv_in = taps[0] * grad_conv + taps[1] * (ahead[1 : count + 1] * same(3)) + taps[2] * (ahead[2 : count + 2] * same(4))
    grad_taps = jnp.stack([jnp.sum(grad_conv * part, axis=0) for part in (current, prev_one, prev_two)])
    grad_mixed = jnp.concatenate([grad_conv_in * x_part, grad_gated * convolved, grad_conv_in * b_part], axis=1).astype(BF)
    grad_normed_a = dot_nt(grad_mixed, in_mat)
    grad_resident = grad_hidden + norm_back(grad_normed_a * gain_a, unit_a, inverse_a)
    return (
        output.astype(BF)[None],
        grad_resident.astype(BF)[None],
        spread(dot_tn(normed_a, grad_mixed)),
        spread(dot_tn(gated, grad_branch)),
        spread(dot_tn(normed_b, grad_gate_pre)),
        spread(dot_tn(normed_b, grad_up_pre)),
        spread(dot_tn(active, grad_low)),
        spread(jnp.sum(grad_normed_a * unit_a, axis=0)),
        spread(jnp.sum(grad_normed_b * unit_b, axis=0)),
        jnp.transpose(spread(jnp.transpose(grad_taps))),
    )


def solution(mesh):
    n_dp, n_seq = mesh.shape["dp"], mesh.shape["seq"]

    def body(*args):
        tokens, in_weight, gate_weight, down_weight = args[0], args[3], args[5], args[7]
        width = tokens.shape[2]
        unit = 3 * width // max(n_dp, 1)
        fits = (
            n_dp == 4
            and n_seq % 2 == 0
            and tokens.shape[0] == 1
            and in_weight.shape[0] % 16 == 0
            and down_weight.shape[0] % 16 == 0
            and 128 % in_weight.shape[0] == 0
            and unit % 256 == 0
            and 2 * gate_weight.shape[1] == 3 * unit * n_dp
        )
        if fits:
            return fast_body(n_dp, n_seq, *args)
        return plain_body(*args)

    return jax.shard_map(
        body,
        mesh=mesh,
        in_specs=(
            P("dp", "seq", None),
            P("dp", None),
            P("dp", "seq", None),
            P(("dp", "seq"), None),
            P(("dp", "seq"), None),
            P(("dp", "seq"), None),
            P(("dp", "seq"), None),
            P(("dp", "seq"), None),
            P(("dp", "seq")),
            P(("dp", "seq")),
            P(None, ("dp", "seq")),
        ),
        out_specs=(
            P("dp", "seq", None),
            P("dp", "seq", None),
            P(("dp", "seq"), None),
            P(("dp", "seq"), None),
            P(("dp", "seq"), None),
            P(("dp", "seq"), None),
            P(("dp", "seq"), None),
            P(("dp", "seq")),
            P(("dp", "seq")),
            P(None, ("dp", "seq")),
        ),
        check_vma=False,
    )
```

time: 1340 us -> 246 us (0.18)
  waiting for transfers between devices: 996 us -> 0 us
  Pallas kernels: 0 us -> 229 us
  blocking collectives: 92.2 us -> 0 us
  matrix products: 86.7 us -> 0 us
  other arithmetic: 62.1 us -> 2.12 us
  starting transfers between devices: 42.5 us -> 0 us
  local copies, waits for them, and re-layouts: 40.1 us -> 13.8 us
  between operations: 14.9 us -> 0.79 us
    all_to_all x8 -> x0, waiting for transfers between devices: 711 us -> none  [the longest x1 191 us: spread_all(): lax.all_to_all(shaped[2].astype(jnp.bfloat16), 'seq', split_axis=1, conca...]
    all_gather x5 -> x0, waiting for transfers between devices: 263 us -> none  [the longest x1 82 us: body(): lax.all_gather(gate_weight.astype(jnp.bfloat16), ('dp', 'seq'), axis=0, t...]
    pallas_call x0 -> x1, Pallas kernels: none -> 229 us  [fast_body(): pl.pallas_call(functools.partial(block_kernel, dims), out_shape=(jax.Shap...]
    dot_general x15 -> x0, matrix products: 86.7 us -> none  [the longest x5 36 us: matmul(): return jnp.dot(left, right, preferred_element_type=jnp.float32)]
    unnamed x2 -> x0, blocking collectives: 51.6 us -> none
    all_gather x1 -> x0, blocking collectives: 40.6 us -> none  [body(): lax.all_gather(kernel.astype(jnp.bfloat16), ('dp', 'seq'), axis=1, tiled=...]
    all_to_all x8 -> x0, starting transfers between devices: 38.6 us -> none  [the longest x1 5.47 us: spread_all(): lax.all_to_all(shaped[3].astype(jnp.bfloat16), 'seq', split_axis=1, conca...]
    convert_element_type x13 -> x0, local copies, waits for them, and re-layouts: 34.8 us -> none  [the longest x1 9.13 us: spread_all(): shaped[4].astype(jnp.bfloat16)]
  transfers between devices with their start and end apart: 20 -> 0, of which waited for: 13 -> 0; matrix products, arithmetic and copies ran while one was open for 12% -> 0% of each run, Pallas kernels for 0% -> 0%
where the time goes in v1:
time: 246 us
  Pallas kernels  229 us (93%)
  local copies, waits for them, and re-layouts  13.8 us (6%)
    pallas_call x1, Pallas kernels, fast_body(): pl.pallas_call(functools.partial(block_kernel, dims), out_shape=(jax.Shap...  229 us

profile of v1, /device:TPU:0, one launch (start us, length us, event | category | flops | bytes accessed | tf_op | source)
XLA Modules:
  0.0 246.1 jit_solution(9979563528047226910)
XLA Ops:
  0.7 0.7 convert.15
  1.3 0.7 convert_bitcast_fusion
  2.0 0.3 dynamic_update_slice.3.gain_ref
  2.4 0.6 copy-done.5
  2.9 0.8 concatenate.7
  3.8 0.1 slice_compare_fusion.3
  3.9 0.2 copy.35
  4.1 0.7 pad_convert_fusion.mask_ref
  4.8 229.4 %shard_map.186 = (bf16[256,1024]{1,0:T(8,128)(2,1)}, bf16[256,1024]{1,0:T(8,128)(2,1)}, bf16[4,32,3072]{2,1,0:T(8,128)(2,1)}, f32[32,1024]{1,0:T(8,128)}, f32[144,1024]{1,0:T(8,128)}, /*index=5*/f32[16,128]{1,0:T(8,128)}) custom-call(bf16[256,1024]{1,0:T(8,128)(2,1)} %bitcast.21, bf16[256,1024]{1,0:T(8,128)(2,1)} %bitcast.22, ...), custom_call_target="tpu_custom_call" | custom-call | tf_op jit(solution)/shard_map/pallas_call | solution.py:764
  234.2 1.3 dynamic-slice_bitcast_fusion
  235.6 1.3 dynamic-slice.2
  236.9 1.0 slice.50
  237.9 0.2 reshape.34
  238.1 0.3 copy.36
  238.4 0.9 reshape.35
  239.4 0.6 reshape.36
  240.1 0.4 copy.39
  240.5 0.3 fusion
  240.8 1.1 squeeze.25
  241.9 1.1 squeeze.24
  243.1 0.8 copy.45
  243.9 0.8 copy.46
  244.7 0.7 copy.47
  245.3 0.8 copy.48
  (21 shorter events, 0.2 us)
Async XLA Ops:
  2.4 0.6 copy-start.5
  236.9 2.5 %copy-start = (bf16[4,32,3072]{2,1,0:T(8,128)(2,1)S(1)}, bf16[4,32,3072]{2,1,0:T(8,128)(2,1)}, u32[]{:S(2)}) copy-start(bf16[4,32,3072]{2,1,0:T(8,128)(2,1)} %get-tuple-element.18) | copy-start | bytes 2359300
  240.8 2.3 copy-start.3
  240.8 3.1 %copy-start.2 = (bf16[256,1024]{1,0:T(8,128)(2,1)S(1)}, bf16[256,1024]{1,0:T(8,128)(2,1)}, u32[]{:S(2)}) copy-start(bf16[256,1024]{1,0:T(8,128)(2,1)} %get-tuple-element.17) | copy-start | bytes 1572868
  241.9 2.7 %copy-start.4 = (f32[32,1024]{1,0:T(8,128)S(1)}, f32[32,1024]{1,0:T(8,128)}, u32[]{:S(2)}) copy-start(f32[32,1024]{1,0:T(8,128)} %get-tuple-element.45) | copy-start | bytes 393220
  241.9 3.4 %copy-start.1 = (f32[144,1024]{1,0:T(8,128)S(1)}, f32[144,1024]{1,0:T(8,128)}, u32[]{:S(2)}) copy-start(f32[144,1024]{1,0:T(8,128)} %get-tuple-element.48) | copy-start | bytes 1769476

commit v2 on v1

--- a/solution.py
+++ b/solution.py
@@ -33,7 +33,6 @@
 
 
 GAIN, IN, OUT, GU0, DOWN, GU1, GU2 = range(7)
-UNITS = (GAIN, IN, OUT, GU0, DOWN, GU1, GU2)
 SLOT = {IN: 0, GU0: 1, GU1: 2, GU2: 3}
 AX, AZ, AO, AR = range(4)
 
@@ -41,12 +40,12 @@
 def block_kernel(
     dims,
     x_ref, do_ref, mask_ref, gain_ref, win_ref, wout_ref, wg_ref, wu_ref, wdn_ref,
-    out_ref, gtok_ref, rbuf, gout_ref, gdown_ref, gsmall_ref,
+    out_ref, gtok_ref, gin_ref, gout_ref, ggate_ref, gup_ref, gdown_ref, gsmall_ref, gains_ref,
     stage, wall, wo, wd, gb, gv, xa, ma, za, oa, ra, big, mbuf, pbuf, ybuf, halo_p, halo_q,
-    sb_a, rx_a, ry_a, fx_a, fy_a, rx_b, ry_b, fx_b, fy_b, hid, own, dh,
+    sb_a, sb_b, rx_a, ry_a, fx_a, fy_a, rx_b, ry_b, fx_b, fy_b, hid, dh,
     gw, gd, go, dd_g, dd_d, dd_o, up_g, up_d, up_o, dn_g, dn_d, dn_o,
-    gvec, sg, sgx, s2, dd_s, up_s, dn_s,
-    zs, zr, ws, wr, gs, gr, ms, mr, hs, hr, ags, agr, rss, rsr, ds_, dr_, us, ur, vs, vr, qs, qr, ss, sr, ins,
+    rbuf, gsum, s2, dd_s, up_s, dn_s,
+    zs, zr, ws, wr, gs, gr, ms, mr, hs, hr, ags, agr, rss, rsr, ds_, dr_, us, ur, vs, vr, qs, qr, ins,
 ):
     tok, wid, nz, rows, ch, fs, cj, uw, drows = dims
     half = tok // 2
@@ -261,48 +260,24 @@
         else:
             dst[...] = sum(p[...].astype(F32) for p in parts).astype(dst.dtype)
 
-    def g_up(unit, cond):
-        for zt in range(top, 0, -1):
-            pred = jnp.logical_and(cond, z < zt)
-            mine, pair, came = (lambda: g_own(unit, zt, c)), (lambda: g_in(unit, t_dd, zt)), (lambda: g_in(unit, t_up, zt - 1))
-
-            def first():
-                g_add(unit, mine(), (mine(), pair()))
-
-            def later():
-                g_add(unit, mine(), (mine(), pair(), came()))
-
-            recv(jnp.logical_and(pred, z > 0), came, lambda: ur.at[unit * top + zt - 1])
-            pl.when(jnp.logical_and(pred, z == 0))(first)
-            pl.when(jnp.logical_and(pred, z > 0))(later)
-            send("g", pred, lambda zt=zt: g_own(unit, zt, c), lambda zt=zt: g_in(unit, t_up, zt - 1),
-                 lambda zt=zt: us.at[(unit * top + zt - 1) * 2 + (0 if cond is low_z else 1)],
-                 lambda zt=zt: ur.at[unit * top + zt - 1], to_up)
-
-    def g_down(unit):
-        for zt in range(top):
-            pred = z > zt
-            mine, pair, came = (lambda: g_own(unit, zt, c)), (lambda: g_in(unit, t_dd, zt)), (lambda: g_in(unit, t_dn, zt))
-
-            def first():
-                g_add(unit, mine(), (mine(), pair()))
-
-            def later():
-                g_add(unit, mine(), (mine(), pair(), came()))
-
-            recv(jnp.logical_and(pred, z < top), came, lambda: vr.at[unit * top + zt])
-            pl.when(jnp.logical_and(pred, z == top))(first)
-            pl.when(jnp.logical_and(pred, z < top))(later)
-            send("g", pred, lambda zt=zt: g_own(unit, zt, c), lambda zt=zt: g_in(unit, t_dn, zt),
-                 lambda zt=zt: vs.at[unit * top + zt], lambda zt=zt: vr.at[unit * top + zt], to_dn)
-
-    low_z = z < nz // 2
-    high_z = z >= nz // 2
-
-    def g_line(unit):
-        g_up(unit, low_z)
-        g_down(unit)
-        g_up(unit, high_z)
+    def g_step(unit, pred, zt, come, came, csem, ssem, rsem, there, tgt):
+        mine, pair = (lambda: g_own(unit, zt, c)), (lambda: g_in(unit, t_dd, zt))
+        if come:
+            recv(pred, came, csem)
+            pl.when(pred)(lambda: g_add(unit, mine(), (mine(), pair(), came())))
+        else:
+            pl.when(pred)(lambda: g_add(unit, mine(), (mine(), pair())))
+        send("g", pred, mine, there, ssem, rsem, tgt)
+
+    def g_hop(unit, h):
+        for zt in range(top, h, -1):
+            came = lambda zt=zt: g_in(unit, t_up, zt - 1)
+            sem = lambda zt=zt: ur.at[unit * top + zt - 1]
+            g_step(unit, z == h, zt, h > 0, came, sem, lambda zt=zt: us.at[unit * top + zt - 1], sem, came, to_up)
+        for zt in range(top - h):
+            came = lambda zt=zt: g_in(unit, t_dn, zt)
+            sem = lambda zt=zt: vr.at[unit * top + zt]
+            g_step(unit, z == top - h, zt, h > 0, came, sem, lambda zt=zt: vs.at[unit * top + zt], sem, came, to_dn)
 
     def g_last(unit, acc):
         up_ref = lambda: g_in(unit, t_up, z - 1)
@@ -313,17 +288,20 @@
         pl.when(has_dn)(lambda: g_add(unit, acc, (acc, up_ref())))
         pl.when(has_up)(lambda: g_add(unit, acc, (acc, dn_ref())))
 
+    def row_send(unit, idx):
+        return big.at[idx, pl.ds(SLOT[unit] * rows, rows), pl.ds(2 * fs, uw)]
+
     def g_rows(unit):
         facc = mbuf.at[:, pl.ds(0, rows), :]
         g_last(unit, facc)
         u = SLOT[unit]
         for k in range(4):
-            stage[k, :, cols(unit)] = facc[k].astype(BF)
+            big[k, pl.ds(u * rows, rows), pl.ds(2 * fs, uw)] = facc[k].astype(BF)
         rbuf[d, :, cols(unit)] = facc[d].astype(BF)
         for k, (idx, tgt) in enumerate(peers):
             send(
-                "stage", True,
-                lambda idx=idx: stage.at[idx, :, cols(unit)],
+                "rows", True,
+                lambda idx=idx: row_send(unit, idx),
                 lambda: rbuf.at[d, :, cols(unit)],
                 lambda k=k: qs.at[u * 3 + k], lambda k=k: qr.at[u * 3 + k], tgt,
             )
@@ -332,6 +310,14 @@
         u = SLOT[unit]
         for k, (idx, _) in enumerate(peers):
             recv(True, lambda idx=idx: rbuf.at[idx, :, cols(unit)], lambda k=k: qr.at[u * 3 + k])
+        for k in range(4):
+            if unit == IN:
+                for p in range(3):
+                    gin_ref[:, pl.ds(p * wid + k * ch, ch)] = rbuf[k, :, pl.ds(p * ch, ch)].astype(F32)
+            else:
+                j = u - 1
+                ggate_ref[:, pl.ds(k * fs + j * cj, cj)] = rbuf[k, :, pl.ds(u * uw, cj)].astype(F32)
+                gup_ref[:, pl.ds(k * fs + j * cj, cj)] = rbuf[k, :, pl.ds(u * uw + cj, cj)].astype(F32)
 
     count = 4 * fs // uw
 
@@ -345,20 +331,42 @@
         b = i * count + first // uw
         return mbuf[b // 8, pl.ds((b % 8) * rows, rows), pl.ds(first % uw, n)]
 
+    x_in = pltpu.make_async_copy(x_ref.at[0], xa.at[d], ins.at[2 * count])
+    do_in = pltpu.make_async_copy(do_ref.at[0], oa.at[d], ins.at[2 * count + 1])
+    def down_in(i):
+        n = (uw, wid - uw)[i]
+        return pltpu.make_async_copy(
+            wdn_ref.at[:, pl.ds(i * uw, n)], mbuf.at[2, pl.ds(i * drows, drows), pl.ds(0, n)] if i == 0
+            else mbuf.at[3, pl.ds(0, drows), pl.ds(0, n)], ins.at[2 * count + 2 + i]
+        )
+
+    def first_in(i):
+        return pltpu.make_async_copy(
+            win_ref.at[:, pl.ds(i * uw, uw)], mbuf.at[2 + i // 2, pl.ds(tok - rows * (1 + i % 2), rows), :], ins.at[2 * count + 4 + i]
+        )
+
+    for i in range(4):
+        first_in(i).start()
+    x_in.start()
     for i in range(2 * count):
         wide_in(i).start()
+    for i in range(2):
+        down_in(i).start()
+    do_in.start()
+    for i in range(4):
+        first_in(i).wait()
     for k in range(4):
         for p in range(3):
-            stage[k, :, pl.ds(p * ch, ch)] = win_ref[:, pl.ds(p * wid + k * ch, ch)].astype(BF)
+            b, first = divmod(p * wid + k * ch, uw)
+            stage[k, :, pl.ds(p * ch, ch)] = mbuf[2 + b // 2, pl.ds(tok - rows * (1 + b % 2), rows), pl.ds(first, ch)].astype(BF)
     w_slice(IN)
     gb[d, z, c] = gain_ref[...]
     z_own(GAIN)
-    xa[d] = x_ref[...]
+    x_in.wait()
     ag_start(AX, xa)
+    wo[pl.ds(pl.multiple_of(s * rows, rows), rows), :] = wout_ref[...].astype(BF)
+    z_own(OUT)
     ma[d] = mask_ref[...]
-    for k, (idx, tgt) in enumerate(peers):
-        send("ag", True, lambda: ma.at[d], lambda: ma.at[d], lambda k=k: ms.at[k], lambda k=k: mr.at[k], tgt)
-    wo[pl.ds(pl.multiple_of(s * rows, rows), rows), :] = wout_ref[...].astype(BF)
     for i in range(2 * count):
         wide_in(i).wait()
     for k in range(4):
@@ -367,25 +375,28 @@
             stage[k, :, pl.ds((1 + j) * uw + cj, cj)] = wide_read(1, k * fs + j * cj, cj).astype(BF)
     w_slice_wait(IN)
     z_own(IN)
-    z_own(OUT)
-    for unit in (GU0, GU1, GU2):
-        w_slice(unit)
-    wd[pl.ds(pl.multiple_of(s * drows, drows), drows), :] = wdn_ref[...].astype(BF)
+    for i in range(2):
+        down_in(i).wait()
+    wd[pl.ds(pl.multiple_of(s * drows, drows), drows), pl.ds(0, uw)] = mbuf[2, pl.ds(0, drows), :].astype(BF)
+    wd[pl.ds(pl.multiple_of(s * drows, drows), drows), pl.ds(uw, wid - uw)] = mbuf[3, pl.ds(0, drows), pl.ds(0, wid - uw)].astype(BF)
     z_fwd(GAIN, 1)
+    z_fwd(OUT, 1)
+    ag_fwd(AX, xa)
+    for k, (idx, tgt) in enumerate(peers):
+        send("ag", True, lambda: ma.at[d], lambda: ma.at[d], lambda k=k: ms.at[k], lambda k=k: mr.at[k], tgt)
+    w_slice(GU0)
+    z_fwd(GAIN, 2)
     z_fwd(IN, 1)
-    ag_fwd(AX, xa)
-    z_fwd(GAIN, 2)
-    z_fwd(IN, 2)
-    z_fwd(OUT, 1)
-    w_slice_wait(GU0)
-    z_own(GU0)
+    z_fwd(OUT, 2)
     z_fwd(GAIN, 3)
     z_finish(GAIN)
     for k, (idx, tgt) in enumerate(peers):
         send("w", True, lambda: gb.at[d], lambda: gb.at[d], lambda k=k: gs.at[k], lambda k=k: gr.at[k], tgt)
-    z_fwd(IN, 3)
-    z_fwd(OUT, 2)
+    w_slice(GU1)
+    w_slice(GU2)
     ag_near(AX, xa)
+    z_fwd(IN, 2)
+    z_fwd(OUT, 3)
     for k, (idx, _) in enumerate(peers):
         recv(True, lambda idx=idx: gb.at[idx], lambda k=k: gr.at[k])
     per = 128 // rows
@@ -396,7 +407,6 @@
             piece = gb[dd, q // 2, q % 2].astype(F32)
             tot = piece if tot is None else tot + piece
         gv[:, pl.ds(g * 128, 128)] = tot
-    ag_far(AX, xa)
 
     step = 32
 
@@ -404,19 +414,24 @@
         return lax.rsqrt(jnp.mean(xv * xv, axis=1, keepdims=True) + epsilon)
 
     zcol = pl.ds(0, wid)
-
-    def make_z1():
-        @pl.loop(0, 4 * tok // step)
+    zstep = 64
+
+    def make_z1(dd):
+        @pl.loop(0, tok // zstep)
         def _(i):
-            dd = lax.div(i, tok // step)
-            rr = pl.ds(pl.multiple_of(lax.rem(i, tok // step) * step, step), step)
+            rr = pl.ds(pl.multiple_of(i * zstep, zstep), zstep)
             xv = xa[dd, rr, :].astype(F32)
             big[dd, rr, zcol] = (xv * norm_rows(xv) * gv[0:1, :]).astype(BF)
 
-    make_z1()
+    make_z1(d)
+    make_z1(xn)
+    make_z1(yn)
+    z_fwd(IN, 3)
+    w_slice_wait(GU0)
+    z_own(GU0)
+    ag_far(AX, xa)
+    make_z1(dg)
     z_finish(IN)
-    z_own(DOWN)
-    z_fwd(GU0, 1)
     for k, (idx, _) in enumerate(peers):
         recv(True, lambda idx=idx: ma.at[idx], lambda k=k: mr.at[k])
 
@@ -437,8 +452,10 @@
     def _():
         halo_p[...] = jnp.zeros_like(halo_p)
 
-    z_fwd(OUT, 3)
     z_finish(OUT)
+    z_fwd(GU0, 1)
+    w_slice_wait(GU1)
+    z_own(GU1)
     recv(s > 0, lambda: halo_p, lambda: hr.at[0])
     tap_cols = pl.ds(pl.multiple_of(d * ch, ch), ch)
     row = lax.broadcasted_iota(jnp.int32, (tok, ch), 0)
@@ -454,67 +471,66 @@
     def convolve(cur, one, two):
         return gv[2:3, tap_cols] * cur + gv[3:4, tap_cols] * one + gv[4:5, tap_cols] * two
 
-    @pl.loop(0, 4)
-    def _(dd):
+    def conv_rows(dd):
         cur, one, two, _ = past(dd)
         ybuf[dd] = (mbuf[dd, :, pl.ds(ch, ch)] * convolve(cur, one, two)).astype(BF)
 
     def h_tile(dd):
+        conv_rows(dd)
         return dot_nn(ybuf[dd], wo[...])
 
     rs_run(0, sb_a, bufs_a, h_tile, "rs0")
-    own[...] = h_tile(d)
-    w_slice_wait(GU1)
-    z_own(GU1)
+    hid[...] = h_tile(d)
     z_fwd(GU0, 2)
-    rs_pass(0, sb_a, bufs_a, "rs0")
-    z_fwd(DOWN, 1)
-    z_fwd(GU0, 3)
     w_slice_wait(GU2)
     z_own(GU2)
     z_fwd(GU1, 1)
-    z_fwd(DOWN, 2)
+    rs_pass(0, sb_a, bufs_a, "rs0")
+    z_fwd(GU0, 3)
+    z_own(DOWN)
+    z_fwd(GU1, 2)
+    z_fwd(GU2, 1)
     rs_wait(0, bufs_a)
 
     @pl.loop(0, tok // step)
     def _(i):
         rr = pl.ds(pl.multiple_of(i * step, step), step)
-        h = xa[d, rr, :].astype(F32) + own[rr, :] + rx_a[rr, :].astype(F32) + ry_a[rr, :].astype(F32)
+        h = xa[d, rr, :].astype(F32) + hid[rr, :] + rx_a[rr, :].astype(F32) + ry_a[rr, :].astype(F32)
         hid[rr, :] = h
         za[d, rr, :] = (h * norm_rows(h) * gv[1:2, :]).astype(BF)
 
     ag_start(AZ, za)
-    oa[d] = do_ref[...]
-    ag_start(AO, oa)
-    z_fwd(GU1, 2)
-    z_fwd(DOWN, 3)
-    z_fwd(GU2, 1)
-    ag_fwd(AZ, za)
-    z_fwd(GU1, 3)
-    z_fwd(GU2, 2)
-    z_finish(GU0)
-    ag_near(AZ, za)
-    ag_far(AZ, za)
-    ag_fwd(AO, oa)
-    z_finish(DOWN)
-    ag_near(AO, oa)
-    ag_far(AO, oa)
-
-    def gated(j):
-        acol = pl.ds(j * cj, cj)
-        gcol = pl.ds(fs + j * uw, cj)
-        ucol = pl.ds(fs + j * uw + cj, cj)
-
+    do_in.wait()
+
+    def acol(j):
+        return pl.ds(j * cj, cj)
+
+    def gcol(j):
+        return pl.ds(fs + j * uw, cj)
+
+    def ucol(j):
+        return pl.ds(fs + j * uw + cj, cj)
+
+    def gate_one(j, dd):
+        gu = dot_nn(za[dd], unit_w((1 + j) * uw, uw))
+        g, u = gu[:, :cj], gu[:, cj:]
+        sig = jax.nn.sigmoid(g)
+        sw = g * sig
+        big[dd, :, acol(j)] = (sw * u).astype(BF)
+        big[dd, :, gcol(j)] = (u * sig * (1.0 + g * (1.0 - sig))).astype(BF)
+        big[dd, :, ucol(j)] = sw.astype(BF)
+
+    def gate_all(j):
         @pl.loop(0, 4)
         def _(dd):
-            gu = dot_nn(za[dd], unit_w((1 + j) * uw, uw))
+            gate_one(j, dd)
+
+    def back_all(j):
+        @pl.loop(0, 4)
+        def _(dd):
             da = dot_nt(oa[dd], wd[pl.ds(j * cj, cj), :])
-            g, u = gu[:, :cj], gu[:, cj:]
-            sig = jax.nn.sigmoid(g)
-            sw = g * sig
-            big[dd, :, acol] = (sw * u).astype(BF)
-            big[dd, :, gcol] = (da * u * sig * (1.0 + g * (1.0 - sig))).astype(BF)
-            big[dd, :, ucol] = (da * sw).astype(BF)
+            big[dd, :, gcol(j)] = (da * big[dd, :, gcol(j)].astype(F32)).astype(BF)
+            big[dd, :, ucol(j)] = (da * big[dd, :, ucol(j)].astype(F32)).astype(BF)
 
     def grad_gu(j):
         @pl.loop(0, 4)
@@ -524,42 +540,69 @@
             res = dot_tn(left, right).astype(BF)
             gw[dd, :, :, :, pl.ds((1 + j) * uw, uw)] = res.reshape(nz, 2, rows, uw)
 
-    gated(0)
-    grad_gu(0)
-    g_pair(GU0)
-    z_fwd(GU2, 3)
-    z_finish(GU1)
-    gated(1)
-    z_finish(GU2)
-    gated(2)
-
-    drain("rs0")
-
-    def dz2_tile(dd):
-        return dot_nt(big[dd, :, pl.ds(fs, 3 * uw)], unit_w(uw, 3 * uw))
-
-    rs_run(1, sb_a, bufs_a, dz2_tile, "rs1")
-    own[...] = dz2_tile(d)
-    rs_pass(1, sb_a, bufs_a, "rs1")
-    g_pair_wait(GU0)
-    g_line(GU0)
-    grad_gu(1)
-    g_pair(GU1)
-
     def grad_down(j):
         left = big[:, :, pl.ds(j * cj, cj)].reshape(4 * tok, cj)
         gd[pl.ds(j * cj, cj), :] = dot_tn(left, oa[...].reshape(4 * tok, wid)).astype(BF)
 
+    def dz2_tile(dd):
+        return dot_nt(big[dd, :, pl.ds(fs, 3 * uw)], unit_w(uw, 3 * uw))
+
+    def out_tile(dd):
+        return dot_nn(big[dd, :, pl.ds(0, fs)], wd[...])
+
+    z_finish(GU0)
+    gate_one(0, d)
+    z_fwd(GU1, 3)
+    z_fwd(GU2, 2)
+    ag_fwd(AZ, za)
+    ag_start(AO, oa)
+    z_finish(GU1)
+    gate_one(1, d)
+    z_fwd(DOWN, 1)
+    ag_near(AZ, za)
+    z_fwd(GU2, 3)
+    z_finish(GU2)
+    gate_one(2, d)
+    for j in range(3):
+        gate_one(j, xn)
+    ag_fwd(AO, oa)
+    z_fwd(DOWN, 2)
+    for j in range(3):
+        gate_one(j, yn)
+    ag_far(AZ, za)
+    for j in range(3):
+        gate_one(j, dg)
+    z_fwd(DOWN, 3)
+    z_finish(DOWN)
+    rs_run(2, sb_b, bufs_b, out_tile, "rs2")
+    ag_near(AO, oa)
+    ag_far(AO, oa)
+    for j in range(3):
+        grad_down(j)
+    g_pair(DOWN)
+    for j in range(3):
+        back_all(j)
+    g_pair_wait(DOWN)
+    g_hop(DOWN, 0)
+
+    drain("rs0")
+    rs_run(1, sb_a, bufs_a, dz2_tile, "rs1")
+    rs_pass(2, sb_b, bufs_b, "rs2")
+    dh[...] = dz2_tile(d)
+    grad_gu(0)
+    g_pair(GU0)
+    rs_pass(1, sb_a, bufs_a, "rs1")
+    g_hop(DOWN, 1)
+    g_pair_wait(GU0)
+    g_hop(GU0, 0)
+    grad_gu(1)
+    g_pair(GU1)
     rs_wait(1, bufs_a)
-    gvec[...] = jnp.zeros_like(gvec)
-    zero_row = jnp.zeros((8, wid), F32)
-
-    def fold(v):
-        return v.reshape(step // 8, 8, wid).sum(axis=0)
-
-    def back_two(i, acc):
+
+    @pl.loop(0, tok // step)
+    def _(i):
         rr = pl.ds(pl.multiple_of(i * step, step), step)
-        dz = own[rr, :] + rx_a[rr, :].astype(F32) + ry_a[rr, :].astype(F32)
+        dz = dh[rr, :] + rx_a[rr, :].astype(F32) + ry_a[rr, :].astype(F32)
         h = hid[rr, :]
         inv = norm_rows(h)
         unit = h * inv
@@ -567,41 +610,45 @@
         g = oa[d, rr, :].astype(F32) + inv * (e - unit * jnp.mean(e * unit, axis=1, keepdims=True))
         dh[rr, :] = g
         ra[d, rr, :] = g.astype(BF)
-        return acc + fold(dz * unit)
-
-    gain2 = lax.fori_loop(0, tok // step, back_two, zero_row)
-    gvec[1:2, :] = jnp.sum(gain2, axis=0, keepdims=True)
+
     ag_start(AR, ra)
+    g_hop(DOWN, 2)
+    g_hop(GU0, 1)
     g_pair_wait(GU1)
-    g_line(GU1)
+    g_hop(GU1, 0)
     grad_gu(2)
     g_pair(GU2)
     ag_fwd(AR, ra)
-    for j in range(3):
-        grad_down(j)
-    g_pair(DOWN)
+    hid[...] = hid[...] + out_tile(d)
+    rs_wait(2, bufs_b)
+
+    @pl.loop(0, tok // step)
+    def _(i):
+        rr = pl.ds(pl.multiple_of(i * step, step), step)
+        sb_b[d, rr, :] = (hid[rr, :] + rx_b[rr, :].astype(F32) + ry_b[rr, :].astype(F32)).astype(BF)
+
+    result = pltpu.make_async_copy(sb_b.at[d], out_ref.at[0], ins.at[2 * count])
+    result.start()
+    for dd in (d, xn, yn, dg):
+        make_z1(dd)
+    g_hop(GU0, 2)
     g_pair_wait(GU2)
-    g_line(GU2)
-
-    def out_tile(dd):
-        return dot_nn(big[dd, :, pl.ds(0, fs)], wd[...])
-
+    g_hop(GU2, 0)
     ag_near(AR, ra)
     ag_far(AR, ra)
 
     mcol = fs
-
-    @pl.loop(0, 4)
-    def _(dd):
+    zero_tap = jnp.zeros((8, ch), F32)
+
+    def back_conv(dd, acc):
         dy = dot_nt(ra[dd], wo[...])
         cur, one, two, _ = past(dd)
         q = dy * mbuf[dd, :, pl.ds(ch, ch)]
         mbuf[dd, :, pl.ds(ch, ch)] = q
         big[dd, :, pl.ds(mcol + ch, ch)] = (dy * convolve(cur, one, two)).astype(BF)
-        gvec[2:3, tap_cols] = gvec[2:3, tap_cols] + jnp.sum(q * cur, axis=0, keepdims=True)
-        gvec[3:4, tap_cols] = gvec[3:4, tap_cols] + jnp.sum(q * one, axis=0, keepdims=True)
-        gvec[4:5, tap_cols] = gvec[4:5, tap_cols] + jnp.sum(q * two, axis=0, keepdims=True)
-
+        return tuple(a + (q * v).reshape(tok // 8, 8, ch).sum(axis=0) for a, v in zip(acc, (cur, one, two)))
+
+    taps = lax.fori_loop(0, 4, back_conv, (zero_tap, zero_tap, zero_tap))
     head = 8
     send("halo", s > 0, lambda: mbuf.at[:, pl.ds(0, head), pl.ds(ch, ch)], lambda: halo_q, lambda: hs.at[1], lambda: hr.at[1], to_prev)
 
@@ -609,15 +656,16 @@
     def _():
         halo_q[...] = jnp.zeros_like(halo_q)
 
-    rs_run(2, big, bufs_b, out_tile, "rs2", 2 * fs)
-    own[...] = out_tile(d)
-    rs_pass(2, big, bufs_b, "rs2", 2 * fs)
-    make_z1()
-    go[...] = dot_tn(ybuf[...].reshape(4 * tok, ch), ra[...].reshape(4 * tok, wid)).astype(BF)
-    g_pair(OUT)
-    g_pair_wait(DOWN)
-    g_line(DOWN)
+    lines = lax.broadcasted_iota(jnp.int32, (16, ch), 0)
+    tap_rows = jnp.zeros((16, ch), F32)
+    for k in range(3):
+        tap_rows = jnp.where(lines == k, jnp.sum(taps[k], axis=0, keepdims=True), tap_rows)
+    for q in range(2 * nz):
+        first = (q * rows) // 128 * 128
+        s2[q // 2, q % 2] = tap_rows[:, first : first + 128].astype(BF)
+    g_hop(GU1, 1)
     recv(s < 2 * nz - 1, lambda: halo_q, lambda: hr.at[1])
+
     @pl.loop(0, 4)
     def _(dd):
         q = mbuf[dd, :, pl.ds(ch, ch)]
@@ -629,20 +677,12 @@
         big[dd, :, pl.ds(mcol, ch)] = (dp * mbuf[dd, :, pl.ds(2 * ch, ch)]).astype(BF)
         big[dd, :, pl.ds(mcol + 2 * ch, ch)] = (dp * mbuf[dd, :, pl.ds(0, ch)]).astype(BF)
 
-    rs_wait(2, bufs_b)
-
-    @pl.loop(0, tok // step)
-    def _(i):
-        rr = pl.ds(pl.multiple_of(i * step, step), step)
-        out_ref[rr, :] = (hid[rr, :] + own[rr, :] + rx_b[rr, :].astype(F32) + ry_b[rr, :].astype(F32)).astype(BF)
-
     drain("rs1")
 
     def dz1_tile(dd):
         return dot_nt(big[dd, :, pl.ds(mcol, uw)], unit_w(0, uw))
 
     rs_run(3, sb_a, bufs_a, dz1_tile, "rs3")
-    own[...] = dz1_tile(d)
 
     @pl.loop(0, 4)
     def _(dd):
@@ -651,56 +691,70 @@
         gw[dd, :, :, :, pl.ds(0, uw)] = dot_tn(left, right).astype(BF).reshape(nz, 2, rows, uw)
 
     g_pair(IN)
+    g_hop(GU2, 1)
+    g_hop(GU1, 2)
+    go[...] = dot_tn(ybuf[...].reshape(4 * tok, ch), ra[...].reshape(4 * tok, wid)).astype(BF)
+    g_pair(OUT)
+    g_pair(GAIN)
     rs_pass(3, sb_a, bufs_a, "rs3")
+    g_pair_wait(IN)
+    g_hop(IN, 0)
     g_pair_wait(OUT)
-    g_line(OUT)
-    g_pair_wait(IN)
-    g_line(IN)
+    g_hop(OUT, 0)
+    g_pair_wait(GAIN)
+    g_hop(GAIN, 0)
+    hid[...] = dz1_tile(d)
     drain("halo")
-    drain("stage")
+    drain("rs2")
+    g_hop(GU2, 2)
     g_rows(GU0)
+    g_hop(IN, 1)
+    g_hop(OUT, 1)
+    g_hop(GAIN, 1)
+    g_last(DOWN, gdown_ref)
     g_rows(GU1)
+    rs_wait(3, bufs_a)
+    g_hop(IN, 2)
+    g_hop(OUT, 2)
+    g_hop(GAIN, 2)
     g_rows(GU2)
-    rs_wait(3, bufs_a)
-
-    def back_one(i, acc):
+    g_rows_wait(GU0)
+
+    @pl.loop(0, tok // step)
+    def _(i):
         rr = pl.ds(pl.multiple_of(i * step, step), step)
-        dz = own[rr, :] + rx_a[rr, :].astype(F32) + ry_a[rr, :].astype(F32)
+        dz = hid[rr, :] + rx_a[rr, :].astype(F32) + ry_a[rr, :].astype(F32)
         xv = xa[d, rr, :].astype(F32)
         inv = norm_rows(xv)
         unit = xv * inv
         e = dz * gv[0:1, :]
         g = dh[rr, :] + inv * (e - unit * jnp.mean(e * unit, axis=1, keepdims=True))
-        gtok_ref[rr, :] = g.astype(BF)
-        return acc + fold(dz * unit)
-
-    gain1 = lax.fori_loop(0, tok // step, back_one, zero_row)
-    gvec[0:1, :] = jnp.sum(gain1, axis=0, keepdims=True)
-    for g in range(wid // 128):
-        val = gvec[:, pl.ds(g * 128, 128)].astype(BF)
-        for i in range(g * per, (g + 1) * per):
-            dd, q = i // (2 * nz), i % (2 * nz)
-            sg[dd, q // 2, q % 2] = val
-    for k, (idx, tgt) in enumerate(peers):
-        send("g", True, lambda idx=idx: sg.at[idx], lambda k=k: sgx.at[k], lambda k=k: ss.at[k], lambda k=k: sr.at[k], tgt)
+        sb_a[d, rr, :] = g.astype(BF)
+
+    grads = pltpu.make_async_copy(sb_a.at[d], gtok_ref.at[0], ins.at[2 * count + 1])
+    grads.start()
+
+    g_rows_wait(GU1)
     g_rows(IN)
-    for unit in (GU0, GU1, GU2):
-        g_rows_wait(unit)
-    g_last(DOWN, gdown_ref)
     g_last(OUT, gout_ref)
-    for k in range(3):
-        recv(True, lambda k=k: sgx.at[k], lambda k=k: sr.at[k])
-    for zz in range(nz):
-        for cc in range(2):
-            tot = sg[d, zz, cc].astype(F32)
-            for k in range(3):
-                tot = tot + sgx[k, zz, cc].astype(F32)
-            s2[zz, cc] = tot.astype(BF)
-    g_pair(GAIN)
+    g_last(GAIN, gsum)
+    g_rows_wait(GU2)
+    lane0 = lax.rem(s * rows, 128)
+    gsmall_ref[...] = pltpu.roll(gsum[...], lax.rem(128 - lane0, 128), 1)
     g_rows_wait(IN)
-    g_pair_wait(GAIN)
-    g_line(GAIN)
-    g_last(GAIN, gsmall_ref)
+
+    def gain_sum(first, n):
+        acc = jnp.zeros((rows, 128), F32)
+        for k in range(4):
+            for q in range(n // 128):
+                cc = pl.ds(first + q * 128, 128)
+                acc = acc + stage[k, :, cc].astype(F32) * rbuf[k, :, cc].astype(F32)
+        return acc
+
+    gains_ref[0] = gain_sum(0, uw)
+    gains_ref[1] = gain_sum(uw, 3 * uw)
+    result.wait()
+    grads.wait()
     drain()
 
 
@@ -743,41 +797,37 @@
         plane(uw, F32), plane(ch), plane(ch),
         vm((n_dp, 16, ch), BF),
         vm((n_dp, 8, ch), F32),
-        plane(wid),
+        plane(wid), plane(wid),
         *rs_set, *rs_set,
-        vm((tok, wid), F32), vm((tok, wid), F32), vm((tok, wid), F32),
+        vm((tok, wid), F32), vm((tok, wid), F32),
         vm((n_dp, nz, 2, rows, 4 * uw), BF), vm((fs, wid), BF), vm((ch, wid), BF),
         vm((nz, n_dp, rows, 4 * uw), BF), vm((nz, drows, wid), BF), vm((nz, rows, wid), BF),
         vm((top, n_dp, rows, 4 * uw), BF), vm((top, drows, wid), BF), vm((top, rows, wid), BF),
         vm((top, n_dp, rows, 4 * uw), BF), vm((top, drows, wid), BF), vm((top, rows, wid), BF),
-        vm((16, wid), F32),
-        vm((n_dp, nz, 2, 16, 128), BF),
-        vm((3, nz, 2, 16, 128), BF),
+        vm((n_dp, rows, 4 * uw), BF), vm((16, 128), F32),
         vm((nz, 2, 16, 128), BF),
         vm((nz, 16, 128), BF), vm((top, 16, 128), BF), vm((top, 16, 128), BF),
         dma(7 * 13), dma(7 * 2 * nz), dma(12), dma(12), dma(3), dma(3), dma(3), dma(3), dma(2), dma(2),
         dma(24), dma(24), dma(24), dma(24), dma(7 * nz), dma(7 * nz),
-        dma(7 * top * 2), dma(7 * top), dma(7 * top), dma(7 * top), dma(12), dma(12), dma(3), dma(3), dma(8 * fs // uw),
+        dma(7 * top), dma(7 * top), dma(7 * top), dma(7 * top), dma(12), dma(12), dma(8 * fs // uw + 8),
     ]
     f32 = lambda a: jax.ShapeDtypeStruct(a.shape, F32)
-    vspec = pl.BlockSpec(memory_space=vm)
+    vspec, anywhere = pl.BlockSpec(memory_space=vm), pl.BlockSpec(memory_space=pl.ANY)
     res = pl.pallas_call(
         functools.partial(block_kernel, dims),
         out_shape=(
-            jax.ShapeDtypeStruct((tok, wid), BF), jax.ShapeDtypeStruct((tok, wid), BF),
-            jax.ShapeDtypeStruct((n_dp, rows, 4 * uw), BF), f32(out_weight), f32(down_weight),
-            jax.ShapeDtypeStruct((16, 128), F32),
+            jax.ShapeDtypeStruct(tokens.shape, BF), jax.ShapeDtypeStruct(tokens.shape, BF),
+            f32(in_weight), f32(out_weight), f32(gate_weight), f32(up_weight), f32(down_weight),
+            jax.ShapeDtypeStruct((16, 128), F32), jax.ShapeDtypeStruct((2, rows, 128), F32),
         ),
-        in_specs=[vspec] * 6 + [pl.BlockSpec(memory_space=pl.ANY)] * 2 + [vspec],
-        out_specs=(vspec,) * 6,
+        in_specs=[anywhere] * 2 + [vspec] * 2 + [anywhere, vspec] + [anywhere] * 3,
+        out_specs=(anywhere,) * 2 + (vspec,) * 7,
         scratch_shapes=scratch,
         compiler_params=pltpu.CompilerParams(collective_id=0, has_side_effects=True, vmem_limit_bytes=64 * 1024 * 1024),
-    )(tokens[0], cotangent[0], masks, gain_tile, in_weight, out_weight, gate_weight, up_weight, down_weight)
-    grad_tile = res[2].astype(F32)
-    grad_in = grad_tile[:, :, :uw].reshape(n_dp, rows, 3, ch).transpose(1, 2, 0, 3).reshape(rows, 3 * wid)
-    pairs = grad_tile[:, :, uw:].reshape(n_dp, rows, 3, 2, cj).transpose(3, 1, 0, 2, 4).reshape(2, rows, n_dp * fs)
-    small = lax.dynamic_slice(res[5], (0, lane0), (16, lanes))
-    return (res[0][None], res[1][None], grad_in, res[3], pairs[0], pairs[1], res[4], small[0], small[1], small[2:5])
+    )(tokens, cotangent, masks, gain_tile, in_weight, out_weight, gate_weight, up_weight, down_weight)
+    sums = jnp.sum(res[8], axis=2)
+    low = lambda g: g.astype(BF).astype(F32)
+    return (*res[:7], sums[0] / low(norm_one), sums[1] / low(norm_two), res[7][:3, :lanes])
 
 
 def gather(value, axis=0):

time: 246 us -> 217 us (0.88)
  Pallas kernels: 229 us -> 201 us
    pallas_call x1, Pallas kernels: 229 us -> 201 us  [fast_body(): pl.pallas_call(functools.partial(block_kernel, dims), out_shape=(jax.Shap...]
    unnamed x16 -> x33, local copies, waits for them, and re-layouts: 3.66 us -> 10.1 us
    squeeze x3 -> x0, local copies, waits for them, and re-layouts: 3.63 us -> none  [the longest x1 1.34 us: fast_body(): small[1]]
where the time goes in v2:
time: 217 us; the launch traced here: 216 us
  Pallas kernels  201 us (93%)
  local copies, waits for them, and re-layouts  12 us (6%)
    pallas_call x1, Pallas kernels, fast_body(): pl.pallas_call(functools.partial(block_kernel, dims), out_shape=(jax.Shap...  201 us
    unnamed x33, local copies, waits for them, and re-layouts  10.1 us

profile of v2, /device:TPU:0, one launch (start us, length us, event | category | flops | bytes accessed | tf_op | source)
XLA Modules:
  0.0 215.7 jit_solution(7184923660424395348)
XLA Ops:
  0.7 0.7 copy-done.8
  1.3 0.6 copy-done.9
  2.0 0.3 dynamic_update_slice.3.gain_ref
  2.4 0.6 copy-done.6
  3.0 0.1 concatenate.7
  3.0 0.1 dynamic_slice.3
  3.1 0.1 slice_compare_fusion.3
  3.3 0.2 copy.25
  3.4 0.7 pad_convert_fusion.mask_ref
  4.1 200.8 %shard_map.186 = (bf16[1,256,1024]{2,1,0:T(8,128)(2,1)}, bf16[1,256,1024]{2,1,0:T(8,128)(2,1)}, f32[32,3072]{1,0:T(8,128)}, f32[32,1024]{1,0:T(8,128)}, f32[32,4...) custom-call(bf16[1,256,1024]{2,1,0:T(8,128)(2,1)} %x_ref.1, ...), custom_call_target="tpu_custom_call" | custom-call | tf_op jit(solution)/shard_map/pallas_call | solution.py:816
  204.9 0.9 reduce_sum.9
  205.8 0.5 bitcast_divide_fusion
  206.3 1.3 slice.31
  207.6 1.9 copy.34
  209.5 0.8 copy.35
  210.3 0.4 copy-done.4
  210.7 0.7 copy.36
  211.4 0.2 copy-done.5
  211.7 0.7 copy.37
  212.3 0.8 copy.38
  213.2 0.5 copy-done.1
  213.6 0.8 copy.39
  214.4 0.5 copy-done
  214.9 0.8 copy.40
  (29 shorter events, 0.1 us)
Async XLA Ops:
  0.7 0.7 copy-start.8
  1.3 0.7 copy-start.9
  1.3 0.7 copy-start.11
  2.0 0.9 copy-start.7
  2.4 0.6 copy-start.6
  204.9 0.9 copy-start.10
  204.9 0.9 copy-start.12
  207.6 1.9 copy-start.3
  209.5 1.2 copy-start.4
  210.7 1.0 copy-start.5
  210.7 1.7 copy-start.2
  212.3 1.3 copy-start.1
  213.6 1.3 copy-start

commit v3 on v2

--- a/solution.py
+++ b/solution.py
@@ -32,19 +32,20 @@
         pl.when(pred)(body)
 
 
-GAIN, IN, OUT, GU0, DOWN, GU1, GU2 = range(7)
-SLOT = {IN: 0, GU0: 1, GU1: 2, GU2: 3}
+GAIN, IN, OUT, GU0, DOWN, GU1, GU2, IN_A, IN_B, IN_C = range(10)
+SLOT = {IN: 0, GU0: 1, GU1: 2, GU2: 3, IN_A: 4, IN_B: 5, IN_C: 6}
+PIECES = (IN_A, IN_B, IN_C)
 AX, AZ, AO, AR = range(4)
 
 
 def block_kernel(
     dims,
-    x_ref, do_ref, mask_ref, gain_ref, win_ref, wout_ref, wg_ref, wu_ref, wdn_ref,
-    out_ref, gtok_ref, gin_ref, gout_ref, ggate_ref, gup_ref, gdown_ref, gsmall_ref, gains_ref,
+    x_ref, do_ref, seg_ref, n1_ref, n2_ref, taps_ref, win_ref, wout_ref, wg_ref, wu_ref, wdn_ref,
+    out_ref, gtok_ref, gin_ref, gout_ref, ggate_ref, gup_ref, gdown_ref, gsmall_ref,
     stage, wall, wo, wd, gb, gv, xa, ma, za, oa, ra, big, mbuf, pbuf, ybuf, halo_p, halo_q,
     sb_a, sb_b, rx_a, ry_a, fx_a, fy_a, rx_b, ry_b, fx_b, fy_b, hid, dh,
     gw, gd, go, dd_g, dd_d, dd_o, up_g, up_d, up_o, dn_g, dn_d, dn_o,
-    rbuf, gsum, s2, dd_s, up_s, dn_s,
+    rbuf, gsum, near, fm, s2, dd_s, up_s, dn_s,
     zs, zr, ws, wr, gs, gr, ms, mr, hs, hr, ags, agr, rss, rsr, ds_, dr_, us, ur, vs, vr, qs, qr, ins,
 ):
     tok, wid, nz, rows, ch, fs, cj, uw, drows = dims
@@ -104,12 +105,17 @@
     ones = [jnp.where(p, 1, 0) for p in (has_up, has_dn, cross_next, cross_prev)]
     pl.semaphore_wait(barrier, 4 + ones[0] + ones[1] + ones[2] + ones[3])
 
+    def span(unit):
+        if unit in PIECES:
+            return (SLOT[unit] - SLOT[IN_A]) * ch, ch
+        return SLOT[unit] * uw, uw
+
     def cols(unit):
-        return pl.ds(SLOT[unit] * uw, uw)
+        return pl.ds(*span(unit))
 
     def w_block(unit, zz, cc):
         if unit == GAIN:
-            return gb.at[d, zz, cc]
+            return gb.at[:, zz, cc]
         if unit == OUT:
             return wo.at[pl.ds(pl.multiple_of((2 * zz + cc) * rows, rows), rows), :]
         if unit == DOWN:
@@ -165,11 +171,17 @@
         blk = lambda: buf.at[idx, part, :]
         send("ag", True, blk, blk, lambda: ags.at[a * 6 + k], lambda: agr.at[a * 6 + rk], tgt)
 
-    def ag_start(a, buf):
+    def ag_first(a, buf):
         ag_send(a, buf, d, hi, 0, 1, to_x)
         ag_send(a, buf, d, lo, 1, 2, to_y)
+
+    def ag_second(a, buf):
         ag_send(a, buf, d, lo, 2, 0, to_x)
         ag_send(a, buf, d, hi, 3, 3, to_y)
+
+    def ag_start(a, buf):
+        ag_first(a, buf)
+        ag_second(a, buf)
 
     def ag_recv(a, buf, idx, part, rk):
         recv(True, lambda: buf.at[idx, part, :], lambda: agr.at[a * 6 + rk])
@@ -191,12 +203,14 @@
     def rs_send(r, tag, src, dst, k, tgt):
         send(tag, True, src, dst, lambda: rss.at[r * 6 + k], lambda: rsr.at[r * 6 + k], tgt)
 
-    def rs_run(r, sb, bufs, tile, tag, first=0):
+    def rs_run(r, sb, bufs, tile, tag, first=0, between=None):
         wide = pl.ds(first, wid)
         rx, ry, fx, fy = bufs
         sb[dg, :, wide] = tile(dg).astype(BF)
         rs_send(r, tag, lambda: sb.at[dg, lo, wide], lambda: fx, 0, to_x)
         rs_send(r, tag, lambda: sb.at[dg, hi, wide], lambda: fy, 1, to_y)
+        if between is not None:
+            between()
         sb[xn, :, wide] = tile(xn).astype(BF)
         rs_send(r, tag, lambda: sb.at[xn, lo, wide], lambda: rx.at[lo, :], 2, to_x)
         sb[yn, :, wide] = tile(yn).astype(BF)
@@ -289,14 +303,17 @@
         pl.when(has_up)(lambda: g_add(unit, acc, (acc, dn_ref())))
 
     def row_send(unit, idx):
-        return big.at[idx, pl.ds(SLOT[unit] * rows, rows), pl.ds(2 * fs, uw)]
+        first, n = span(unit)
+        row = 0 if unit in PIECES else SLOT[unit]
+        return big.at[idx, pl.ds(row * rows, rows), pl.ds(2 * fs + (first if unit in PIECES else 0), n)]
 
     def g_rows(unit):
-        facc = mbuf.at[:, pl.ds(0, rows), :]
+        first, n = span(unit)
+        facc = mbuf.at[:, pl.ds(0, rows), pl.ds(0, n)]
         g_last(unit, facc)
         u = SLOT[unit]
         for k in range(4):
-            big[k, pl.ds(u * rows, rows), pl.ds(2 * fs, uw)] = facc[k].astype(BF)
+            row_send(unit, k)[...] = facc[k].astype(BF)
         rbuf[d, :, cols(unit)] = facc[d].astype(BF)
         for k, (idx, tgt) in enumerate(peers):
             send(
@@ -308,16 +325,16 @@
 
     def g_rows_wait(unit):
         u = SLOT[unit]
+        first, n = span(unit)
         for k, (idx, _) in enumerate(peers):
             recv(True, lambda idx=idx: rbuf.at[idx, :, cols(unit)], lambda k=k: qr.at[u * 3 + k])
         for k in range(4):
-            if unit == IN:
-                for p in range(3):
-                    gin_ref[:, pl.ds(p * wid + k * ch, ch)] = rbuf[k, :, pl.ds(p * ch, ch)].astype(F32)
+            if unit in PIECES:
+                gin_ref[:, pl.ds(first // ch * wid + k * ch, ch)] = rbuf[k, :, cols(unit)].astype(F32)
             else:
                 j = u - 1
-                ggate_ref[:, pl.ds(k * fs + j * cj, cj)] = rbuf[k, :, pl.ds(u * uw, cj)].astype(F32)
-                gup_ref[:, pl.ds(k * fs + j * cj, cj)] = rbuf[k, :, pl.ds(u * uw + cj, cj)].astype(F32)
+                ggate_ref[:, pl.ds(k * fs + j * cj, cj)] = rbuf[k, :, pl.ds(first, cj)].astype(F32)
+                gup_ref[:, pl.ds(k * fs + j * cj, cj)] = rbuf[k, :, pl.ds(first + cj, cj)].astype(F32)
 
     count = 4 * fs // uw
 
@@ -359,46 +376,70 @@
         for p in range(3):
             b, first = divmod(p * wid + k * ch, uw)
             stage[k, :, pl.ds(p * ch, ch)] = mbuf[2 + b // 2, pl.ds(tok - rows * (1 + b % 2), rows), pl.ds(first, ch)].astype(BF)
+    lanes = taps_ref.shape[1]
+    lane0 = lax.rem(s * rows, 128)
+    gsum[...] = jnp.zeros_like(gsum)
+    gsum[0:1, 0:lanes] = n1_ref[...]
+    gsum[1:2, 0:lanes] = n2_ref[...]
+    gsum[2:5, 0:lanes] = taps_ref[...]
+    gb[d, z, c] = pltpu.roll(gsum[...], lane0, 1).astype(BF)
+    for k, (idx, tgt) in enumerate(peers):
+        send("w", True, lambda: gb.at[d, z, c], lambda: gb.at[d, z, c], lambda k=k: gs.at[k], lambda k=k: gr.at[k], tgt)
     w_slice(IN)
-    gb[d, z, c] = gain_ref[...]
-    z_own(GAIN)
     x_in.wait()
     ag_start(AX, xa)
     wo[pl.ds(pl.multiple_of(s * rows, rows), rows), :] = wout_ref[...].astype(BF)
     z_own(OUT)
-    ma[d] = mask_ref[...]
+    mid = seg_ref[:, pl.ds(pl.multiple_of(s * tok, tok), tok)]
+    near[:, pl.ds(128, tok)] = mid
+    near[:, pl.ds(0, 128)] = jnp.full((1, 128), -1, jnp.int32)
+    near[:, pl.ds(128 + tok, 128)] = jnp.full((1, 128), -1, jnp.int32)
+
+    @pl.when(s > 0)
+    def _():
+        near[:, pl.ds(0, 128)] = seg_ref[:, pl.ds(pl.multiple_of(s * tok - 128, 128), 128)]
+
+    @pl.when(s < 2 * nz - 1)
+    def _():
+        near[:, pl.ds(128 + tok, 128)] = seg_ref[:, pl.ds(pl.multiple_of(s * tok + tok, 128), 128)]
+
+    around = near[...]
+    lane = lax.broadcasted_iota(jnp.int32, (128, tok), 0)
+    flags = jnp.zeros((128, tok), F32)
+    for k, move in enumerate((1, 2, tok + 255, tok + 254)):
+        moved = pltpu.roll(around, move, 1)[:, 128 : 128 + tok]
+        flags = jnp.where(lane == k, jnp.where(moved == mid, 1.0, 0.0), flags)
+    fm[d] = flags[:16].astype(BF)
+    for k, (idx, _) in enumerate(peers):
+        recv(True, lambda idx=idx: gb.at[idx, z, c], lambda k=k: gr.at[k])
+    z_own(GAIN)
+    w_slice_wait(IN)
+    z_own(IN)
     for i in range(2 * count):
         wide_in(i).wait()
     for k in range(4):
         for j in range(3):
             stage[k, :, pl.ds((1 + j) * uw, cj)] = wide_read(0, k * fs + j * cj, cj).astype(BF)
             stage[k, :, pl.ds((1 + j) * uw + cj, cj)] = wide_read(1, k * fs + j * cj, cj).astype(BF)
-    w_slice_wait(IN)
-    z_own(IN)
     for i in range(2):
         down_in(i).wait()
     wd[pl.ds(pl.multiple_of(s * drows, drows), drows), pl.ds(0, uw)] = mbuf[2, pl.ds(0, drows), :].astype(BF)
     wd[pl.ds(pl.multiple_of(s * drows, drows), drows), pl.ds(uw, wid - uw)] = mbuf[3, pl.ds(0, drows), pl.ds(0, wid - uw)].astype(BF)
+    z_fwd(OUT, 1)
     z_fwd(GAIN, 1)
-    z_fwd(OUT, 1)
     ag_fwd(AX, xa)
     for k, (idx, tgt) in enumerate(peers):
-        send("ag", True, lambda: ma.at[d], lambda: ma.at[d], lambda k=k: ms.at[k], lambda k=k: mr.at[k], tgt)
+        send("ag", True, lambda: fm.at[d], lambda: fm.at[d], lambda k=k: ms.at[k], lambda k=k: mr.at[k], tgt)
     w_slice(GU0)
+    z_fwd(IN, 1)
     z_fwd(GAIN, 2)
-    z_fwd(IN, 1)
     z_fwd(OUT, 2)
+    w_slice(GU1)
+    w_slice(GU2)
+    do_in.wait()
+    ag_first(AO, oa)
     z_fwd(GAIN, 3)
     z_finish(GAIN)
-    for k, (idx, tgt) in enumerate(peers):
-        send("w", True, lambda: gb.at[d], lambda: gb.at[d], lambda k=k: gs.at[k], lambda k=k: gr.at[k], tgt)
-    w_slice(GU1)
-    w_slice(GU2)
-    ag_near(AX, xa)
-    z_fwd(IN, 2)
-    z_fwd(OUT, 3)
-    for k, (idx, _) in enumerate(peers):
-        recv(True, lambda idx=idx: gb.at[idx], lambda k=k: gr.at[k])
     per = 128 // rows
     for g in range(wid // 128):
         tot = None
@@ -424,16 +465,22 @@
             big[dd, rr, zcol] = (xv * norm_rows(xv) * gv[0:1, :]).astype(BF)
 
     make_z1(d)
+    ag_near(AX, xa)
     make_z1(xn)
     make_z1(yn)
-    z_fwd(IN, 3)
+    z_fwd(IN, 2)
+    z_fwd(OUT, 3)
+    z_own(DOWN)
+    ag_far(AX, xa)
+    make_z1(dg)
     w_slice_wait(GU0)
     z_own(GU0)
-    ag_far(AX, xa)
-    make_z1(dg)
+    z_fwd(IN, 3)
     z_finish(IN)
     for k, (idx, _) in enumerate(peers):
-        recv(True, lambda idx=idx: ma.at[idx], lambda k=k: mr.at[k])
+        recv(True, lambda idx=idx: fm.at[idx], lambda k=k: mr.at[k])
+    for dd in range(4):
+        ma[dd] = jnp.concatenate([fm[dd].astype(F32), jnp.zeros((112, tok), F32)], axis=0).T.astype(BF)
 
     def unit_w(lo_col, n):
         return wall[:, :, :, :, pl.ds(lo_col, n)].reshape(wid, n)
@@ -453,7 +500,6 @@
         halo_p[...] = jnp.zeros_like(halo_p)
 
     z_finish(OUT)
-    z_fwd(GU0, 1)
     w_slice_wait(GU1)
     z_own(GU1)
     recv(s > 0, lambda: halo_p, lambda: hr.at[0])
@@ -481,15 +527,14 @@
 
     rs_run(0, sb_a, bufs_a, h_tile, "rs0")
     hid[...] = h_tile(d)
-    z_fwd(GU0, 2)
+    z_fwd(DOWN, 1)
     w_slice_wait(GU2)
     z_own(GU2)
+    z_fwd(GU0, 1)
+    rs_pass(0, sb_a, bufs_a, "rs0")
     z_fwd(GU1, 1)
-    rs_pass(0, sb_a, bufs_a, "rs0")
-    z_fwd(GU0, 3)
-    z_own(DOWN)
-    z_fwd(GU1, 2)
     z_fwd(GU2, 1)
+    z_fwd(DOWN, 2)
     rs_wait(0, bufs_a)
 
     @pl.loop(0, tok // step)
@@ -500,7 +545,6 @@
         za[d, rr, :] = (h * norm_rows(h) * gv[1:2, :]).astype(BF)
 
     ag_start(AZ, za)
-    do_in.wait()
 
     def acol(j):
         return pl.ds(j * cj, cj)
@@ -550,53 +594,56 @@
     def out_tile(dd):
         return dot_nn(big[dd, :, pl.ds(0, fs)], wd[...])
 
+    z_fwd(GU0, 2)
+    z_fwd(GU1, 2)
+    ag_fwd(AZ, za)
+    ag_fwd(AO, oa)
+    ag_second(AO, oa)
+    z_fwd(GU2, 2)
+    z_fwd(DOWN, 3)
+    z_finish(DOWN)
+    ag_near(AZ, za)
+    z_fwd(GU0, 3)
     z_finish(GU0)
-    gate_one(0, d)
+    ag_far(AZ, za)
+    gate_all(0)
     z_fwd(GU1, 3)
-    z_fwd(GU2, 2)
-    ag_fwd(AZ, za)
-    ag_start(AO, oa)
     z_finish(GU1)
-    gate_one(1, d)
-    z_fwd(DOWN, 1)
-    ag_near(AZ, za)
+    gate_all(1)
     z_fwd(GU2, 3)
     z_finish(GU2)
-    gate_one(2, d)
-    for j in range(3):
-        gate_one(j, xn)
-    ag_fwd(AO, oa)
-    z_fwd(DOWN, 2)
-    for j in range(3):
-        gate_one(j, yn)
-    ag_far(AZ, za)
-    for j in range(3):
-        gate_one(j, dg)
-    z_fwd(DOWN, 3)
-    z_finish(DOWN)
-    rs_run(2, sb_b, bufs_b, out_tile, "rs2")
+    gate_all(2)
     ag_near(AO, oa)
     ag_far(AO, oa)
     for j in range(3):
         grad_down(j)
     g_pair(DOWN)
+
+    def down_off():
+        g_pair_wait(DOWN)
+        g_hop(DOWN, 0)
+
+    rs_run(2, sb_b, bufs_b, out_tile, "rs2", between=down_off)
     for j in range(3):
         back_all(j)
-    g_pair_wait(DOWN)
-    g_hop(DOWN, 0)
 
     drain("rs0")
     rs_run(1, sb_a, bufs_a, dz2_tile, "rs1")
-    rs_pass(2, sb_b, bufs_b, "rs2")
-    dh[...] = dz2_tile(d)
     grad_gu(0)
     g_pair(GU0)
-    rs_pass(1, sb_a, bufs_a, "rs1")
     g_hop(DOWN, 1)
+    dh[...] = dz2_tile(d)
     g_pair_wait(GU0)
     g_hop(GU0, 0)
+    rs_pass(1, sb_a, bufs_a, "rs1")
     grad_gu(1)
     g_pair(GU1)
+    g_hop(DOWN, 2)
+    g_pair_wait(GU1)
+    g_hop(GU1, 0)
+    grad_gu(2)
+    g_pair(GU2)
+    g_hop(GU0, 1)
     rs_wait(1, bufs_a)
 
     @pl.loop(0, tok // step)
@@ -612,29 +659,17 @@
         ra[d, rr, :] = g.astype(BF)
 
     ag_start(AR, ra)
-    g_hop(DOWN, 2)
-    g_hop(GU0, 1)
-    g_pair_wait(GU1)
-    g_hop(GU1, 0)
-    grad_gu(2)
-    g_pair(GU2)
-    ag_fwd(AR, ra)
+    g_pair_wait(GU2)
+    g_hop(GU2, 0)
     hid[...] = hid[...] + out_tile(d)
-    rs_wait(2, bufs_b)
-
-    @pl.loop(0, tok // step)
-    def _(i):
-        rr = pl.ds(pl.multiple_of(i * step, step), step)
-        sb_b[d, rr, :] = (hid[rr, :] + rx_b[rr, :].astype(F32) + ry_b[rr, :].astype(F32)).astype(BF)
-
-    result = pltpu.make_async_copy(sb_b.at[d], out_ref.at[0], ins.at[2 * count])
-    result.start()
     for dd in (d, xn, yn, dg):
         make_z1(dd)
     g_hop(GU0, 2)
-    g_pair_wait(GU2)
-    g_hop(GU2, 0)
+    ag_fwd(AR, ra)
+    g_hop(GU1, 1)
+    rs_pass(2, sb_b, bufs_b, "rs2")
     ag_near(AR, ra)
+    g_hop(GU1, 2)
     ag_far(AR, ra)
 
     mcol = fs
@@ -663,7 +698,10 @@
     for q in range(2 * nz):
         first = (q * rows) // 128 * 128
         s2[q // 2, q % 2] = tap_rows[:, first : first + 128].astype(BF)
-    g_hop(GU1, 1)
+    go[...] = dot_tn(ybuf[...].reshape(4 * tok, ch), ra[...].reshape(4 * tok, wid)).astype(BF)
+    g_pair(OUT)
+    g_pair(GAIN)
+    g_hop(GU2, 1)
     recv(s < 2 * nz - 1, lambda: halo_q, lambda: hr.at[1])
 
     @pl.loop(0, 4)
@@ -684,41 +722,57 @@
 
     rs_run(3, sb_a, bufs_a, dz1_tile, "rs3")
 
-    @pl.loop(0, 4)
-    def _(dd):
-        left = big[:, :, pl.ds(pl.multiple_of(dd * ch, ch), ch)].reshape(4 * tok, ch)
-        right = big[:, :, pl.ds(mcol, uw)].reshape(4 * tok, uw)
-        gw[dd, :, :, :, pl.ds(0, uw)] = dot_tn(left, right).astype(BF).reshape(nz, 2, rows, uw)
-
-    g_pair(IN)
-    g_hop(GU2, 1)
-    g_hop(GU1, 2)
-    go[...] = dot_tn(ybuf[...].reshape(4 * tok, ch), ra[...].reshape(4 * tok, wid)).astype(BF)
-    g_pair(OUT)
-    g_pair(GAIN)
-    rs_pass(3, sb_a, bufs_a, "rs3")
-    g_pair_wait(IN)
-    g_hop(IN, 0)
+    def grad_in(p):
+        left = big[:, :, zcol].reshape(4 * tok, wid)
+        right = big[:, :, pl.ds(mcol + p * ch, ch)].reshape(4 * tok, ch)
+        gw[:, :, :, :, pl.ds(p * ch, ch)] = dot_tn(left, right).astype(BF).reshape(4, nz, 2, rows, ch)
+
     g_pair_wait(OUT)
     g_hop(OUT, 0)
     g_pair_wait(GAIN)
     g_hop(GAIN, 0)
+    grad_in(0)
+    g_pair(IN_A)
+    grad_in(1)
+    g_pair(IN_B)
+    g_pair_wait(IN_A)
+    g_hop(IN_A, 0)
+    grad_in(2)
+    g_pair(IN_C)
+    g_pair_wait(IN_B)
+    g_hop(IN_B, 0)
+    g_hop(GU2, 2)
+    g_pair_wait(IN_C)
+    g_hop(IN_C, 0)
+    rs_pass(3, sb_a, bufs_a, "rs3")
+    g_hop(OUT, 1)
+    g_hop(GAIN, 1)
+    rs_wait(2, bufs_b)
+
+    @pl.loop(0, tok // step)
+    def _(i):
+        rr = pl.ds(pl.multiple_of(i * step, step), step)
+        sb_b[d, rr, :] = (hid[rr, :] + rx_b[rr, :].astype(F32) + ry_b[rr, :].astype(F32)).astype(BF)
+
+    result = pltpu.make_async_copy(sb_b.at[d], out_ref.at[0], ins.at[2 * count])
+    result.start()
     hid[...] = dz1_tile(d)
     drain("halo")
-    drain("rs2")
-    g_hop(GU2, 2)
-    g_rows(GU0)
-    g_hop(IN, 1)
-    g_hop(OUT, 1)
-    g_hop(GAIN, 1)
-    g_last(DOWN, gdown_ref)
-    g_rows(GU1)
-    rs_wait(3, bufs_a)
-    g_hop(IN, 2)
+    g_hop(IN_A, 1)
     g_hop(OUT, 2)
     g_hop(GAIN, 2)
+    g_rows(GU0)
+    g_hop(IN_B, 1)
+    g_hop(IN_A, 2)
+    g_rows(GU1)
+    g_hop(IN_C, 1)
+    g_hop(IN_B, 2)
+    g_last(DOWN, gdown_ref)
+    g_hop(IN_C, 2)
     g_rows(GU2)
     g_rows_wait(GU0)
+    g_rows_wait(GU1)
+    rs_wait(3, bufs_a)
 
     @pl.loop(0, tok // step)
     def _(i):
@@ -734,14 +788,12 @@
     grads = pltpu.make_async_copy(sb_a.at[d], gtok_ref.at[0], ins.at[2 * count + 1])
     grads.start()
 
-    g_rows_wait(GU1)
-    g_rows(IN)
+    g_rows(IN_A)
     g_last(OUT, gout_ref)
     g_last(GAIN, gsum)
+    gsmall_ref[pl.ds(8, 8), :] = pltpu.roll(gsum[...], lax.rem(128 - lane0, 128), 1)[:8]
     g_rows_wait(GU2)
-    lane0 = lax.rem(s * rows, 128)
-    gsmall_ref[...] = pltpu.roll(gsum[...], lax.rem(128 - lane0, 128), 1)
-    g_rows_wait(IN)
+    g_rows(IN_B)
 
     def gain_sum(first, n):
         acc = jnp.zeros((rows, 128), F32)
@@ -751,11 +803,39 @@
                 acc = acc + stage[k, :, cc].astype(F32) * rbuf[k, :, cc].astype(F32)
         return acc
 
-    gains_ref[0] = gain_sum(0, uw)
-    gains_ref[1] = gain_sum(uw, 3 * uw)
+    def gain_out(k, first, n, gain):
+        total = lax.dot_general(
+            jnp.ones((8, 128), F32), gain_sum(first, n), (((1,), (1,)), ((), ())),
+            precision=lax.Precision.HIGHEST, preferred_element_type=F32,
+        )
+        gsmall_ref[k : k + 1, 0:lanes] = total[0:1] / gain[...].astype(BF).astype(F32)
+
+    gain_out(1, uw, 3 * uw, n2_ref)
+    g_rows(IN_C)
+    for unit in PIECES:
+        g_rows_wait(unit)
+    gain_out(0, 0, uw, n1_ref)
     result.wait()
     grads.wait()
     drain()
+
+
+def move_out(lanes, *refs):
+    n = (len(refs) - 6) // 3
+    small_ref, one_ref, two_ref, taps_ref = refs[n], *refs[2 * n + 1 : 2 * n + 4]
+    outs, held, sems, done = refs[n + 1 : 2 * n + 1], refs[2 * n + 4 : 3 * n + 4], refs[-2], refs[-1]
+    loads = [pltpu.make_async_copy(refs[k], held[k], sems.at[k]) for k in range(n)]
+    stores = [pltpu.make_async_copy(held[k], outs[k], done.at[k]) for k in range(n)]
+    for load in loads:
+        load.start()
+    one_ref[...] = small_ref[0:1, 0:lanes]
+    two_ref[...] = small_ref[1:2, 0:lanes]
+    taps_ref[...] = small_ref[8:11, 0:lanes]
+    for load, store in zip(loads, stores):
+        load.wait()
+        store.start()
+    for store in stores:
+        store.wait()
 
 
 def fast_body(n_dp, n_seq, tokens, segments, cotangent, in_weight, out_weight, gate_weight, up_weight, down_weight, norm_one, norm_two, kernel):
@@ -768,16 +848,6 @@
     uw = 3 * ch
     cj = uw // 2
     lanes = kernel.shape[1]
-    place = lax.axis_index("dp") * n_seq + lax.axis_index("seq")
-    lane0 = lax.rem(place, 128 // lanes) * lanes
-    gains = jnp.concatenate([norm_one[None], norm_two[None], kernel], axis=0).astype(BF)
-    gain_tile = lax.dynamic_update_slice(jnp.zeros((16, 128), BF), gains, (0, lane0))
-    offset = lax.axis_index("seq") * tok
-    filler = jnp.full((2,), -1, jnp.int32)
-    near = lax.dynamic_slice_in_dim(jnp.concatenate([filler, segments[0], filler]), offset, tok + 4)
-    mid = near[2 : tok + 2]
-    same = [mid == near[1 : tok + 1], mid == near[0:tok], mid == near[3 : tok + 3], mid == near[4 : tok + 4]]
-    masks = jnp.pad(jnp.stack(same, axis=1).astype(BF), ((0, 0), (0, 124)))
 
     dims = (tok, wid, nz, rows, ch, fs, cj, uw, drows)
     top = nz - 1
@@ -804,12 +874,12 @@
         vm((nz, n_dp, rows, 4 * uw), BF), vm((nz, drows, wid), BF), vm((nz, rows, wid), BF),
         vm((top, n_dp, rows, 4 * uw), BF), vm((top, drows, wid), BF), vm((top, rows, wid), BF),
         vm((top, n_dp, rows, 4 * uw), BF), vm((top, drows, wid), BF), vm((top, rows, wid), BF),
-        vm((n_dp, rows, 4 * uw), BF), vm((16, 128), F32),
+        vm((n_dp, rows, 4 * uw), BF), vm((16, 128), F32), vm((1, tok + 256), jnp.int32), vm((n_dp, 16, tok), BF),
         vm((nz, 2, 16, 128), BF),
         vm((nz, 16, 128), BF), vm((top, 16, 128), BF), vm((top, 16, 128), BF),
         dma(7 * 13), dma(7 * 2 * nz), dma(12), dma(12), dma(3), dma(3), dma(3), dma(3), dma(2), dma(2),
-        dma(24), dma(24), dma(24), dma(24), dma(7 * nz), dma(7 * nz),
-        dma(7 * top), dma(7 * top), dma(7 * top), dma(7 * top), dma(12), dma(12), dma(8 * fs // uw + 8),
+        dma(24), dma(24), dma(24), dma(24), dma(10 * nz), dma(10 * nz),
+        dma(10 * top), dma(10 * top), dma(10 * top), dma(10 * top), dma(21), dma(21), dma(8 * fs // uw + 8),
     ]
     f32 = lambda a: jax.ShapeDtypeStruct(a.shape, F32)
     vspec, anywhere = pl.BlockSpec(memory_space=vm), pl.BlockSpec(memory_space=pl.ANY)
@@ -818,16 +888,23 @@
         out_shape=(
             jax.ShapeDtypeStruct(tokens.shape, BF), jax.ShapeDtypeStruct(tokens.shape, BF),
             f32(in_weight), f32(out_weight), f32(gate_weight), f32(up_weight), f32(down_weight),
-            jax.ShapeDtypeStruct((16, 128), F32), jax.ShapeDtypeStruct((2, rows, 128), F32),
+            jax.ShapeDtypeStruct((16, 128), F32),
         ),
-        in_specs=[anywhere] * 2 + [vspec] * 2 + [anywhere, vspec] + [anywhere] * 3,
-        out_specs=(anywhere,) * 2 + (vspec,) * 7,
+        in_specs=[anywhere] * 2 + [vspec] * 4 + [anywhere, vspec] + [anywhere] * 3,
+        out_specs=(anywhere,) * 2 + (vspec,) * 6,
         scratch_shapes=scratch,
         compiler_params=pltpu.CompilerParams(collective_id=0, has_side_effects=True, vmem_limit_bytes=64 * 1024 * 1024),
-    )(tokens, cotangent, masks, gain_tile, in_weight, out_weight, gate_weight, up_weight, down_weight)
-    sums = jnp.sum(res[8], axis=2)
-    low = lambda g: g.astype(BF).astype(F32)
-    return (*res[:7], sums[0] / low(norm_one), sums[1] / low(norm_two), res[7][:3, :lanes])
+    )(tokens, cotangent, segments, norm_one[None], norm_two[None], kernel, in_weight, out_weight, gate_weight, up_weight, down_weight)
+    final = [jax.ShapeDtypeStruct(v.shape, v.dtype) for v in res[:7]]
+    final += [jax.ShapeDtypeStruct((k, lanes), F32) for k in (1, 1, 3)]
+    moved = pl.pallas_call(
+        functools.partial(move_out, lanes),
+        out_shape=tuple(final),
+        in_specs=[anywhere] * 7 + [vspec],
+        out_specs=(anywhere,) * 7 + (vspec,) * 3,
+        scratch_shapes=[vm(v.shape, v.dtype) for v in res[:7]] + [dma(7), dma(7)],
+    )(*res)
+    return (*moved[:7], moved[7][0], moved[8][0], moved[9])
 
 
 def gather(value, axis=0):

time: 217 us -> 195 us (0.90)
  local copies, waits for them, and re-layouts: 12 us -> 0 us
  Pallas kernels: 201 us -> 193 us
    pallas_call x1, Pallas kernels: 201 us -> 189 us  [fast_body(): pl.pallas_call(functools.partial(block_kernel, dims), out_shape=(jax.Shap...]
    unnamed x33 -> x0, local copies, waits for them, and re-layouts: 10.1 us -> none
    pallas_call x0 -> x1, Pallas kernels: none -> 4.17 us  [fast_body(): pl.pallas_call(functools.partial(move_out, lanes), out_shape=tuple(final)...]
where the time goes in v3:
time: 195 us; the launch traced here: 194 us
  Pallas kernels  193 us (99%)
    pallas_call x1, Pallas kernels, fast_body(): pl.pallas_call(functools.partial(block_kernel, dims), out_shape=(jax.Shap...  189 us
    pallas_call x1, Pallas kernels, fast_body(): pl.pallas_call(functools.partial(move_out, lanes), out_shape=tuple(final)...  4.17 us

profile of v3, /device:TPU:0, one launch (start us, length us, event | category | flops | bytes accessed | tf_op | source)
XLA Modules:
  0.0 194.1 jit_solution(3330827334710059573)
XLA Ops:
  0.6 189.1 %shard_map.186 = (bf16[1,256,1024]{2,1,0:T(8,128)(2,1)}, bf16[1,256,1024]{2,1,0:T(8,128)(2,1)}, f32[32,3072]{1,0:T(8,128)}, f32[32,1024]{1,0:T(8,128)}, f32[32,4...) custom-call(bf16[1,256,1024]{2,1,0:T(8,128)(2,1)} %x_ref.1, ...), custom_call_target="tpu_custom_call" | custom-call | tf_op jit(solution)/shard_map/pallas_call | solution.py:886
  189.8 4.2 %shard_map.187 = (bf16[1,256,1024]{2,1,0:T(8,128)(2,1)}, bf16[1,256,1024]{2,1,0:T(8,128)(2,1)}, f32[32,3072]{1,0:T(8,128)}, f32[32,1024]{1,0:T(8,128)}, f32[32,4...) custom-call(bf16[1,256,1024]{2,1,0:T(8,128)(2,1)} %get-tuple-element, ...), custom_call_target="tpu_custom_call" | custom-call | tf_op jit(solution)/shard_map/pallas_call | solution.py:900

commit v4 on v3

--- a/solution.py
+++ b/solution.py
@@ -41,11 +41,11 @@
 def block_kernel(
     dims,
     x_ref, do_ref, seg_ref, n1_ref, n2_ref, taps_ref, win_ref, wout_ref, wg_ref, wu_ref, wdn_ref,
-    out_ref, gtok_ref, gin_ref, gout_ref, ggate_ref, gup_ref, gdown_ref, gsmall_ref,
+    out_ref, gtok_ref, rbuf, gout_ref, gdown_ref, gsmall_ref,
     stage, wall, wo, wd, gb, gv, xa, ma, za, oa, ra, big, mbuf, pbuf, ybuf, halo_p, halo_q,
     sb_a, sb_b, rx_a, ry_a, fx_a, fy_a, rx_b, ry_b, fx_b, fy_b, hid, dh,
     gw, gd, go, dd_g, dd_d, dd_o, up_g, up_d, up_o, dn_g, dn_d, dn_o,
-    rbuf, gsum, near, fm, s2, dd_s, up_s, dn_s,
+    gsum, near, fm, oacc,
     zs, zr, ws, wr, gs, gr, ms, mr, hs, hr, ags, agr, rss, rsr, ds_, dr_, us, ur, vs, vr, qs, qr, ins,
 ):
     tok, wid, nz, rows, ch, fs, cj, uw, drows = dims
@@ -102,8 +102,9 @@
     cross_prev = jnp.logical_and(c == 0, z > 0)
     pl.when(cross_next)(lambda: greet(to_next))
     pl.when(cross_prev)(lambda: greet(to_prev))
-    ones = [jnp.where(p, 1, 0) for p in (has_up, has_dn, cross_next, cross_prev)]
-    pl.semaphore_wait(barrier, 4 + ones[0] + ones[1] + ones[2] + ones[3])
+    def enter():
+        ones = [jnp.where(p, 1, 0) for p in (has_up, has_dn, cross_next, cross_prev)]
+        pl.semaphore_wait(barrier, 4 + ones[0] + ones[1] + ones[2] + ones[3])
 
     def span(unit):
         if unit in PIECES:
@@ -237,8 +238,6 @@
     bufs_b = (rx_b, ry_b, fx_b, fy_b)
 
     def g_own(unit, zz, cc):
-        if unit == GAIN:
-            return s2.at[zz, cc]
         if unit == OUT:
             return go.at[pl.ds(pl.multiple_of((2 * zz + cc) * rows, rows), rows), :]
         if unit == DOWN:
@@ -246,41 +245,37 @@
         return gw.at[:, zz, cc, :, cols(unit)]
 
     def g_in(unit, trio, zz):
-        buf = trio[{GAIN: 3, OUT: 2, DOWN: 1}.get(unit, 0)]
+        buf = trio[{OUT: 2, DOWN: 1}.get(unit, 0)]
         if unit in SLOT:
             return buf.at[zz, :, :, cols(unit)]
         return buf.at[zz]
 
-    t_dd = (dd_g, dd_d, dd_o, dd_s)
-    t_up = (up_g, up_d, up_o, up_s)
-    t_dn = (dn_g, dn_d, dn_o, dn_s)
-
-    def g_pair(unit):
-        for zz in range(nz):
+    t_dd = (dd_g, dd_d, dd_o)
+    t_up = (up_g, up_d, up_o)
+    t_dn = (dn_g, dn_d, dn_o)
+
+    def g_pair(unit, which=range(nz)):
+        for zz in which:
             send(
                 "g", True, lambda zz=zz: g_own(unit, zz, oc), lambda zz=zz: g_in(unit, t_dd, zz),
                 lambda zz=zz: ds_.at[unit * nz + zz], lambda zz=zz: dr_.at[unit * nz + zz], to_sib,
             )
 
-    def g_pair_wait(unit):
-        for zz in range(nz):
-            recv(True, lambda zz=zz: g_in(unit, t_dd, zz), lambda zz=zz: dr_.at[unit * nz + zz])
-
-    def g_add(unit, dst, parts):
-        shape = dst.shape
-        if len(shape) == 3:
-            for k in range(shape[0]):
+    def g_add(dst, parts):
+        if len(dst.shape) == 3:
+            for k in range(dst.shape[0]):
                 dst[k] = sum(p[k].astype(F32) for p in parts).astype(dst.dtype)
         else:
             dst[...] = sum(p[...].astype(F32) for p in parts).astype(dst.dtype)
 
     def g_step(unit, pred, zt, come, came, csem, ssem, rsem, there, tgt):
         mine, pair = (lambda: g_own(unit, zt, c)), (lambda: g_in(unit, t_dd, zt))
+        recv(pred, pair, lambda: dr_.at[unit * nz + zt])
         if come:
             recv(pred, came, csem)
-            pl.when(pred)(lambda: g_add(unit, mine(), (mine(), pair(), came())))
+            pl.when(pred)(lambda: g_add(mine(), (mine(), pair(), came())))
         else:
-            pl.when(pred)(lambda: g_add(unit, mine(), (mine(), pair())))
+            pl.when(pred)(lambda: g_add(mine(), (mine(), pair())))
         send("g", pred, mine, there, ssem, rsem, tgt)
 
     def g_hop(unit, h):
@@ -296,11 +291,12 @@
     def g_last(unit, acc):
         up_ref = lambda: g_in(unit, t_up, z - 1)
         dn_ref = lambda: g_in(unit, t_dn, z)
+        recv(True, lambda: g_in(unit, t_dd, z), lambda: dr_.at[unit * nz + z])
         recv(has_dn, up_ref, lambda: ur.at[unit * top + z - 1])
         recv(has_up, dn_ref, lambda: vr.at[unit * top + z])
-        g_add(unit, acc, (g_own(unit, z, c), g_in(unit, t_dd, z)))
-        pl.when(has_dn)(lambda: g_add(unit, acc, (acc, up_ref())))
-        pl.when(has_up)(lambda: g_add(unit, acc, (acc, dn_ref())))
+        g_add(acc, (g_own(unit, z, c), g_in(unit, t_dd, z)))
+        pl.when(has_dn)(lambda: g_add(acc, (acc, up_ref())))
+        pl.when(has_up)(lambda: g_add(acc, (acc, dn_ref())))
 
     def row_send(unit, idx):
         first, n = span(unit)
@@ -328,13 +324,6 @@
         first, n = span(unit)
         for k, (idx, _) in enumerate(peers):
             recv(True, lambda idx=idx: rbuf.at[idx, :, cols(unit)], lambda k=k: qr.at[u * 3 + k])
-        for k in range(4):
-            if unit in PIECES:
-                gin_ref[:, pl.ds(first // ch * wid + k * ch, ch)] = rbuf[k, :, cols(unit)].astype(F32)
-            else:
-                j = u - 1
-                ggate_ref[:, pl.ds(k * fs + j * cj, cj)] = rbuf[k, :, pl.ds(first, cj)].astype(F32)
-                gup_ref[:, pl.ds(k * fs + j * cj, cj)] = rbuf[k, :, pl.ds(first + cj, cj)].astype(F32)
 
     count = 4 * fs // uw
 
@@ -383,12 +372,13 @@
     gsum[1:2, 0:lanes] = n2_ref[...]
     gsum[2:5, 0:lanes] = taps_ref[...]
     gb[d, z, c] = pltpu.roll(gsum[...], lane0, 1).astype(BF)
+    wo[pl.ds(pl.multiple_of(s * rows, rows), rows), :] = wout_ref[...].astype(BF)
+    enter()
     for k, (idx, tgt) in enumerate(peers):
         send("w", True, lambda: gb.at[d, z, c], lambda: gb.at[d, z, c], lambda k=k: gs.at[k], lambda k=k: gr.at[k], tgt)
     w_slice(IN)
     x_in.wait()
     ag_start(AX, xa)
-    wo[pl.ds(pl.multiple_of(s * rows, rows), rows), :] = wout_ref[...].astype(BF)
     z_own(OUT)
     mid = seg_ref[:, pl.ds(pl.multiple_of(s * tok, tok), tok)]
     near[:, pl.ds(128, tok)] = mid
@@ -527,14 +517,15 @@
 
     rs_run(0, sb_a, bufs_a, h_tile, "rs0")
     hid[...] = h_tile(d)
-    z_fwd(DOWN, 1)
     w_slice_wait(GU2)
     z_own(GU2)
     z_fwd(GU0, 1)
     rs_pass(0, sb_a, bufs_a, "rs0")
+    ag_fwd(AO, oa)
     z_fwd(GU1, 1)
     z_fwd(GU2, 1)
-    z_fwd(DOWN, 2)
+    z_fwd(DOWN, 1)
+    z_fwd(GU0, 2)
     rs_wait(0, bufs_a)
 
     @pl.loop(0, tok // step)
@@ -594,36 +585,36 @@
     def out_tile(dd):
         return dot_nn(big[dd, :, pl.ds(0, fs)], wd[...])
 
-    z_fwd(GU0, 2)
     z_fwd(GU1, 2)
     ag_fwd(AZ, za)
-    ag_fwd(AO, oa)
     ag_second(AO, oa)
+    z_fwd(GU0, 3)
     z_fwd(GU2, 2)
-    z_fwd(DOWN, 3)
-    z_finish(DOWN)
     ag_near(AZ, za)
-    z_fwd(GU0, 3)
     z_finish(GU0)
-    ag_far(AZ, za)
-    gate_all(0)
+    for dd in (d, xn, yn):
+        gate_one(0, dd)
+    z_fwd(DOWN, 2)
     z_fwd(GU1, 3)
     z_finish(GU1)
+    ag_far(AZ, za)
+    gate_one(0, dg)
     gate_all(1)
     z_fwd(GU2, 3)
     z_finish(GU2)
     gate_all(2)
     ag_near(AO, oa)
     ag_far(AO, oa)
-    for j in range(3):
-        grad_down(j)
-    g_pair(DOWN)
-
-    def down_off():
-        g_pair_wait(DOWN)
-        g_hop(DOWN, 0)
-
-    rs_run(2, sb_b, bufs_b, out_tile, "rs2", between=down_off)
+    grad_down(0)
+    g_pair(DOWN, (0,))
+    grad_down(2)
+    g_pair(DOWN, (3,))
+    grad_down(1)
+    g_pair(DOWN, (1, 2))
+    g_hop(DOWN, 0)
+    z_fwd(DOWN, 3)
+    z_finish(DOWN)
+    rs_run(2, sb_b, bufs_b, out_tile, "rs2")
     for j in range(3):
         back_all(j)
 
@@ -633,13 +624,11 @@
     g_pair(GU0)
     g_hop(DOWN, 1)
     dh[...] = dz2_tile(d)
-    g_pair_wait(GU0)
     g_hop(GU0, 0)
     rs_pass(1, sb_a, bufs_a, "rs1")
     grad_gu(1)
     g_pair(GU1)
     g_hop(DOWN, 2)
-    g_pair_wait(GU1)
     g_hop(GU1, 0)
     grad_gu(2)
     g_pair(GU2)
@@ -659,7 +648,6 @@
         ra[d, rr, :] = g.astype(BF)
 
     ag_start(AR, ra)
-    g_pair_wait(GU2)
     g_hop(GU2, 0)
     hid[...] = hid[...] + out_tile(d)
     for dd in (d, xn, yn, dg):
@@ -691,16 +679,15 @@
     def _():
         halo_q[...] = jnp.zeros_like(halo_q)
 
-    lines = lax.broadcasted_iota(jnp.int32, (16, ch), 0)
-    tap_rows = jnp.zeros((16, ch), F32)
+    lines = lax.broadcasted_iota(jnp.int32, (rows, ch), 0)
+    tap_rows = jnp.zeros((rows, ch), F32)
     for k in range(3):
         tap_rows = jnp.where(lines == k, jnp.sum(taps[k], axis=0, keepdims=True), tap_rows)
     for q in range(2 * nz):
         first = (q * rows) // 128 * 128
-        s2[q // 2, q % 2] = tap_rows[:, first : first + 128].astype(BF)
-    go[...] = dot_tn(ybuf[...].reshape(4 * tok, ch), ra[...].reshape(4 * tok, wid)).astype(BF)
+        go[pl.ds(q * rows, rows), pl.ds(wid, 128)] = tap_rows[:, first : first + 128].astype(BF)
+    go[:, pl.ds(0, wid)] = dot_tn(ybuf[...].reshape(4 * tok, ch), ra[...].reshape(4 * tok, wid)).astype(BF)
     g_pair(OUT)
-    g_pair(GAIN)
     g_hop(GU2, 1)
     recv(s < 2 * nz - 1, lambda: halo_q, lambda: hr.at[1])
 
@@ -727,26 +714,19 @@
         right = big[:, :, pl.ds(mcol + p * ch, ch)].reshape(4 * tok, ch)
         gw[:, :, :, :, pl.ds(p * ch, ch)] = dot_tn(left, right).astype(BF).reshape(4, nz, 2, rows, ch)
 
-    g_pair_wait(OUT)
     g_hop(OUT, 0)
-    g_pair_wait(GAIN)
-    g_hop(GAIN, 0)
     grad_in(0)
     g_pair(IN_A)
     grad_in(1)
     g_pair(IN_B)
-    g_pair_wait(IN_A)
     g_hop(IN_A, 0)
     grad_in(2)
     g_pair(IN_C)
-    g_pair_wait(IN_B)
     g_hop(IN_B, 0)
     g_hop(GU2, 2)
-    g_pair_wait(IN_C)
     g_hop(IN_C, 0)
     rs_pass(3, sb_a, bufs_a, "rs3")
     g_hop(OUT, 1)
-    g_hop(GAIN, 1)
     rs_wait(2, bufs_b)
 
     @pl.loop(0, tok // step)
@@ -760,18 +740,15 @@
     drain("halo")
     g_hop(IN_A, 1)
     g_hop(OUT, 2)
-    g_hop(GAIN, 2)
-    g_rows(GU0)
     g_hop(IN_B, 1)
     g_hop(IN_A, 2)
-    g_rows(GU1)
+    g_rows(GU0)
     g_hop(IN_C, 1)
     g_hop(IN_B, 2)
+    g_rows(GU1)
     g_last(DOWN, gdown_ref)
     g_hop(IN_C, 2)
     g_rows(GU2)
-    g_rows_wait(GU0)
-    g_rows_wait(GU1)
     rs_wait(3, bufs_a)
 
     @pl.loop(0, tok // step)
@@ -789,10 +766,11 @@
     grads.start()
 
     g_rows(IN_A)
-    g_last(OUT, gout_ref)
-    g_last(GAIN, gsum)
-    gsmall_ref[pl.ds(8, 8), :] = pltpu.roll(gsum[...], lax.rem(128 - lane0, 128), 1)[:8]
-    g_rows_wait(GU2)
+    g_last(OUT, oacc)
+    gout_ref[...] = oacc[:, pl.ds(0, wid)]
+    gsmall_ref[pl.ds(8, 8), :] = pltpu.roll(oacc[0:16, pl.ds(wid, 128)], lax.rem(128 - lane0, 128), 1)[:8]
+    for unit in (GU0, GU1, GU2):
+        g_rows_wait(unit)
     g_rows(IN_B)
 
     def gain_sum(first, n):
@@ -820,18 +798,30 @@
     drain()
 
 
-def move_out(lanes, *refs):
-    n = (len(refs) - 6) // 3
-    small_ref, one_ref, two_ref, taps_ref = refs[n], *refs[2 * n + 1 : 2 * n + 4]
-    outs, held, sems, done = refs[n + 1 : 2 * n + 1], refs[2 * n + 4 : 3 * n + 4], refs[-2], refs[-1]
-    loads = [pltpu.make_async_copy(refs[k], held[k], sems.at[k]) for k in range(n)]
-    stores = [pltpu.make_async_copy(held[k], outs[k], done.at[k]) for k in range(n)]
+def move_out(shape, *refs):
+    lanes, ch, fs, cj, uw = shape
+    out_in, tok_in, tile_in, go_in, gd_in, small, out_ref, tok_ref, in_ref, go_ref, gate_ref, up_ref, gd_ref = refs[:13]
+    one_ref, two_ref, taps_ref, a, b, tile, e, f, gin, gate, up, sems, done = refs[13:]
+    wid = 4 * ch
+    pairs = ((tile_in, tile, None), (out_in, a, out_ref), (tok_in, b, tok_ref), (gd_in, f, gd_ref), (go_in, e, go_ref))
+    loads = [pltpu.make_async_copy(p[0], p[1], sems.at[k]) for k, p in enumerate(pairs)]
     for load in loads:
         load.start()
-    one_ref[...] = small_ref[0:1, 0:lanes]
-    two_ref[...] = small_ref[1:2, 0:lanes]
-    taps_ref[...] = small_ref[8:11, 0:lanes]
-    for load, store in zip(loads, stores):
+    one_ref[...] = small[0:1, 0:lanes]
+    two_ref[...] = small[1:2, 0:lanes]
+    taps_ref[...] = small[8:11, 0:lanes]
+    stores = [pltpu.make_async_copy(p[1], p[2], done.at[k + 1]) for k, p in enumerate(pairs[1:])]
+    loads[0].wait()
+    for k in range(4):
+        for p in range(3):
+            gin[:, pl.ds(p * wid + k * ch, ch)] = tile[k, :, pl.ds(p * ch, ch)].astype(F32)
+            first = (1 + p) * uw
+            gate[:, pl.ds(k * fs + p * cj, cj)] = tile[k, :, pl.ds(first, cj)].astype(F32)
+            up[:, pl.ds(k * fs + p * cj, cj)] = tile[k, :, pl.ds(first + cj, cj)].astype(F32)
+    stores += [pltpu.make_async_copy(v, r, done.at[5 + k]) for k, (v, r) in enumerate(((gin, in_ref), (gate, gate_ref), (up, up_ref)))]
+    for store in stores[4:]:
+        store.start()
+    for load, store in zip(loads[1:], stores):
         load.wait()
         store.start()
     for store in stores:
@@ -855,6 +845,7 @@
     dma = lambda n: pltpu.SemaphoreType.DMA((n,))
     plane = lambda w, t=BF: vm((n_dp, tok, w), t)
     rs_set = [vm((tok, wid), BF)] * 2 + [vm((tok // 2, wid), BF)] * 2
+    came = lambda n: (vm((n, n_dp, rows, 4 * uw), BF), vm((n, drows, wid), BF), vm((n, rows, wid + 128), BF))
     scratch = [
         vm((n_dp, rows, 4 * uw), BF),
         vm((n_dp, nz, 2, rows, 4 * uw), BF),
@@ -870,13 +861,9 @@
         plane(wid), plane(wid),
         *rs_set, *rs_set,
         vm((tok, wid), F32), vm((tok, wid), F32),
-        vm((n_dp, nz, 2, rows, 4 * uw), BF), vm((fs, wid), BF), vm((ch, wid), BF),
-        vm((nz, n_dp, rows, 4 * uw), BF), vm((nz, drows, wid), BF), vm((nz, rows, wid), BF),
-        vm((top, n_dp, rows, 4 * uw), BF), vm((top, drows, wid), BF), vm((top, rows, wid), BF),
-        vm((top, n_dp, rows, 4 * uw), BF), vm((top, drows, wid), BF), vm((top, rows, wid), BF),
-        vm((n_dp, rows, 4 * uw), BF), vm((16, 128), F32), vm((1, tok + 256), jnp.int32), vm((n_dp, 16, tok), BF),
-        vm((nz, 2, 16, 128), BF),
-        vm((nz, 16, 128), BF), vm((top, 16, 128), BF), vm((top, 16, 128), BF),
+        vm((n_dp, nz, 2, rows, 4 * uw), BF), vm((fs, wid), BF), vm((ch, wid + 128), BF),
+        *came(nz), *came(top), *came(top),
+        vm((16, 128), F32), vm((1, tok + 256), jnp.int32), vm((n_dp, 16, tok), BF), vm((rows, wid + 128), F32),
         dma(7 * 13), dma(7 * 2 * nz), dma(12), dma(12), dma(3), dma(3), dma(3), dma(3), dma(2), dma(2),
         dma(24), dma(24), dma(24), dma(24), dma(10 * nz), dma(10 * nz),
         dma(10 * top), dma(10 * top), dma(10 * top), dma(10 * top), dma(21), dma(21), dma(8 * fs // uw + 8),
@@ -887,22 +874,24 @@
         functools.partial(block_kernel, dims),
         out_shape=(
             jax.ShapeDtypeStruct(tokens.shape, BF), jax.ShapeDtypeStruct(tokens.shape, BF),
-            f32(in_weight), f32(out_weight), f32(gate_weight), f32(up_weight), f32(down_weight),
+            jax.ShapeDtypeStruct((n_dp, rows, 4 * uw), BF), f32(out_weight), f32(down_weight),
             jax.ShapeDtypeStruct((16, 128), F32),
         ),
         in_specs=[anywhere] * 2 + [vspec] * 4 + [anywhere, vspec] + [anywhere] * 3,
-        out_specs=(anywhere,) * 2 + (vspec,) * 6,
+        out_specs=(anywhere,) * 2 + (vspec,) * 4,
         scratch_shapes=scratch,
         compiler_params=pltpu.CompilerParams(collective_id=0, has_side_effects=True, vmem_limit_bytes=64 * 1024 * 1024),
     )(tokens, cotangent, segments, norm_one[None], norm_two[None], kernel, in_weight, out_weight, gate_weight, up_weight, down_weight)
-    final = [jax.ShapeDtypeStruct(v.shape, v.dtype) for v in res[:7]]
+    final = [jax.ShapeDtypeStruct(v.shape, v.dtype) for v in res[:2]]
+    final += [f32(w) for w in (in_weight, out_weight, gate_weight, up_weight, down_weight)]
     final += [jax.ShapeDtypeStruct((k, lanes), F32) for k in (1, 1, 3)]
     moved = pl.pallas_call(
-        functools.partial(move_out, lanes),
+        functools.partial(move_out, (lanes, ch, fs, cj, uw)),
         out_shape=tuple(final),
-        in_specs=[anywhere] * 7 + [vspec],
+        in_specs=[anywhere] * 5 + [vspec],
         out_specs=(anywhere,) * 7 + (vspec,) * 3,
-        scratch_shapes=[vm(v.shape, v.dtype) for v in res[:7]] + [dma(7), dma(7)],
+        scratch_shapes=[vm(v.shape, v.dtype) for v in res[:5]]
+        + [vm(w.shape, F32) for w in (in_weight, gate_weight, up_weight)] + [dma(5), dma(8)],
     )(*res)
     return (*moved[:7], moved[7][0], moved[8][0], moved[9])
 

time: 195 us -> 189 us (0.969)
  Pallas kernels: 193 us -> 188 us
    pallas_call x1, Pallas kernels: 189 us -> 184 us  [fast_body(): pl.pallas_call(functools.partial(block_kernel, dims), out_shape=(jax.Shap...]
where the time goes in v4:
time: 189 us
  Pallas kernels  188 us (99%)
    pallas_call x1, Pallas kernels, fast_body(): pl.pallas_call(functools.partial(block_kernel, dims), out_shape=(jax.Shap...  184 us
    pallas_call x1, Pallas kernels, fast_body(): pl.pallas_call(functools.partial(move_out, (lanes, ch, fs, cj, uw)), out_...  4.27 us

profile of v4, /device:TPU:0, one launch (start us, length us, event | category | flops | bytes accessed | tf_op | source)
XLA Modules:
  0.0 188.7 jit_solution(9680973567503223317)
XLA Ops:
  0.6 183.6 %shard_map.186 = (bf16[1,256,1024]{2,1,0:T(8,128)(2,1)}, bf16[1,256,1024]{2,1,0:T(8,128)(2,1)}, bf16[4,32,3072]{2,1,0:T(8,128)(2,1)}, f32[32,1024]{1,0:T(8,128)}...) custom-call(bf16[1,256,1024]{2,1,0:T(8,128)(2,1)} %x_ref.1, bf16[1,256,1024]{2,1,0:T(8,128)(2,1)} %do_ref.1, s32[1,2048]{1,0:T(1,128)} %seg_ref.1, ...), custom_call_target="tpu_custom_call" | custom-call | tf_op jit(solution)/shard_map/pallas_call | solution.py:873
  184.3 4.3 %shard_map.187 = (bf16[1,256,1024]{2,1,0:T(8,128)(2,1)}, bf16[1,256,1024]{2,1,0:T(8,128)(2,1)}, f32[32,3072]{1,0:T(8,128)}, f32[32,1024]{1,0:T(8,128)}, f32[32,4...) custom-call(bf16[1,256,1024]{2,1,0:T(8,128)(2,1)} %get-tuple-element, ...), custom_call_target="tpu_custom_call" | custom-call | tf_op jit(solution)/shard_map/pallas_call | solution.py:888

commit v5 on v4

--- a/solution.py
+++ b/solution.py
@@ -45,7 +45,7 @@
     stage, wall, wo, wd, gb, gv, xa, ma, za, oa, ra, big, mbuf, pbuf, ybuf, halo_p, halo_q,
     sb_a, sb_b, rx_a, ry_a, fx_a, fy_a, rx_b, ry_b, fx_b, fy_b, hid, dh,
     gw, gd, go, dd_g, dd_d, dd_o, up_g, up_d, up_o, dn_g, dn_d, dn_o,
-    gsum, near, fm, oacc,
+    gsum, near, fm, oacc, fbuf,
     zs, zr, ws, wr, gs, gr, ms, mr, hs, hr, ags, agr, rss, rsr, ds_, dr_, us, ur, vs, vr, qs, qr, ins,
 ):
     tok, wid, nz, rows, ch, fs, cj, uw, drows = dims
@@ -204,18 +204,22 @@
     def rs_send(r, tag, src, dst, k, tgt):
         send(tag, True, src, dst, lambda: rss.at[r * 6 + k], lambda: rsr.at[r * 6 + k], tgt)
 
-    def rs_run(r, sb, bufs, tile, tag, first=0, between=None):
-        wide = pl.ds(first, wid)
-        rx, ry, fx, fy = bufs
-        sb[dg, :, wide] = tile(dg).astype(BF)
-        rs_send(r, tag, lambda: sb.at[dg, lo, wide], lambda: fx, 0, to_x)
-        rs_send(r, tag, lambda: sb.at[dg, hi, wide], lambda: fy, 1, to_y)
-        if between is not None:
-            between()
-        sb[xn, :, wide] = tile(xn).astype(BF)
-        rs_send(r, tag, lambda: sb.at[xn, lo, wide], lambda: rx.at[lo, :], 2, to_x)
-        sb[yn, :, wide] = tile(yn).astype(BF)
-        rs_send(r, tag, lambda: sb.at[yn, hi, wide], lambda: ry.at[hi, :], 3, to_y)
+    def rs_far(r, sb, bufs, tile, tag):
+        sb[dg] = tile(dg).astype(BF)
+        rs_send(r, tag, lambda: sb.at[dg, lo, :], lambda: bufs[2], 0, to_x)
+        rs_send(r, tag, lambda: sb.at[dg, hi, :], lambda: bufs[3], 1, to_y)
+
+    def rs_direct(r, sb, bufs, tile, tag):
+        if tile is not None:
+            sb[xn] = tile(xn).astype(BF)
+        rs_send(r, tag, lambda: sb.at[xn, lo, :], lambda: bufs[0].at[lo, :], 2, to_x)
+        if tile is not None:
+            sb[yn] = tile(yn).astype(BF)
+        rs_send(r, tag, lambda: sb.at[yn, hi, :], lambda: bufs[1].at[hi, :], 3, to_y)
+
+    def rs_run(r, sb, bufs, tile, tag):
+        rs_far(r, sb, bufs, tile, tag)
+        rs_direct(r, sb, bufs, tile, tag)
 
     def rs_pass(r, sb, bufs, tag, first=0):
         wide = pl.ds(first, wid)
@@ -278,12 +282,12 @@
             pl.when(pred)(lambda: g_add(mine(), (mine(), pair())))
         send("g", pred, mine, there, ssem, rsem, tgt)
 
-    def g_hop(unit, h):
-        for zt in range(top, h, -1):
+    def g_hop(unit, h, up=True, down=(0, nz)):
+        for zt in range(top, h if up else top, -1):
             came = lambda zt=zt: g_in(unit, t_up, zt - 1)
             sem = lambda zt=zt: ur.at[unit * top + zt - 1]
             g_step(unit, z == h, zt, h > 0, came, sem, lambda zt=zt: us.at[unit * top + zt - 1], sem, came, to_up)
-        for zt in range(top - h):
+        for zt in range(down[0], min(down[1], top - h)):
             came = lambda zt=zt: g_in(unit, t_dn, zt)
             sem = lambda zt=zt: vr.at[unit * top + zt]
             g_step(unit, z == top - h, zt, h > 0, came, sem, lambda zt=zt: vs.at[unit * top + zt], sem, came, to_dn)
@@ -305,7 +309,7 @@
 
     def g_rows(unit):
         first, n = span(unit)
-        facc = mbuf.at[:, pl.ds(0, rows), pl.ds(0, n)]
+        facc = fbuf.at[:, :, pl.ds(0, n)]
         g_last(unit, facc)
         u = SLOT[unit]
         for k in range(4):
@@ -354,10 +358,10 @@
     for i in range(4):
         first_in(i).start()
     x_in.start()
+    for i in range(2):
+        down_in(i).start()
     for i in range(2 * count):
         wide_in(i).start()
-    for i in range(2):
-        down_in(i).start()
     do_in.start()
     for i in range(4):
         first_in(i).wait()
@@ -373,12 +377,17 @@
     gsum[2:5, 0:lanes] = taps_ref[...]
     gb[d, z, c] = pltpu.roll(gsum[...], lane0, 1).astype(BF)
     wo[pl.ds(pl.multiple_of(s * rows, rows), rows), :] = wout_ref[...].astype(BF)
+    for i in range(2):
+        down_in(i).wait()
+    wd[pl.ds(pl.multiple_of(s * drows, drows), drows), pl.ds(0, uw)] = mbuf[2, pl.ds(0, drows), :].astype(BF)
+    wd[pl.ds(pl.multiple_of(s * drows, drows), drows), pl.ds(uw, wid - uw)] = mbuf[3, pl.ds(0, drows), pl.ds(0, wid - uw)].astype(BF)
     enter()
     for k, (idx, tgt) in enumerate(peers):
         send("w", True, lambda: gb.at[d, z, c], lambda: gb.at[d, z, c], lambda k=k: gs.at[k], lambda k=k: gr.at[k], tgt)
     w_slice(IN)
     x_in.wait()
     ag_start(AX, xa)
+    z_own(DOWN)
     z_own(OUT)
     mid = seg_ref[:, pl.ds(pl.multiple_of(s * tok, tok), tok)]
     near[:, pl.ds(128, tok)] = mid
@@ -411,10 +420,6 @@
         for j in range(3):
             stage[k, :, pl.ds((1 + j) * uw, cj)] = wide_read(0, k * fs + j * cj, cj).astype(BF)
             stage[k, :, pl.ds((1 + j) * uw + cj, cj)] = wide_read(1, k * fs + j * cj, cj).astype(BF)
-    for i in range(2):
-        down_in(i).wait()
-    wd[pl.ds(pl.multiple_of(s * drows, drows), drows), pl.ds(0, uw)] = mbuf[2, pl.ds(0, drows), :].astype(BF)
-    wd[pl.ds(pl.multiple_of(s * drows, drows), drows), pl.ds(uw, wid - uw)] = mbuf[3, pl.ds(0, drows), pl.ds(0, wid - uw)].astype(BF)
     z_fwd(OUT, 1)
     z_fwd(GAIN, 1)
     ag_fwd(AX, xa)
@@ -439,7 +444,7 @@
             tot = piece if tot is None else tot + piece
         gv[:, pl.ds(g * 128, 128)] = tot
 
-    step = 32
+    step = 64
 
     def norm_rows(xv):
         return lax.rsqrt(jnp.mean(xv * xv, axis=1, keepdims=True) + epsilon)
@@ -460,7 +465,6 @@
     make_z1(yn)
     z_fwd(IN, 2)
     z_fwd(OUT, 3)
-    z_own(DOWN)
     ag_far(AX, xa)
     make_z1(dg)
     w_slice_wait(GU0)
@@ -528,14 +532,19 @@
     z_fwd(GU0, 2)
     rs_wait(0, bufs_a)
 
-    @pl.loop(0, tok // step)
-    def _(i):
-        rr = pl.ds(pl.multiple_of(i * step, step), step)
-        h = xa[d, rr, :].astype(F32) + hid[rr, :] + rx_a[rr, :].astype(F32) + ry_a[rr, :].astype(F32)
-        hid[rr, :] = h
-        za[d, rr, :] = (h * norm_rows(h) * gv[1:2, :]).astype(BF)
-
-    ag_start(AZ, za)
+    def hidden_rows(first):
+        @pl.loop(0, half // step)
+        def _(i):
+            rr = pl.ds(pl.multiple_of(first + i * step, step), step)
+            h = xa[d, rr, :].astype(F32) + hid[rr, :] + rx_a[rr, :].astype(F32) + ry_a[rr, :].astype(F32)
+            hid[rr, :] = h
+            za[d, rr, :] = (h * norm_rows(h) * gv[1:2, :]).astype(BF)
+
+    hidden_rows(half)
+    ag_send(AZ, za, d, hi, 0, 1, to_x)
+    hidden_rows(0)
+    ag_send(AZ, za, d, lo, 1, 2, to_y)
+    ag_second(AZ, za)
 
     def acol(j):
         return pl.ds(j * cj, cj)
@@ -603,6 +612,10 @@
     z_fwd(GU2, 3)
     z_finish(GU2)
     gate_all(2)
+    z_fwd(DOWN, 3)
+    z_finish(DOWN)
+
+    rs_far(2, sb_b, bufs_b, out_tile, "rs2")
     ag_near(AO, oa)
     ag_far(AO, oa)
     grad_down(0)
@@ -612,9 +625,7 @@
     grad_down(1)
     g_pair(DOWN, (1, 2))
     g_hop(DOWN, 0)
-    z_fwd(DOWN, 3)
-    z_finish(DOWN)
-    rs_run(2, sb_b, bufs_b, out_tile, "rs2")
+    rs_direct(2, sb_b, bufs_b, out_tile, "rs2")
     for j in range(3):
         back_all(j)
 
@@ -632,12 +643,10 @@
     g_hop(GU1, 0)
     grad_gu(2)
     g_pair(GU2)
-    g_hop(GU0, 1)
     rs_wait(1, bufs_a)
 
-    @pl.loop(0, tok // step)
-    def _(i):
-        rr = pl.ds(pl.multiple_of(i * step, step), step)
+    def back_two(first, i):
+        rr = pl.ds(pl.multiple_of(first + i * step, step), step)
         dz = dh[rr, :] + rx_a[rr, :].astype(F32) + ry_a[rr, :].astype(F32)
         h = hid[rr, :]
         inv = norm_rows(h)
@@ -647,18 +656,21 @@
         dh[rr, :] = g
         ra[d, rr, :] = g.astype(BF)
 
-    ag_start(AR, ra)
-    g_hop(GU2, 0)
+    pl.loop(0, half // step)(functools.partial(back_two, half))
+    ag_send(AR, ra, d, hi, 0, 1, to_x)
+    pl.loop(0, half // step)(functools.partial(back_two, 0))
+    ag_send(AR, ra, d, lo, 1, 2, to_y)
+    ag_second(AR, ra)
+    g_hop(GU2, 0, down=(0, 1))
+    g_hop(GU0, 1)
     hid[...] = hid[...] + out_tile(d)
     for dd in (d, xn, yn, dg):
         make_z1(dd)
+    ag_fwd(AR, ra)
+    rs_pass(2, sb_b, bufs_b, "rs2")
     g_hop(GU0, 2)
-    ag_fwd(AR, ra)
-    g_hop(GU1, 1)
-    rs_pass(2, sb_b, bufs_b, "rs2")
+    g_last(DOWN, gdown_ref)
     ag_near(AR, ra)
-    g_hop(GU1, 2)
-    ag_far(AR, ra)
 
     mcol = fs
     zero_tap = jnp.zeros((8, ch), F32)
@@ -671,9 +683,16 @@
         big[dd, :, pl.ds(mcol + ch, ch)] = (dy * convolve(cur, one, two)).astype(BF)
         return tuple(a + (q * v).reshape(tok // 8, 8, ch).sum(axis=0) for a, v in zip(acc, (cur, one, two)))
 
-    taps = lax.fori_loop(0, 4, back_conv, (zero_tap, zero_tap, zero_tap))
+    taps = (zero_tap, zero_tap, zero_tap)
+    for dd in (d, xn, yn):
+        taps = back_conv(dd, taps)
+    g_hop(GU1, 1)
+    ag_far(AR, ra)
+    taps = back_conv(dg, taps)
     head = 8
     send("halo", s > 0, lambda: mbuf.at[:, pl.ds(0, head), pl.ds(ch, ch)], lambda: halo_q, lambda: hs.at[1], lambda: hr.at[1], to_prev)
+
+    g_hop(GU2, 0, up=False, down=(1, nz))
 
     @pl.when(s == 2 * nz - 1)
     def _():
@@ -688,7 +707,7 @@
         go[pl.ds(q * rows, rows), pl.ds(wid, 128)] = tap_rows[:, first : first + 128].astype(BF)
     go[:, pl.ds(0, wid)] = dot_tn(ybuf[...].reshape(4 * tok, ch), ra[...].reshape(4 * tok, wid)).astype(BF)
     g_pair(OUT)
-    g_hop(GU2, 1)
+    g_hop(GU1, 2)
     recv(s < 2 * nz - 1, lambda: halo_q, lambda: hr.at[1])
 
     @pl.loop(0, 4)
@@ -707,26 +726,28 @@
     def dz1_tile(dd):
         return dot_nt(big[dd, :, pl.ds(mcol, uw)], unit_w(0, uw))
 
-    rs_run(3, sb_a, bufs_a, dz1_tile, "rs3")
-
     def grad_in(p):
         left = big[:, :, zcol].reshape(4 * tok, wid)
         right = big[:, :, pl.ds(mcol + p * ch, ch)].reshape(4 * tok, ch)
         gw[:, :, :, :, pl.ds(p * ch, ch)] = dot_tn(left, right).astype(BF).reshape(4, nz, 2, rows, ch)
 
-    g_hop(OUT, 0)
     grad_in(0)
     g_pair(IN_A)
+    rs_run(3, sb_a, bufs_a, dz1_tile, "rs3")
+    g_hop(IN_A, 0)
     grad_in(1)
     g_pair(IN_B)
-    g_hop(IN_A, 0)
     grad_in(2)
     g_pair(IN_C)
     g_hop(IN_B, 0)
+    g_hop(IN_C, 0)
+    g_hop(OUT, 0)
+    g_hop(GU2, 1)
+    rs_pass(3, sb_a, bufs_a, "rs3")
+    g_rows(GU0)
+    g_rows(GU1)
     g_hop(GU2, 2)
-    g_hop(IN_C, 0)
-    rs_pass(3, sb_a, bufs_a, "rs3")
-    g_hop(OUT, 1)
+    g_hop(IN_A, 1)
     rs_wait(2, bufs_b)
 
     @pl.loop(0, tok // step)
@@ -737,18 +758,15 @@
     result = pltpu.make_async_copy(sb_b.at[d], out_ref.at[0], ins.at[2 * count])
     result.start()
     hid[...] = dz1_tile(d)
-    drain("halo")
-    g_hop(IN_A, 1)
-    g_hop(OUT, 2)
+    g_hop(IN_A, 2)
     g_hop(IN_B, 1)
-    g_hop(IN_A, 2)
-    g_rows(GU0)
+    g_hop(IN_B, 2)
+    g_rows(GU2)
+    g_rows(IN_A)
     g_hop(IN_C, 1)
-    g_hop(IN_B, 2)
-    g_rows(GU1)
-    g_last(DOWN, gdown_ref)
+    g_hop(OUT, 1)
+    g_rows(IN_B)
     g_hop(IN_C, 2)
-    g_rows(GU2)
     rs_wait(3, bufs_a)
 
     @pl.loop(0, tok // step)
@@ -765,13 +783,9 @@
     grads = pltpu.make_async_copy(sb_a.at[d], gtok_ref.at[0], ins.at[2 * count + 1])
     grads.start()
 
-    g_rows(IN_A)
-    g_last(OUT, oacc)
-    gout_ref[...] = oacc[:, pl.ds(0, wid)]
-    gsmall_ref[pl.ds(8, 8), :] = pltpu.roll(oacc[0:16, pl.ds(wid, 128)], lax.rem(128 - lane0, 128), 1)[:8]
+    g_hop(OUT, 2)
     for unit in (GU0, GU1, GU2):
         g_rows_wait(unit)
-    g_rows(IN_B)
 
     def gain_sum(first, n):
         acc = jnp.zeros((rows, 128), F32)
@@ -788,8 +802,11 @@
         )
         gsmall_ref[k : k + 1, 0:lanes] = total[0:1] / gain[...].astype(BF).astype(F32)
 
+    g_rows(IN_C)
     gain_out(1, uw, 3 * uw, n2_ref)
-    g_rows(IN_C)
+    g_last(OUT, oacc)
+    gout_ref[...] = oacc[:, pl.ds(0, wid)]
+    gsmall_ref[pl.ds(8, 8), :] = pltpu.roll(oacc[0:16, pl.ds(wid, 128)], lax.rem(128 - lane0, 128), 1)[:8]
     for unit in PIECES:
         g_rows_wait(unit)
     gain_out(0, 0, uw, n1_ref)
@@ -863,7 +880,7 @@
         vm((tok, wid), F32), vm((tok, wid), F32),
         vm((n_dp, nz, 2, rows, 4 * uw), BF), vm((fs, wid), BF), vm((ch, wid + 128), BF),
         *came(nz), *came(top), *came(top),
-        vm((16, 128), F32), vm((1, tok + 256), jnp.int32), vm((n_dp, 16, tok), BF), vm((rows, wid + 128), F32),
+        vm((16, 128), F32), vm((1, tok + 256), jnp.int32), vm((n_dp, 16, tok), BF), vm((rows, wid + 128), F32), vm((n_dp, rows, uw), F32),
         dma(7 * 13), dma(7 * 2 * nz), dma(12), dma(12), dma(3), dma(3), dma(3), dma(3), dma(2), dma(2),
         dma(24), dma(24), dma(24), dma(24), dma(10 * nz), dma(10 * nz),
         dma(10 * top), dma(10 * top), dma(10 * top), dma(10 * top), dma(21), dma(21), dma(8 * fs // uw + 8),

time: 189 us -> 185 us (0.979)
  Pallas kernels: 188 us -> 184 us
    pallas_call x1, Pallas kernels: 184 us -> 180 us  [fast_body(): pl.pallas_call(functools.partial(block_kernel, dims), out_shape=(jax.Shap...]
where the time goes in v5:
time: 185 us
  Pallas kernels  184 us (99%)
    pallas_call x1, Pallas kernels, fast_body(): pl.pallas_call(functools.partial(block_kernel, dims), out_shape=(jax.Shap...  180 us
    pallas_call x1, Pallas kernels, fast_body(): pl.pallas_call(functools.partial(move_out, (lanes, ch, fs, cj, uw)), out_...  4.27 us

profile of v5, /device:TPU:0, one launch (start us, length us, event | category | flops | bytes accessed | tf_op | source)
XLA Modules:
  0.0 185.2 jit_solution(11343982316230087954)
XLA Ops:
  0.6 180.1 %shard_map.186 = (bf16[1,256,1024]{2,1,0:T(8,128)(2,1)}, bf16[1,256,1024]{2,1,0:T(8,128)(2,1)}, bf16[4,32,3072]{2,1,0:T(8,128)(2,1)}, f32[32,1024]{1,0:T(8,128)}...) custom-call(bf16[1,256,1024]{2,1,0:T(8,128)(2,1)} %x_ref.1, bf16[1,256,1024]{2,1,0:T(8,128)(2,1)} %do_ref.1, s32[1,2048]{1,0:T(1,128)} %seg_ref.1, ...), custom_call_target="tpu_custom_call" | custom-call | tf_op jit(solution)/shard_map/pallas_call | solution.py:890
  180.8 4.3 %shard_map.187 = (bf16[1,256,1024]{2,1,0:T(8,128)(2,1)}, bf16[1,256,1024]{2,1,0:T(8,128)(2,1)}, f32[32,3072]{1,0:T(8,128)}, f32[32,1024]{1,0:T(8,128)}, f32[32,4...) custom-call(bf16[1,256,1024]{2,1,0:T(8,128)(2,1)} %get-tuple-element, ...), custom_call_target="tpu_custom_call" | custom-call | tf_op jit(solution)/shard_map/pallas_call | solution.py:905

commit v6 on v5

--- a/solution.py
+++ b/solution.py
@@ -40,13 +40,13 @@
 
 def block_kernel(
     dims,
-    x_ref, do_ref, seg_ref, n1_ref, n2_ref, taps_ref, win_ref, wout_ref, wg_ref, wu_ref, wdn_ref,
+    x_ref, do_ref, seg_in, n1_in, n2_in, taps_in, win_ref, wout_in, wg_ref, wu_ref, wdn_ref,
     out_ref, gtok_ref, rbuf, gout_ref, gdown_ref, gsmall_ref,
     stage, wall, wo, wd, gb, gv, xa, ma, za, oa, ra, big, mbuf, pbuf, ybuf, halo_p, halo_q,
     sb_a, sb_b, rx_a, ry_a, fx_a, fy_a, rx_b, ry_b, fx_b, fy_b, hid, dh,
     gw, gd, go, dd_g, dd_d, dd_o, up_g, up_d, up_o, dn_g, dn_d, dn_o,
-    gsum, near, fm, oacc, fbuf,
-    zs, zr, ws, wr, gs, gr, ms, mr, hs, hr, ags, agr, rss, rsr, ds_, dr_, us, ur, vs, vr, qs, qr, ins,
+    gsum, near, fm, oacc, fbuf, seg_ref, n1_ref, n2_ref, taps_ref, wout_ref,
+    zs, zr, ws, wr, gs, gr, ms, mr, hs, hr, ags, agr, rss, rsr, ds_, dr_, us, ur, vs, vr, qs, qr, ins, sms,
 ):
     tok, wid, nz, rows, ch, fs, cj, uw, drows = dims
     half = tok // 2
@@ -88,6 +88,13 @@
                 keep.append(item)
         pending[:] = keep
 
+    small_in = [
+        pltpu.make_async_copy(a, b, sms.at[k])
+        for k, (a, b) in enumerate(((n1_in, n1_ref), (n2_in, n2_ref), (taps_in, taps_ref), (wout_in, wout_ref), (seg_in, seg_ref)))
+    ]
+    for move in small_in:
+        move.start()
+
     barrier = pltpu.get_barrier_semaphore()
 
     def greet(tgt):
@@ -261,7 +268,7 @@
     def g_pair(unit, which=range(nz)):
         for zz in which:
             send(
-                "g", True, lambda zz=zz: g_own(unit, zz, oc), lambda zz=zz: g_in(unit, t_dd, zz),
+                ("g", unit), True, lambda zz=zz: g_own(unit, zz, oc), lambda zz=zz: g_in(unit, t_dd, zz),
                 lambda zz=zz: ds_.at[unit * nz + zz], lambda zz=zz: dr_.at[unit * nz + zz], to_sib,
             )
 
@@ -280,7 +287,7 @@
             pl.when(pred)(lambda: g_add(mine(), (mine(), pair(), came())))
         else:
             pl.when(pred)(lambda: g_add(mine(), (mine(), pair())))
-        send("g", pred, mine, there, ssem, rsem, tgt)
+        send(("g", unit), pred, mine, there, ssem, rsem, tgt)
 
     def g_hop(unit, h, up=True, down=(0, nz)):
         for zt in range(top, h if up else top, -1):
@@ -371,6 +378,8 @@
             stage[k, :, pl.ds(p * ch, ch)] = mbuf[2 + b // 2, pl.ds(tok - rows * (1 + b % 2), rows), pl.ds(first, ch)].astype(BF)
     lanes = taps_ref.shape[1]
     lane0 = lax.rem(s * rows, 128)
+    for move in small_in:
+        move.wait()
     gsum[...] = jnp.zeros_like(gsum)
     gsum[0:1, 0:lanes] = n1_ref[...]
     gsum[1:2, 0:lanes] = n2_ref[...]
@@ -670,6 +679,8 @@
     rs_pass(2, sb_b, bufs_b, "rs2")
     g_hop(GU0, 2)
     g_last(DOWN, gdown_ref)
+    drain("w")
+    drain("stage")
     ag_near(AR, ra)
 
     mcol = fs
@@ -748,6 +759,9 @@
     g_rows(GU1)
     g_hop(GU2, 2)
     g_hop(IN_A, 1)
+    drain("ag")
+    for unit in (DOWN, GU0):
+        drain(("g", unit))
     rs_wait(2, bufs_b)
 
     @pl.loop(0, tok // step)
@@ -766,6 +780,10 @@
     g_hop(IN_C, 1)
     g_hop(OUT, 1)
     g_rows(IN_B)
+    drain("halo")
+    drain("rs2")
+    for unit in (GU1, GU2):
+        drain(("g", unit))
     g_hop(IN_C, 2)
     rs_wait(3, bufs_a)
 
@@ -820,27 +838,37 @@
     out_in, tok_in, tile_in, go_in, gd_in, small, out_ref, tok_ref, in_ref, go_ref, gate_ref, up_ref, gd_ref = refs[:13]
     one_ref, two_ref, taps_ref, a, b, tile, e, f, gin, gate, up, sems, done = refs[13:]
     wid = 4 * ch
-    pairs = ((tile_in, tile, None), (out_in, a, out_ref), (tok_in, b, tok_ref), (gd_in, f, gd_ref), (go_in, e, go_ref))
-    loads = [pltpu.make_async_copy(p[0], p[1], sems.at[k]) for k, p in enumerate(pairs)]
+    tile_load = pltpu.make_async_copy(tile_in, tile, sems.at[0])
+    tile_load.start()
+    pairs = ((gd_in, f, gd_ref), (out_in, a, out_ref), (tok_in, b, tok_ref), (go_in, e, go_ref))
+    loads = [pltpu.make_async_copy(p[0], p[1], sems.at[k + 1]) for k, p in enumerate(pairs)]
+    stores = [pltpu.make_async_copy(p[1], p[2], done.at[k]) for k, p in enumerate(pairs)]
     for load in loads:
         load.start()
     one_ref[...] = small[0:1, 0:lanes]
     two_ref[...] = small[1:2, 0:lanes]
     taps_ref[...] = small[8:11, 0:lanes]
-    stores = [pltpu.make_async_copy(p[1], p[2], done.at[k + 1]) for k, p in enumerate(pairs[1:])]
-    loads[0].wait()
+    tile_load.wait()
+    for k in range(4):
+        for p in range(3):
+            first = (1 + p) * uw
+            gate[:, pl.ds(k * fs + p * cj, cj)] = tile[k, :, pl.ds(first, cj)].astype(F32)
+    stores.append(pltpu.make_async_copy(gate, gate_ref, done.at[4]))
+    stores[-1].start()
+    for load, store in zip(loads, stores):
+        load.wait()
+        store.start()
+    for k in range(4):
+        for p in range(3):
+            first = (1 + p) * uw
+            up[:, pl.ds(k * fs + p * cj, cj)] = tile[k, :, pl.ds(first + cj, cj)].astype(F32)
+    stores.append(pltpu.make_async_copy(up, up_ref, done.at[5]))
+    stores[-1].start()
     for k in range(4):
         for p in range(3):
             gin[:, pl.ds(p * wid + k * ch, ch)] = tile[k, :, pl.ds(p * ch, ch)].astype(F32)
-            first = (1 + p) * uw
-            gate[:, pl.ds(k * fs + p * cj, cj)] = tile[k, :, pl.ds(first, cj)].astype(F32)
-            up[:, pl.ds(k * fs + p * cj, cj)] = tile[k, :, pl.ds(first + cj, cj)].astype(F32)
-    stores += [pltpu.make_async_copy(v, r, done.at[5 + k]) for k, (v, r) in enumerate(((gin, in_ref), (gate, gate_ref), (up, up_ref)))]
-    for store in stores[4:]:
-        store.start()
-    for load, store in zip(loads[1:], stores):
-        load.wait()
-        store.start()
+    stores.append(pltpu.make_async_copy(gin, in_ref, done.at[6]))
+    stores[-1].start()
     for store in stores:
         store.wait()
 
@@ -881,9 +909,10 @@
         vm((n_dp, nz, 2, rows, 4 * uw), BF), vm((fs, wid), BF), vm((ch, wid + 128), BF),
         *came(nz), *came(top), *came(top),
         vm((16, 128), F32), vm((1, tok + 256), jnp.int32), vm((n_dp, 16, tok), BF), vm((rows, wid + 128), F32), vm((n_dp, rows, uw), F32),
+        vm(segments.shape, jnp.int32), vm((1, lanes), F32), vm((1, lanes), F32), vm(kernel.shape, F32), vm(out_weight.shape, F32),
         dma(7 * 13), dma(7 * 2 * nz), dma(12), dma(12), dma(3), dma(3), dma(3), dma(3), dma(2), dma(2),
         dma(24), dma(24), dma(24), dma(24), dma(10 * nz), dma(10 * nz),
-        dma(10 * top), dma(10 * top), dma(10 * top), dma(10 * top), dma(21), dma(21), dma(8 * fs // uw + 8),
+        dma(10 * top), dma(10 * top), dma(10 * top), dma(10 * top), dma(21), dma(21), dma(8 * fs // uw + 8), dma(5),
     ]
     f32 = lambda a: jax.ShapeDtypeStruct(a.shape, F32)
     vspec, anywhere = pl.BlockSpec(memory_space=vm), pl.BlockSpec(memory_space=pl.ANY)
@@ -894,7 +923,7 @@
             jax.ShapeDtypeStruct((n_dp, rows, 4 * uw), BF), f32(out_weight), f32(down_weight),
             jax.ShapeDtypeStruct((16, 128), F32),
         ),
-        in_specs=[anywhere] * 2 + [vspec] * 4 + [anywhere, vspec] + [anywhere] * 3,
+        in_specs=[anywhere] * 11,
         out_specs=(anywhere,) * 2 + (vspec,) * 4,
         scratch_shapes=scratch,
         compiler_params=pltpu.CompilerParams(collective_id=0, has_side_effects=True, vmem_limit_bytes=64 * 1024 * 1024),
@@ -908,7 +937,7 @@
         in_specs=[anywhere] * 5 + [vspec],
         out_specs=(anywhere,) * 7 + (vspec,) * 3,
         scratch_shapes=[vm(v.shape, v.dtype) for v in res[:5]]
-        + [vm(w.shape, F32) for w in (in_weight, gate_weight, up_weight)] + [dma(5), dma(8)],
+        + [vm(w.shape, F32) for w in (in_weight, gate_weight, up_weight)] + [dma(5), dma(7)],
     )(*res)
     return (*moved[:7], moved[7][0], moved[8][0], moved[9])
 

time: 185 us -> 184 us (level)
  no operation moved by 1% of the time
where the time goes in v6:
time: 184 us
  Pallas kernels  183 us (99%)
    pallas_call x1, Pallas kernels, fast_body(): pl.pallas_call(functools.partial(block_kernel, dims), out_shape=(jax.Shap...  179 us
    pallas_call x1, Pallas kernels, fast_body(): pl.pallas_call(functools.partial(move_out, (lanes, ch, fs, cj, uw)), out_...  4.28 us

profile of v6, /device:TPU:0, one launch (start us, length us, event | category | flops | bytes accessed | tf_op | source)
XLA Modules:
  0.0 184.0 jit_solution(1489783942301883819)
XLA Ops:
  0.6 178.9 %shard_map.186 = (bf16[1,256,1024]{2,1,0:T(8,128)(2,1)}, bf16[1,256,1024]{2,1,0:T(8,128)(2,1)}, bf16[4,32,3072]{2,1,0:T(8,128)(2,1)}, f32[32,1024]{1,0:T(8,128)}...) custom-call(bf16[1,256,1024]{2,1,0:T(8,128)(2,1)} %x_ref.1, bf16[1,256,1024]{2,1,0:T(8,128)(2,1)} %do_ref.1, s32[1,2048]{1,0:T(1,128)} %seg_in.1, ...), custom_call_target="tpu_custom_call" | custom-call | tf_op jit(solution)/shard_map/pallas_call | solution.py:919
  179.6 4.3 %shard_map.187 = (bf16[1,256,1024]{2,1,0:T(8,128)(2,1)}, bf16[1,256,1024]{2,1,0:T(8,128)(2,1)}, f32[32,3072]{1,0:T(8,128)}, f32[32,1024]{1,0:T(8,128)}, f32[32,4...) custom-call(bf16[1,256,1024]{2,1,0:T(8,128)(2,1)} %get-tuple-element, ...), custom_call_target="tpu_custom_call" | custom-call | tf_op jit(solution)/shard_map/pallas_call | solution.py:934

commit v7 on v6

--- a/solution.py
+++ b/solution.py
@@ -453,13 +453,13 @@
             tot = piece if tot is None else tot + piece
         gv[:, pl.ds(g * 128, 128)] = tot
 
-    step = 64
+    step = 128
 
     def norm_rows(xv):
         return lax.rsqrt(jnp.mean(xv * xv, axis=1, keepdims=True) + epsilon)
 
     zcol = pl.ds(0, wid)
-    zstep = 64
+    zstep = 128
 
     def make_z1(dd):
         @pl.loop(0, tok // zstep)

time: 184 us -> 184 us (level)
  no operation moved by 1% of the time
where the time goes in v7:
time: 184 us
  Pallas kernels  183 us (99%)
    pallas_call x1, Pallas kernels, fast_body(): pl.pallas_call(functools.partial(block_kernel, dims), out_shape=(jax.Shap...  179 us
    pallas_call x1, Pallas kernels, fast_body(): pl.pallas_call(functools.partial(move_out, (lanes, ch, fs, cj, uw)), out_...  4.28 us

profile of v7, /device:TPU:0, one launch (start us, length us, event | category | flops | bytes accessed | tf_op | source)
XLA Modules:
  0.0 183.7 jit_solution(11020710808166603426)
XLA Ops:
  0.6 178.6 %shard_map.186 = (bf16[1,256,1024]{2,1,0:T(8,128)(2,1)}, bf16[1,256,1024]{2,1,0:T(8,128)(2,1)}, bf16[4,32,3072]{2,1,0:T(8,128)(2,1)}, f32[32,1024]{1,0:T(8,128)}...) custom-call(bf16[1,256,1024]{2,1,0:T(8,128)(2,1)} %x_ref.1, bf16[1,256,1024]{2,1,0:T(8,128)(2,1)} %do_ref.1, s32[1,2048]{1,0:T(1,128)} %seg_in.1, ...), custom_call_target="tpu_custom_call" | custom-call | tf_op jit(solution)/shard_map/pallas_call | solution.py:919
  179.2 4.3 %shard_map.187 = (bf16[1,256,1024]{2,1,0:T(8,128)(2,1)}, bf16[1,256,1024]{2,1,0:T(8,128)(2,1)}, f32[32,3072]{1,0:T(8,128)}, f32[32,1024]{1,0:T(8,128)}, f32[32,4...) custom-call(bf16[1,256,1024]{2,1,0:T(8,128)(2,1)} %get-tuple-element, ...), custom_call_target="tpu_custom_call" | custom-call | tf_op jit(solution)/shard_map/pallas_call | solution.py:934
